TPU v7x, 32 devices: a whole 2x2x4 slice. The times are simulated.
32 devices in a mesh: dp: 8 (over z, x), mp: 4 (over y, core).
Axes of the slice: x: 2, y: 2, z: 4, core: 2. Of those that a mesh axis runs over, the one named last changes fastest.
Arguments:
- block_input: bfloat16 [4096, 2048], P(('dp', 'mp')), may hold values from -6 to 6
- norm_gain: bfloat16 [2048], replicated, may hold values from 0.099609375 to 1.8984375
- w_in: bfloat16 [2, 2048, 4096], P(None, None, 'mp'), may hold values from -0.125 to 0.125
- conv_w: bfloat16 [4, 4096], P(None, 'mp'), may hold values from -3 to 3
- conv_b: bfloat16 [4096], P('mp'), may hold values from -3 to 3
- w_x: bfloat16 [4096, 160], P('mp'), may hold values from -0.09375 to 0.09375
- w_dt: bfloat16 [128, 4096], P(None, 'mp'), may hold values from -0.5 to 0.5
- b_dt: bfloat16 [4096], P('mp'), may hold values from -5 to -1
- d_skip: bfloat16 [4096], P('mp'), may hold values from 0.099609375 to 1.8984375
- w_out: bfloat16 [4096, 2048], P('mp'), may hold values from -0.09375 to 0.09375
- out_grad: bfloat16 [4096, 2048], P(('dp', 'mp')), may hold values from -6 to 6
- seq_counts: int32 [8, 3], P('dp'), may hold values from 0 to 16, as said below
Outputs:
- block_out: bfloat16 [4096, 2048], P(('dp', 'mp'))
- input_grad: bfloat16 [4096, 2048], P(('dp', 'mp'))
- norm_gain_grad: float32 [2048], replicated
- w_in_grad: float32 [2, 2048, 4096], P(None, None, 'mp')
- conv_w_grad: float32 [4, 4096], P(None, 'mp')
- conv_b_grad: float32 [4096], P('mp')
- w_x_grad: float32 [4096, 160], P('mp')
- w_dt_grad: float32 [128, 4096], P(None, 'mp')
- b_dt_grad: float32 [4096], P('mp')
- d_skip_grad: float32 [4096], P('mp')
- w_out_grad: float32 [4096, 2048], P('mp')
Inputs may be any that keep to these rules, and one draw needn't show every extreme that they name: `seq_counts`: row g holds the counts of sequences of 512, 128 and 32 tokens in data group g, in that order; they fill the group's 512 tokens exactly.
All inputs are finite; a program needn't handle non-finite values.
Results may differ from a plain program's by a relative error of at most 0.012.
Values may be sent and summed in bfloat16 or wider, within the bound.
No kernel may reach another device: no remote copies, remote signals or barrier semaphores. Data moves between devices by JAX's collectives and lax.ppermute only.
A program may use at most 448 MiB of HBM per device.

v0:
```python
import jax
import jax.numpy as jnp
from jax import lax
from jax.sharding import PartitionSpec as P

R = 128


def boundaries(bucket_row, length):
    position = jnp.arange(length, dtype=jnp.int32)
    short_len = length // 16
    middle_len = length // 4
    short_end = bucket_row[2] * short_len
    middle_end = short_end + bucket_row[1] * middle_len
    first_short = (position < short_end) & (position % short_len == 0)
    first_middle = (
        (position >= short_end)
        & (position < middle_end)
        & ((position - short_end) % middle_len == 0)
    )
    first_long = (position == middle_end) & (position < length)
    opening = first_short | first_middle | first_long
    return jnp.where(opening, 0.0, 1.0).astype(jnp.float32)


def shift_down(values, lag):
    return jnp.concatenate([jnp.zeros((lag,) + values.shape[1:], values.dtype), values[:-lag]], 0)


def shift_up(values, lag):
    return jnp.concatenate([values[lag:], jnp.zeros((lag,) + values.shape[1:], values.dtype)], 0)


def conv_taps(inner, keep_mask):
    allow_two = keep_mask * shift_down(keep_mask, 1)
    allow_three = allow_two * shift_down(keep_mask, 2)
    taps = [
        inner,
        keep_mask[:, None] * shift_down(inner, 1),
        allow_two[:, None] * shift_down(inner, 2),
        allow_three[:, None] * shift_down(inner, 3),
    ]
    return (taps, [keep_mask, allow_two, allow_three])


def block_scan(decay_rate, drive_term, reverse):
    length = decay_rate.shape[0]
    span = min(16, length)
    count = length // span
    rest = decay_rate.shape[1:]
    decay_runs = decay_rate.reshape((count, span) + rest)
    drive_runs = drive_term.reshape((count, span) + rest)

    def turn(step, carry):
        run_decay, run_drive, out_decay, out_drive = carry
        where = span - 1 - step if reverse else step
        decay_now = lax.dynamic_index_in_dim(decay_runs, where, 1, keepdims=False)
        drive_now = lax.dynamic_index_in_dim(drive_runs, where, 1, keepdims=False)
        run_decay = decay_now * run_decay
        run_drive = decay_now * run_drive + drive_now
        out_decay = lax.dynamic_update_index_in_dim(out_decay, run_decay, where, 1)
        out_drive = lax.dynamic_update_index_in_dim(out_drive, run_drive, where, 1)
        return (run_decay, run_drive, out_decay, out_drive)

    start = (
        jnp.ones((count,) + rest, jnp.float32),
        jnp.zeros((count,) + rest, jnp.float32),
        jnp.zeros_like(decay_runs),
        jnp.zeros_like(drive_runs),
    )
    _, _, out_decay, out_drive = lax.fori_loop(0, span, turn, start)
    edge = 0 if reverse else span - 1
    total_decay = out_decay[:, edge]
    total_drive = out_drive[:, edge]

    def across(carry, item):
        acc_decay, acc_drive = carry
        run_decay, run_drive = item
        return ((run_decay * acc_decay, run_decay * acc_drive + run_drive), (acc_decay, acc_drive))

    first = (jnp.ones(rest, jnp.float32), jnp.zeros(rest, jnp.float32))
    _, (prior_decay, prior_drive) = lax.scan(
        across, first, (total_decay, total_drive), reverse=reverse
    )
    cum_decay = out_decay * prior_decay[:, None]
    cum_drive = out_decay * prior_drive[:, None] + out_drive
    return (cum_decay.reshape(decay_rate.shape), cum_drive.reshape(drive_term.shape))


def coefficients(keep_blk, step_blk, acts_blk, keys_blk):
    act_vals = acts_blk.astype(jnp.float32)
    decay_rate = keep_blk[:, None, None] * (
        1.0 - step_blk[:, None, :] * (keys_blk * keys_blk)[:, :, None]
    )
    drive_term = (step_blk * act_vals)[:, None, :] * keys_blk[:, :, None]
    return (decay_rate, drive_term)


def on_device(
    block_input,
    norm_gain,
    w_in,
    conv_w,
    conv_b,
    w_x,
    w_dt,
    b_dt,
    d_skip,
    w_out,
    out_grad,
    seq_counts,
):
    row_count = block_input.shape[0]
    length = row_count * lax.axis_size("mp")
    channels = w_in.shape[2]
    state_size = (w_x.shape[1] - R) // 2
    source_rows = block_input.astype(jnp.float32)
    inv_root = lax.rsqrt(jnp.mean(source_rows * source_rows, -1, keepdims=True) + 1e-05)
    normed = (source_rows * inv_root * norm_gain).astype(jnp.bfloat16)
    mixed = jnp.einsum(
        "td,kdc->tkc",
        lax.all_gather(normed, "mp", axis=0, tiled=True),
        w_in,
        preferred_element_type=jnp.float32,
    )
    inner = mixed[:, 0]
    gate_in = mixed[:, 1]
    keep_mask = boundaries(seq_counts[0], length)
    taps, allows = conv_taps(inner, keep_mask)
    conv_pre = conv_b + sum((conv_w[index] * taps[index] for index in range(len(taps))))
    acts = jax.nn.silu(conv_pre).astype(jnp.bfloat16)
    proj_part = jnp.einsum("tc,cm->mt", acts, w_x, preferred_element_type=jnp.float32)
    proj = lax.psum(proj_part, "mp")
    low_rank = proj[:R].astype(jnp.bfloat16)
    keys_t = proj[R : R + state_size]
    queries_t = proj[R + state_size :]
    pre_act = jnp.einsum("rt,rc->tc", low_rank, w_dt, preferred_element_type=jnp.float32) + b_dt
    beta = jax.nn.sigmoid(pre_act)
    key_square = jnp.sum(keys_t * keys_t, 0)[:, None]
    denom = 1.0 + beta * key_square
    step_size = beta / denom
    block_count = max(1, length // 512)
    block_len = length // block_count

    def blocks(values):
        return values.reshape((block_count, block_len) + values.shape[1:])

    def columns(values):
        return values.reshape(state_size, block_count, block_len).transpose(1, 2, 0)

    inputs_b = (
        blocks(keep_mask),
        blocks(step_size),
        blocks(acts),
        columns(keys_t),
        columns(queries_t),
    )

    def run_block(state_in, block_item):
        decay_rate, drive_term = coefficients(
            block_item[0], block_item[1], block_item[2], block_item[3]
        )
        cum_decay, cum_drive = block_scan(decay_rate, drive_term, False)
        states = cum_decay * state_in + cum_drive
        outputs = jnp.einsum("tn,tnc->tc", block_item[4], states)
        return (states[-1], (outputs, state_in))

    zero_state = jnp.zeros((state_size, channels), jnp.float32)
    _, (mixer_b, block_starts) = lax.scan(run_block, zero_state, inputs_b)
    mixer = mixer_b.reshape(length, channels) + d_skip * acts
    gate_sig = jax.nn.sigmoid(gate_in)
    gate_silu = gate_in * gate_sig
    gated = (mixer * gate_silu).astype(jnp.bfloat16)
    branch_out = lax.psum_scatter(
        jnp.dot(gated, w_out, preferred_element_type=jnp.float32).astype(jnp.bfloat16),
        "mp",
        scatter_dimension=0,
        tiled=True,
    ).astype(jnp.float32)
    block_out = (source_rows + branch_out).astype(jnp.bfloat16)
    shard_rows = lax.all_gather(out_grad, "mp", axis=0, tiled=True)
    weight_sum = jnp.einsum("tc,td->cd", gated, shard_rows, preferred_element_type=jnp.float32)
    gated_rows = jnp.einsum("td,cd->tc", shard_rows, w_out, preferred_element_type=jnp.float32)
    w_out_grad = weight_sum
    mixer_grad = gated_rows * gate_silu
    gate_grad = gated_rows * mixer * gate_sig * (1.0 + gate_in * (1.0 - gate_sig))
    d_skip_grad = jnp.sum(mixer_grad * acts, 0)

    def back_block(carried, block_item):
        keep_blk, step_blk, acts_blk, keys_blk, queries_blk, ygrad_blk, state_in = block_item
        decay_rate, drive_term = coefficients(keep_blk, step_blk, acts_blk, keys_blk)
        cum_decay, cum_drive = block_scan(decay_rate, drive_term, False)
        states = cum_decay * state_in + cum_drive
        prior_states = jnp.concatenate([state_in[None], states[:-1]], 0)
        source = queries_blk[:, :, None] * ygrad_blk[:, None, :]
        source = source.at[-1].add(carried)
        carry_decay = jnp.concatenate([decay_rate[1:], jnp.zeros_like(decay_rate[:1])], 0)
        _, adjoint = block_scan(carry_decay, source, True)
        act_vals = acts_blk.astype(jnp.float32)
        decay_grad = adjoint * prior_states * keep_blk[:, None, None]
        drive_keys = jnp.sum(adjoint * keys_blk[:, :, None], 1)
        step_grad = act_vals * drive_keys - jnp.sum(
            decay_grad * (keys_blk * keys_blk)[:, :, None], 1
        )
        key_grad = -2.0 * keys_blk * jnp.einsum("tnc,tc->tn", decay_grad, step_blk) + jnp.einsum(
            "tnc,tc->tn", adjoint, step_blk * act_vals
        )
        act_grad = step_blk * drive_keys
        query_grad = jnp.einsum("tnc,tc->tn", states, ygrad_blk)
        return (decay_rate[0] * adjoint[0], (step_grad, key_grad, act_grad, query_grad))

    back_inputs = inputs_b + (blocks(mixer_grad), block_starts)
    _, (step_grad_b, key_grad_b, act_grad_b, query_grad_b) = lax.scan(
        back_block, zero_state, back_inputs, reverse=True
    )
    step_grad = step_grad_b.reshape(length, channels)
    key_grad_t = key_grad_b.transpose(2, 0, 1).reshape(state_size, length)
    query_grad_t = query_grad_b.transpose(2, 0, 1).reshape(state_size, length)
    square_denom = denom * denom
    ksq_grad = jnp.sum(step_grad * (-(beta * beta) / square_denom), 1)
    pre_grad = (step_grad / square_denom * beta * (1.0 - beta)).astype(jnp.bfloat16)
    b_dt_grad = jnp.sum(pre_grad, 0, dtype=jnp.float32)
    w_dt_grad = jnp.einsum("rt,tc->rc", low_rank, pre_grad, preferred_element_type=jnp.float32)
    low_grad = jnp.einsum("rc,tc->rt", w_dt, pre_grad, preferred_element_type=jnp.float32)
    key_grad_t = key_grad_t + 2.0 * keys_t * ksq_grad[None, :]
    proj_grad = lax.psum(jnp.concatenate([low_grad, key_grad_t, query_grad_t], 0), "mp").astype(
        jnp.bfloat16
    )
    w_x_grad = jnp.einsum("tc,mt->cm", acts, proj_grad, preferred_element_type=jnp.float32)
    acts_grad = (
        act_grad_b.reshape(length, channels)
        + mixer_grad * d_skip
        + jnp.einsum("cm,mt->tc", w_x, proj_grad, preferred_element_type=jnp.float32)
    )
    conv_sig = jax.nn.sigmoid(conv_pre)
    conv_grad = acts_grad * conv_sig * (1.0 + conv_pre * (1.0 - conv_sig))
    conv_b_grad = jnp.sum(conv_grad, 0)
    conv_w_grad = jnp.stack([jnp.sum(conv_grad * tap_rows, 0) for tap_rows in taps], 0)
    inner_grad = conv_w[0] * conv_grad + sum(
        (
            shift_up(allows[index - 1][:, None] * conv_grad * conv_w[index], index)
            for index in range(1, len(taps))
        )
    )
    mixed_grad = jnp.stack([inner_grad, gate_grad], 1).astype(jnp.bfloat16)
    grad_part = mixed_grad
    w_in_grad = jnp.einsum(
        "td,tkc->kdc",
        lax.all_gather(normed, "mp", axis=0, tiled=True),
        grad_part,
        preferred_element_type=jnp.float32,
    )
    grad_part = mixed_grad
    normed_grad = lax.psum_scatter(
        jnp.einsum("tkc,kdc->td", grad_part, w_in, preferred_element_type=jnp.float32),
        "mp",
        scatter_dimension=0,
        tiled=True,
    )
    scaled = normed_grad * norm_gain
    gain_part = jnp.sum(normed_grad * source_rows * inv_root, 0)
    cubed = inv_root * inv_root * inv_root
    input_grad = inv_root * scaled - source_rows * cubed * jnp.mean(
        scaled * source_rows, -1, keepdims=True
    )
    input_grad = (out_grad.astype(jnp.float32) + input_grad).astype(jnp.bfloat16)
    norm_gain_grad = lax.psum(gain_part, ("dp", "mp"))
    w_in_grad, conv_w_grad, conv_b_grad, w_x_grad, w_dt_grad, b_dt_grad, d_skip_grad, w_out_grad = (
        lax.psum(
            (
                w_in_grad,
                conv_w_grad,
                conv_b_grad,
                w_x_grad,
                w_dt_grad,
                b_dt_grad,
                d_skip_grad,
                w_out_grad,
            ),
            "dp",
        )
    )
    return (
        block_out,
        input_grad,
        norm_gain_grad,
        w_in_grad,
        conv_w_grad,
        conv_b_grad,
        w_x_grad,
        w_dt_grad,
        b_dt_grad,
        d_skip_grad,
        w_out_grad,
    )


def solution(mesh):
    in_specs = (
        P(("dp", "mp"), None),
        P(),
        P(None, None, "mp"),
        P(None, "mp"),
        P("mp"),
        P("mp", None),
        P(None, "mp"),
        P("mp"),
        P("mp"),
        P("mp", None),
        P(("dp", "mp"), None),
        P("dp", None),
    )
    out_specs = (
        P(("dp", "mp"), None),
        P(("dp", "mp"), None),
        P(),
        P(None, None, "mp"),
        P(None, "mp"),
        P("mp"),
        P("mp", None),
        P(None, "mp"),
        P("mp"),
        P("mp"),
        P("mp", None),
    )
    return jax.shard_map(
        on_device, mesh=mesh, in_specs=in_specs, out_specs=out_specs, check_vma=False
    )
```

profile of v0, /device:TPU:0, one launch (start us, length us, event | category | flops | bytes accessed | tf_op | source)
XLA Modules:
  0.0 1703.1 jit_solution(9333370907623898242)
XLA Ops:
  15.2 22.6 %all-gather.3.cloned.1.call-done = bf16[512,2048]{1,0:T(8,128)(2,1)} async-done(((bf16[128,2048]{1,0:T(8,128)(2,1)}), bf16[512,2048]{1,0:T(8,128)(2,1)}) %all-gather.3.cloned.1.call-update) | async-done | bytes 2097168 | tf_op jit(solution)/shard_map/all_gather | solution.py:122
  57.4 28.3 %all-reduce.15.cloned.1.call-done = f32[160,512]{1,0:T(8,128)} async-done(((f32[160,512]{1,0:T(8,128)}), f32[160,512]{1,0:T(8,128)}) %all-reduce.15.cloned.1.call-update) | async-done | bytes 327696 | tf_op jit(solution)/shard_map/psum | solution.py:133
  102.4 12.9 broadcast_multiply_fusion.1
  115.3 11.4 subtract_multiply_fusion
  149.4 106.3 %while.131 = (s32[]{:T(128)}, f32[32,16,1024]{2,1,0:T(8,128)S(1)}, f32[32,16,1024]{2,1,0:T(8,128)}, f32[32,16,16,1024]{3,2,0,1:T(8,128)}, f32[32,16,16,1024]{3,2...) while((s32[]{:T(128)}, f32[32,16,1024]{2,1,0:T(8,128)S(1)}, ...), condition=%wide.region_4.5_spmd.clone, body=%wide.region_3.4_spmd.clone.sunk | while | flops 2621443 | bytes 16777828 | solution.py:71
  262.3 96.5 %while.132 = (s32[]{:T(128)}, f32[16,1024]{1,0:T(8,128)S(1)}, f32[16,1024]{1,0:T(8,128)}, f32[32,16,1024]{2,1,0:T(8,128)S(1)}, f32[32,16,1024]{2,1,0:T(8,128)}, ...) while((s32[]{:T(128)}, f32[16,1024]{1,0:T(8,128)S(1)}, ...), condition=%wide.region_6.7_spmd.clone, body=%wide.region_5.6_spmd.clone.sunk | while | flops 114691 | bytes 655980 | solution.py:82
  360.1 34.3 %fusion = f32[32,16,16,1024]{3,2,1,0:T(8,128)} fusion(f32[32,16,16,1024]{3,2,0,1:T(8,128)} %get-tuple-element.680, f32[32,16,16,1024]{3,2,0,1:T(8,128)} %get-tuple-element.679, f32[32,16,1024]{2,1,0:T(8,128)} %get-tuple-element.682, f32[32,16,1024]{2,1,0:T(8,128)} %copy-done.17), kind=kLoop, calls=%fused_computation.21 | loop fusion | flops 41943040 | bytes 104857600 | tf_op jit(solution)/shard_map/while/body/eval_jaxpr/add | solution.py:164
  398.4 22.8 %slice.177 = f32[511,16,1024]{2,1,0:T(8,128)} slice(f32[512,16,1024]{2,1,0:T(8,128)} %bitcast.229), slice={[0:511], [0:16], [0:1024]} | slice | bytes 66977792 | tf_op jit(solution)/shard_map/while/body/eval_jaxpr/slice | solution.py:194
  421.2 11.8 fusion.76
  441.2 11.6 broadcast_multiply_fusion
  461.8 13.9 concatenate.47
  487.1 11.4 broadcast.344.clone2.2
  498.5 106.4 %while.133 = (s32[]{:T(128)}, f32[32,16,1024]{2,1,0:T(8,128)S(1)}, f32[32,16,1024]{2,1,0:T(8,128)}, f32[32,16,16,1024]{3,2,0,1:T(8,128)}, f32[32,16,16,1024]{3,2...) while((s32[]{:T(128)}, f32[32,16,1024]{2,1,0:T(8,128)S(1)}, ...), condition=%wide.region_9.10_spmd.clone, body=%wide.region_8.9_spmd.clone.sunk | while | flops 2621447 | bytes 16777384 | solution.py:71
  612.1 30.3 %while.134 = (s32[]{:T(128)}, f32[16,1024]{1,0:T(8,128)S(1)}, f32[32,16,1024]{2,1,0:T(8,128)S(1)}, f32[32,16,1024]{2,1,0:T(8,128)}, f32[32,16,1024]{2,1,0:T(8,128)}, /*index=5*/s32[]{:T(128)}, s32[]{:T(128)}, s32[]{:T(128)}) while((s32[]{:T(128)}, f32[16,1024]{1,0:T(8,128)S(1)}, f32[32,16,1024]{2,1,0:T(8,128)S(1)}, ...), condition=%wide.region_11.12_spmd.clone, body=%wide.region_10.11_spmd.clone.sunk | while | flops 65540 | bytes 393332 | solution.py:82
  642.5 34.3 %multiply_reduce_fusion.1 = (f32[32,16,1024]{2,1,0:T(8,128)}, f32[32,16,16,1024]{3,2,1,0:T(8,128)}) fusion(f32[32,16,16]{2,1,0:T(8,128)} %copy.33, f32[32,16,16,1024]{3,2,0,1:T(8,128)} %get-tuple-element.684, f32[32,16,1024]{2,1,0:T(8,128)S(1)} %get-tuple-element.685, f32[32,16,16,1024]{3,2,0,1:T(8,128)} %get-tuple-element.683), kind=kLoop, calls=%fused_computation.24 | loop fusion | flops 33030144 | bytes 104890368 | tf_op jit(solution)/shard_map/while/body/eval_jaxpr/reduce_sum | solution.py:201
  676.7 23.2 %multiply_reduce_fusion = f32[512,1024]{1,0:T(8,128)} fusion(f32[512,16]{1,0:T(8,128)} %copy.40, f32[512]{0:T(512)S(1)} %copy-done.30, f32[511,16,1024]{2,1,0:T(8,128)} %slice.177, f32[32,16,16,1024]{3,2,1,0:T(8,128)} %get-tuple-element.892), kind=kLoop, calls=%fused_computation.22 | loop fusion | flops 33030144 | bytes 69175296 | tf_op jit(solution)/shard_map/while/body/eval_jaxpr/reduce_sum | solution.py:202
  705.9 23.0 %fusion.1 = f32[512,1,16]{2,1,0:T(1,128)} fusion(f32[512,16,1024]{2,1,0:T(8,128)} %bitcast.232, f32[511,16,1024]{2,1,0:T(8,128)} %slice.177, f32[512]{0:T(512)S(1)} %copy-done.30, f32[512,1024,1]{1,0,2:T(8,128)} %bitcast.237), kind=kOutput, calls=%fused_computation.35 | convolution fusion | flops 33554432 | bytes 69175296 | tf_op jit(solution)/shard_map/while/body/eval_jaxpr/tnc,tc->tn/dot_general | solution.py:205
  730.0 14.8 fusion.16
  746.5 14.5 fusion.14
  764.5 15.2 all-reduce.18
  827.5 37.7 %all-reduce.9 = (f32[4,1024]{1,0:T(4,128)}, f32[1024]{0:T(1024)}, f32[1024]{0:T(1024)}, f32[1024]{0:T(1024)}) all-reduce(f32[4,1024]{1,0:T(4,128)S(1)} %pad_maximum_fusion.4, f32[1024]{0:T(1024)S(1)} %get-tuple-element.812, f32[1024]{0:T(1024)S(1)} %get-tuple-element.889, ...), channel_id=1, replica_groups=mesh['dp'=8,'mp'=4] {'dp'}, use_global_device_ids=true, to_apply=%region_25.26 | all-reduce | flops 7168 | bytes 57344 | tf_op jit(solution)/shard_map/psum | solution.py:269
  866.7 38.4 %psum.79 = f32[2048]{0:T(1024)} all-reduce(f32[2048]{0:T(1024)S(1)} %get-tuple-element.817), channel_id=1, replica_groups=mesh['dp'=8,'mp'=4] {'dp','mp'}, use_global_device_ids=true, to_apply=%region_19.20 | all-reduce | flops 2048 | bytes 16384 | tf_op jit(solution)/shard_map/psum | solution.py:267
  907.7 760.7 %all-reduce.17.cloned.1.call-done = (f32[2,2048,1024]{1,2,0:T(8,128)}, f32[1024,160]{0,1:T(8,128)}, f32[128,1024]{1,0:T(8,128)}, f32[1024,2048]{1,0:T(8,128)}) async-done(((f32[2,2048,1024]{1,2,0:T(8,128)}, f32[1024,160]{0,1:T(8,128)}, f32[128,1024]{1,0:T(8,128)}, f32[1024,2048]{1,0:T(8,128)}), (f32[2,2048,1024]{1,2,0:T(8,128)}, f32[1024,160]{0,1:T(8,128)}, f32[128,1024]{1,0:T(8,128)}, ...) | async-done | bytes 26345488 | tf_op jit(solution)/shard_map/psum | solution.py:269
  1668.4 18.1 %copy.49 = f32[2,2048,1024]{2,1,0:T(8,128)} copy(f32[2,2048,1024]{1,2,0:T(8,128)} %get-tuple-element.877) | data formatting | bytes 33554432
  (385 shorter events, 525.1 us)
Async XLA Ops:
  7.2 44.8 %copy-start = (bf16[1024,160]{0,1:T(8,128)(2,1)S(1)}, bf16[1024,160]{0,1:T(8,128)(2,1)}, u32[]{:S(2)}) copy-start(bf16[1024,160]{0,1:T(8,128)(2,1)} %param.27) | copy-start | bytes 983044
  7.2 30.6 %all-gather.3.cloned.1.call-start = ((), (), s32[]{:S(2)}) async-start(), calls=%async_computation.2 | async-start | bytes 2621440 | tf_op jit(solution)/shard_map/all_gather | solution.py:122
  12.4 73.3 %all-reduce.15.cloned.1.call-start = ((), (), s32[]{:S(2)}) async-start(), calls=%async_computation.3 | async-start | bytes 655360 | tf_op jit(solution)/shard_map/psum | solution.py:133
  14.4 31.6 %copy-start.29 = (f32[512]{0:T(512)}, f32[512]{0:T(512)S(1)}, u32[]{:S(2)}) copy-start(f32[512]{0:T(512)S(1)} %fusion.66) | copy-start | bytes 6148
  15.1 39.0 %copy-start.45 = (f32[512]{0:T(512)}, f32[512]{0:T(512)S(1)}, u32[]{:S(2)}) copy-start(f32[512]{0:T(512)S(1)} %get-tuple-element.898) | copy-start | bytes 6148
  15.1 39.6 %copy-start.43 = (f32[512]{0:T(512)}, f32[512]{0:T(512)S(1)}, u32[]{:S(2)}) copy-start(f32[512]{0:T(512)S(1)} %get-tuple-element.897) | copy-start | bytes 6148
  15.1 30.8 %copy-start.34 = (f32[1,1024]{1,0:T(1,128)}, f32[1,1024]{1,0:T(1,128)S(1)}, u32[]{:S(2)}) copy-start(f32[1,1024]{1,0:T(1,128)S(1)} %get-tuple-element.920) | copy-start | bytes 12292
  15.1 30.8 %copy-start.36 = (f32[1,1024]{1,0:T(1,128)}, f32[1,1024]{1,0:T(1,128)S(1)}, u32[]{:S(2)}) copy-start(f32[1,1024]{1,0:T(1,128)S(1)} %get-tuple-element.921) | copy-start | bytes 12292
  15.2 30.8 %copy-start.38 = (f32[1,1024]{1,0:T(1,128)}, f32[1,1024]{1,0:T(1,128)S(1)}, u32[]{:S(2)}) copy-start(f32[1,1024]{1,0:T(1,128)S(1)} %get-tuple-element.919) | copy-start | bytes 12292
  15.2 30.8 %copy-start.40 = (f32[1,1024]{1,0:T(1,128)}, f32[1,1024]{1,0:T(1,128)S(1)}, u32[]{:S(2)}) copy-start(f32[1,1024]{1,0:T(1,128)S(1)} %get-tuple-element.918) | copy-start | bytes 12292
  53.2 379.8 %all-gather.5.cloned.1.call-start = ((), (), s32[]{:S(2)}) async-start(), calls=%async_computation.5 | async-start | bytes 2621440 | tf_op jit(solution)/shard_map/all_gather | solution.py:181
  53.9 811.2 %reduce-scatter.5.cloned.1.call-start = ((), (), s32[]{:S(2)}) async-start(), calls=%async_computation.6 | async-start | bytes 5242880 | tf_op jit(solution)/shard_map/reduce_scatter | solution.py:254
  360.1 34.3 %copy-start.5 = (f32[512,1024]{1,0:T(8,128)S(1)}, f32[512,1024]{1,0:T(8,128)}, u32[]{:S(2)}) copy-start(f32[512,1024]{1,0:T(8,128)} %copy-done.4) | copy-start | bytes 6291460
  642.4 34.3 %copy-start.30 = (f32[512]{0:T(512)S(1)}, f32[512]{0:T(512)}, u32[]{:S(2)}) copy-start(f32[512]{0:T(512)} %copy-done.29) | copy-start | bytes 6148
  676.7 23.2 %copy-start.3 = (f32[512,1024]{1,0:T(8,128)S(1)}, f32[512,1024]{1,0:T(8,128)}, u32[]{:S(2)}) copy-start(f32[512,1024]{1,0:T(8,128)} %copy-done.2) | copy-start | bytes 6291460
  676.7 23.2 %copy-start.52 = (f32[512]{0:T(512)S(1)}, f32[512]{0:T(512)}, u32[]{:S(2)}) copy-start(f32[512]{0:T(512)} %copy-done.51) | copy-start | bytes 6148
  800.2 105.0 %reduce-scatter.3.cloned.1.call-start = ((), (), s32[]{:S(2)}) async-start(), calls=%async_computation.4 | async-start | bytes 2621440 | tf_op jit(solution)/shard_map/reduce_scatter | solution.py:174
  807.2 861.2 %all-reduce.17.cloned.1.call-start = ((), (), s32[]{:S(2)}) async-start(), calls=%async_computation.7 | async-start | bytes 52690944 | tf_op jit(solution)/shard_map/psum | solution.py:269
  827.4 37.7 %copy-start.19 = (bf16[128,2048]{1,0:T(8,128)(2,1)S(1)}, bf16[128,2048]{1,0:T(8,128)(2,1)}, u32[]{:S(2)}) copy-start(bf16[128,2048]{1,0:T(8,128)(2,1)} %param.22) | copy-start | bytes 1572868
  827.4 37.7 %copy-start.32 = (f32[2048]{0:T(1024)S(1)}, f32[2048]{0:T(1024)}, u32[]{:S(2)}) copy-start(f32[2048]{0:T(1024)} %copy-done.31) | copy-start | bytes 24580
  827.4 37.7 %copy-start.54 = (f32[128]{0:T(128)S(1)}, f32[128]{0:T(128)}, u32[]{:S(2)}) copy-start(f32[128]{0:T(128)} %copy-done.53) | copy-start | bytes 1540
  827.4 77.7 %copy-start.23 = (bf16[128,2048]{1,0:T(8,128)(2,1)S(1)}, bf16[128,2048]{1,0:T(8,128)(2,1)}, u32[]{:S(2)}) copy-start(bf16[128,2048]{1,0:T(8,128)(2,1)} %param.32) | copy-start | bytes 1572868
  827.4 77.7 %copy-start.58 = (f32[128]{0:T(128)S(1)}, f32[128]{0:T(128)}, u32[]{:S(2)}) copy-start(f32[128]{0:T(128)} %get-tuple-element.924) | copy-start | bytes 1540
  865.1 40.0 %copy-start.21 = (f32[128,2048]{1,0:T(8,128)S(1)}, f32[128,2048]{1,0:T(8,128)}, u32[]{:S(2)}) copy-start(f32[128,2048]{1,0:T(8,128)} %reduce-scatter.5.cloned.1.call-done) | copy-start | bytes 3145732
  (47 other events, 268.1 us)
Sparse Core Ops, SparseCore 0:
  12.5 25.2 all-gather.2
  53.3 32.2 all-reduce.14
  87.2 22.5 all-gather.4
  800.3 44.4 reduce-scatter.4
  847.4 32.0 reduce-scatter.2
  885.3 782.9 all-reduce.16
where the time goes:
time: 1710 us; the launch traced here: 1700 us
  waiting for transfers between devices  812 us (47%)
  other arithmetic  499 us (29%)
  local copies, waits for them, and re-layouts  159 us (9%)
  matrix products  124 us (7%)
  blocking collectives  91.2 us (5%)
    psum x1, waiting for transfers between devices, on_device(): lax.psum((w_in_grad, conv_w_grad, conv_b_grad, w_x_grad, w_dt_grad, b_dt_...  761 us
    dynamic_update_slice x32, other arithmetic, turn(): out_drive = lax.dynamic_update_index_in_dim(out_drive, run_drive, where, 1)  213 us
    add x64, other arithmetic, across(): run_decay * acc_drive + run_drive  79.3 us
    another operation x7, local copies, waits for them, and re-layouts  47.5 us
    dynamic_update_slice x64, other arithmetic, block_scan(): lax.scan(across, first, (total_decay, total_drive), reverse=reverse)  46.6 us
    unnamed x134, local copies, waits for them, and re-layouts  41.1 us
    psum x1, blocking collectives, on_device(): norm_gain_grad = lax.psum(gain_part, ('dp', 'mp'))  38.4 us
    psum x1, blocking collectives, on_device(): lax.psum((w_in_grad, conv_w_grad, conv_b_grad, w_x_grad, w_dt_grad, b_dt_...  37.7 us
  transfers between devices with their start and end apart: 6, of which 3 were waited for; matrix products, arithmetic and copies ran while one was open for 22% of the time, Pallas kernels for 0%

commit v1 on v0

v1 whole, which is shorter than its diff:
```python
import jax
import jax.numpy as jnp
from jax import lax
from jax.experimental import pallas as pl
from jax.experimental.pallas import tpu as pltpu
from jax.sharding import PartitionSpec as P

R = 128
CHUNK = 32

def boundaries(bucket_row, length):
    position = jnp.arange(length, dtype=jnp.int32)
    short_len = length // 16
    middle_len = length // 4
    short_end = bucket_row[2] * short_len
    middle_end = short_end + bucket_row[1] * middle_len
    first_short = (position < short_end) & (position % short_len == 0)
    first_middle = (
        (position >= short_end)
        & (position < middle_end)
        & ((position - short_end) % middle_len == 0)
    )
    first_long = (position == middle_end) & (position < length)
    opening = first_short | first_middle | first_long
    return jnp.where(opening, 0.0, 1.0).astype(jnp.float32)


def shift_down(values, lag):
    return jnp.concatenate([jnp.zeros((lag,) + values.shape[1:], values.dtype), values[:-lag]], 0)


def shift_up(values, lag):
    return jnp.concatenate([values[lag:], jnp.zeros((lag,) + values.shape[1:], values.dtype)], 0)


def conv_taps(inner, keep_mask):
    allow_two = keep_mask * shift_down(keep_mask, 1)
    allow_three = allow_two * shift_down(keep_mask, 2)
    taps = [
        inner,
        keep_mask[:, None] * shift_down(inner, 1),
        allow_two[:, None] * shift_down(inner, 2),
        allow_three[:, None] * shift_down(inner, 3),
    ]
    return (taps, [keep_mask, allow_two, allow_three])


def col_sums(values):
    rows = values[0].shape[0]
    if rows != 8:
        return jnp.concatenate([jnp.sum(v, 0, keepdims=True) for v in values], 0)
    row = lax.broadcasted_iota(jnp.int32, (8, 128), 0)
    span = 1
    while len(values) > 1:
        low = (row // span) % 2 == 0
        values = [
            jnp.where(low, a, b) + pltpu.roll(jnp.where(low, b, a), 8 - span, axis=0)
            for a, b in zip(values[0::2], values[1::2])
        ]
        span *= 2
    return values[0]


def fwd_kernel(chunk, n, keys, queries, keeps, step_ref, acts_ref, mix_ref, states_ref, carry):
    index = pl.program_id(0)
    tiles = carry.shape[1]

    @pl.when(index == 0)
    def _():
        carry[...] = jnp.zeros_like(carry)

    keep = keeps[index]
    start = tuple(carry[j] * keep for j in range(n))

    def eight(block, state):
        state = list(state)
        for i in range(8):
            rows = pl.ds(i, tiles, stride=8)
            step = step_ref[block, rows, :]
            act = acts_ref[block, rows, :]
            token = block * 8 + i
            base = (index * chunk + token) * n
            total = None
            for j in range(n):
                k = keys[base + j]
                state[j] = state[j] + (step * k) * (act - state[j] * k)
                states_ref[token, j] = state[j]
                part = state[j] * queries[base + j]
                total = part if total is None else total + part
            mix_ref[block, rows, :] = total
        return tuple(state)

    final = lax.fori_loop(0, chunk // 8, eight, start)
    for j in range(n):
        carry[j] = final[j]


def scan_forward(keys, queries, keeps, step, acts, chunk, n):
    blocks, height, _ = step.shape
    tiles = height // 8
    length = blocks * 8
    count = length // chunk
    wide = pl.BlockSpec((chunk // 8, height, 128), lambda c: (c, 0, 0))
    scal = pl.BlockSpec(memory_space=pltpu.SMEM)
    return pl.pallas_call(
        lambda *refs: fwd_kernel(chunk, n, *refs),
        grid=(count,),
        in_specs=[scal, scal, scal, wide, wide],
        out_specs=[wide, pl.BlockSpec((chunk, n, tiles, 128), lambda c: (c, 0, 0, 0))],
        out_shape=[
            jax.ShapeDtypeStruct(step.shape, jnp.float32),
            jax.ShapeDtypeStruct((length, n, tiles, 128), jnp.float32),
        ],
        scratch_shapes=[pltpu.VMEM((n, tiles, 128), jnp.float32)],
        compiler_params=pltpu.CompilerParams(vmem_limit_bytes=48 << 20),
    )(keys, queries, keeps, step, acts)


def bwd_kernel(
    chunk, n, keys, queries, keeps, step_ref, acts_ref, ygrad_ref, states_ref, prior_ref,
    sgrad_ref, agrad_ref, kred_ref, qred_ref, carry
):
    order = pl.program_id(0)
    index = pl.num_programs(0) - 1 - order
    tiles = carry.shape[1]

    @pl.when(order == 0)
    def _():
        carry[...] = jnp.zeros_like(carry)

    keep = keeps[index]

    def token_step(block, i, adjoint, prior_of):
        rows = pl.ds(i, tiles, stride=8)
        step = step_ref[block, rows, :]
        act = acts_ref[block, rows, :]
        ygrad = ygrad_ref[block, rows, :]
        token = block * 8 + i
        base = (index * chunk + token) * n
        drive = None
        fade = None
        kparts = []
        qparts = []
        for j in range(n):
            k = keys[base + j]
            adj = adjoint[j] + ygrad * queries[base + j]
            prior = prior_of(token, j)
            ka = adj * k
            kp = prior * k
            weighted = step * adj
            kparts.append(weighted * (act - (kp + kp)))
            qparts.append(states_ref[token, j] * ygrad)
            loss = ka * kp
            drive = ka if drive is None else drive + ka
            fade = loss if fade is None else fade + loss
            adjoint[j] = adj - (step * k) * ka
        sgrad_ref[block, rows, :] = act * drive - fade
        agrad_ref[block, rows, :] = step * drive
        for first in range(0, n, 8):
            kred_ref[token, first:first + 8, :] = col_sums(kparts[first:first + 8])
            qred_ref[token, first:first + 8, :] = col_sums(qparts[first:first + 8])
        return adjoint

    def eight(turn, adjoint):
        block = chunk // 8 - 1 - turn
        adjoint = list(adjoint)
        for i in range(7, -1, -1):
            if i > 0:
                adjoint = token_step(block, i, adjoint, lambda token, j: states_ref[token - 1, j])
            else:
                first = block == 0
                held = jnp.where(first, keep, 1.0)
                back = jnp.maximum(block * 8 - 1, 0)
                adjoint = token_step(
                    block, i, adjoint,
                    lambda token, j: jnp.where(first, prior_ref[0, j], states_ref[back, j]) * held,
                )
        return tuple(adjoint)

    final = lax.fori_loop(0, chunk // 8, eight, tuple(carry[j] for j in range(n)))
    for j in range(n):
        carry[j] = final[j] * keep


def scan_backward(keys, queries, keeps, step, acts, ygrad, states, chunk, n):
    blocks, height, _ = step.shape
    tiles = height // 8
    length = blocks * 8
    count = length // chunk
    last = count - 1
    wide = pl.BlockSpec((chunk // 8, height, 128), lambda c: (last - c, 0, 0))
    scal = pl.BlockSpec(memory_space=pltpu.SMEM)
    red = pl.BlockSpec((chunk, n, 128), lambda c: (last - c, 0, 0))
    return pl.pallas_call(
        lambda *refs: bwd_kernel(chunk, n, *refs),
        grid=(count,),
        in_specs=[
            scal, scal, scal, wide, wide, wide,
            pl.BlockSpec((chunk, n, tiles, 128), lambda c: (last - c, 0, 0, 0)),
            pl.BlockSpec((1, n, tiles, 128), lambda c: (jnp.maximum((last - c) * chunk - 1, 0), 0, 0, 0)),
        ],
        out_specs=[wide, wide, red, red],
        out_shape=[jax.ShapeDtypeStruct(step.shape, jnp.float32)] * 2
        + [jax.ShapeDtypeStruct((length, n, 128), jnp.float32)] * 2,
        scratch_shapes=[pltpu.VMEM((n, tiles, 128), jnp.float32)],
        compiler_params=pltpu.CompilerParams(vmem_limit_bytes=48 << 20),
    )(keys, queries, keeps, step, acts, ygrad, states, states)

def to_tiles(values):
    length, channels = values.shape
    parts = values.reshape(length // 8, 8, channels // 128, 128).transpose(0, 2, 1, 3)
    return parts.reshape(length // 8, channels // 16, 128)


def from_tiles(values):
    blocks, height, _ = values.shape
    parts = values.reshape(blocks, height // 8, 8, 128).transpose(0, 2, 1, 3)
    return parts.reshape(blocks * 8, height * 16)


def sum_over(values, axis):
    return lax.psum(values.astype(jnp.bfloat16), axis).astype(jnp.float32)


def on_device(
    block_input,
    norm_gain,
    w_in,
    conv_w,
    conv_b,
    w_x,
    w_dt,
    b_dt,
    d_skip,
    w_out,
    out_grad,
    seq_counts,
):
    row_count = block_input.shape[0]
    length = row_count * lax.axis_size("mp")
    state_size = (w_x.shape[1] - R) // 2
    source_rows = block_input.astype(jnp.float32)
    inv_root = lax.rsqrt(jnp.mean(source_rows * source_rows, -1, keepdims=True) + 1e-05)
    normed = (source_rows * inv_root * norm_gain).astype(jnp.bfloat16)
    all_normed = lax.all_gather(normed, "mp", axis=0, tiled=True)
    all_ograd = lax.all_gather(out_grad, "mp", axis=0, tiled=True)
    inner = jnp.dot(all_normed, w_in[0], preferred_element_type=jnp.float32)
    gate_in = jnp.dot(all_normed, w_in[1], preferred_element_type=jnp.float32)
    keep_mask = boundaries(seq_counts[0], length)
    taps, allows = conv_taps(inner, keep_mask)
    conv_pre = conv_b + sum((conv_w[index] * taps[index] for index in range(len(taps))))
    acts = jax.nn.silu(conv_pre).astype(jnp.bfloat16)
    acts_full = acts.astype(jnp.float32)
    proj = lax.psum(jnp.dot(acts, w_x, preferred_element_type=jnp.float32), "mp")
    low_rank = proj[:, :R].astype(jnp.bfloat16)
    keys = proj[:, R : R + state_size]
    queries = proj[:, R + state_size :]
    pre_act = jnp.dot(low_rank, w_dt, preferred_element_type=jnp.float32) + b_dt
    beta = jax.nn.sigmoid(pre_act)
    key_square = jnp.sum(keys * keys, 1, keepdims=True)
    denom = 1.0 + beta * key_square
    step_size = beta / denom
    flat_keys = keys.reshape(-1)
    flat_queries = queries.reshape(-1)
    keeps = keep_mask[::CHUNK]
    step_tiles = to_tiles(step_size)
    acts_tiles = to_tiles(acts_full)
    mix_tiles, states = scan_forward(
        flat_keys, flat_queries, keeps, step_tiles, acts_tiles, CHUNK, state_size
    )
    mixer = from_tiles(mix_tiles) + d_skip * acts_full
    gate_sig = jax.nn.sigmoid(gate_in)
    gate_silu = gate_in * gate_sig
    gated = (mixer * gate_silu).astype(jnp.bfloat16)
    gated_rows = lax.dot_general(
        all_ograd, w_out, (((1,), (1,)), ((), ())), preferred_element_type=jnp.float32
    )
    gate_grad = (gated_rows * mixer * gate_sig * (1.0 + gate_in * (1.0 - gate_sig))).astype(
        jnp.bfloat16
    )
    mixer_grad = gated_rows * gate_silu
    tokens = (((0,), (0,)), ((), ()))
    w_out_part = lax.dot_general(gated, all_ograd, tokens, preferred_element_type=jnp.float32)
    w_gate_part = lax.dot_general(all_normed, gate_grad, tokens, preferred_element_type=jnp.float32)
    w_out_grad = sum_over(w_out_part, "dp")
    w_gate_grad = sum_over(w_gate_part, "dp")
    sgrad_tiles, agrad_tiles, key_red, query_red = scan_backward(
        flat_keys,
        flat_queries,
        keeps,
        step_tiles,
        acts_tiles,
        to_tiles(mixer_grad),
        states,
        CHUNK,
        state_size,
    )
    branch_out = lax.psum_scatter(
        jnp.dot(gated, w_out, preferred_element_type=jnp.float32).astype(jnp.bfloat16),
        "mp",
        scatter_dimension=0,
        tiled=True,
    ).astype(jnp.float32)
    block_out = (source_rows + branch_out).astype(jnp.bfloat16)
    d_skip_grad = jnp.sum(mixer_grad * acts_full, 0)
    step_grad = from_tiles(sgrad_tiles)
    act_grad = from_tiles(agrad_tiles)
    square_denom = denom * denom
    ksq_grad = jnp.sum(step_grad * (-(beta * beta) / square_denom), 1, keepdims=True)
    pre_grad = (step_grad / square_denom * beta * (1.0 - beta)).astype(jnp.bfloat16)
    b_dt_grad = jnp.sum(pre_grad, 0, dtype=jnp.float32)
    w_dt_grad = lax.dot_general(low_rank, pre_grad, tokens, preferred_element_type=jnp.float32)
    low_grad = lax.dot_general(
        pre_grad, w_dt, (((1,), (1,)), ((), ())), preferred_element_type=jnp.float32
    )
    key_grad = jnp.sum(key_red, -1) + 2.0 * keys * ksq_grad
    query_grad = jnp.sum(query_red, -1)
    proj_grad = lax.psum(jnp.concatenate([low_grad, key_grad, query_grad], 1), "mp").astype(
        jnp.bfloat16
    )
    w_x_grad = lax.dot_general(acts, proj_grad, tokens, preferred_element_type=jnp.float32)
    acts_grad = (
        act_grad
        + mixer_grad * d_skip
        + lax.dot_general(
            proj_grad, w_x, (((1,), (1,)), ((), ())), preferred_element_type=jnp.float32
        )
    )
    conv_sig = jax.nn.sigmoid(conv_pre)
    conv_grad = acts_grad * conv_sig * (1.0 + conv_pre * (1.0 - conv_sig))
    conv_b_grad = jnp.sum(conv_grad, 0)
    conv_w_grad = jnp.stack([jnp.sum(conv_grad * tap_rows, 0) for tap_rows in taps], 0)
    inner_grad = conv_w[0] * conv_grad + sum(
        (
            shift_up(allows[index - 1][:, None] * conv_grad * conv_w[index], index)
            for index in range(1, len(taps))
        )
    )
    inner_grad = inner_grad.astype(jnp.bfloat16)
    w_inner_part = lax.dot_general(
        all_normed, inner_grad, tokens, preferred_element_type=jnp.float32
    )
    w_inner_grad = sum_over(w_inner_part, "dp")
    across = (((1,), (1,)), ((), ()))
    normed_grad = lax.psum_scatter(
        lax.dot_general(inner_grad, w_in[0], across, preferred_element_type=jnp.float32)
        + lax.dot_general(gate_grad, w_in[1], across, preferred_element_type=jnp.float32),
        "mp",
        scatter_dimension=0,
        tiled=True,
    )
    scaled = normed_grad * norm_gain
    gain_part = jnp.sum(normed_grad * source_rows * inv_root, 0)
    cubed = inv_root * inv_root * inv_root
    input_grad = inv_root * scaled - source_rows * cubed * jnp.mean(
        scaled * source_rows, -1, keepdims=True
    )
    input_grad = (out_grad.astype(jnp.float32) + input_grad).astype(jnp.bfloat16)
    norm_gain_grad = lax.psum(gain_part, ("dp", "mp"))
    conv_w_grad, conv_b_grad, w_x_grad, w_dt_grad, b_dt_grad, d_skip_grad = lax.psum(
        (conv_w_grad, conv_b_grad, w_x_grad, w_dt_grad, b_dt_grad, d_skip_grad), "dp"
    )
    return (
        block_out,
        input_grad,
        norm_gain_grad,
        jnp.stack([w_inner_grad, w_gate_grad]),
        conv_w_grad,
        conv_b_grad,
        w_x_grad,
        w_dt_grad,
        b_dt_grad,
        d_skip_grad,
        w_out_grad,
    )


def solution(mesh):
    in_specs = (
        P(("dp", "mp"), None),
        P(),
        P(None, None, "mp"),
        P(None, "mp"),
        P("mp"),
        P("mp", None),
        P(None, "mp"),
        P("mp"),
        P("mp"),
        P("mp", None),
        P(("dp", "mp"), None),
        P("dp", None),
    )
    out_specs = (
        P(("dp", "mp"), None),
        P(("dp", "mp"), None),
        P(),
        P(None, None, "mp"),
        P(None, "mp"),
        P("mp"),
        P("mp", None),
        P(None, "mp"),
        P("mp"),
        P("mp"),
        P("mp", None),
    )
    return jax.shard_map(
        on_device, mesh=mesh, in_specs=in_specs, out_specs=out_specs, check_vma=False
    )
```

time: 1710 us -> 801 us (0.47)
  other arithmetic: 499 us -> 48 us
  waiting for transfers between devices: 812 us -> 508 us
  local copies, waits for them, and re-layouts: 159 us -> 16.5 us
  matrix products: 124 us -> 61.9 us
  Pallas kernels: 0 us -> 51.1 us
    psum x2 -> x3, waiting for transfers between devices: 789 us -> 476 us  [the longest x1 377 us: sum_over(): return lax.psum(values.astype(jnp.bfloat16), axis).astype(jnp.float32)]
    dynamic_update_slice x96 -> x0, other arithmetic: 259 us -> none  [the longest x32 213 us: turn(): out_drive = lax.dynamic_update_index_in_dim(out_drive, run_drive, where, 1)]
    add x66 -> x1, other arithmetic: 114 us -> 0.78 us  [on_device(): key_grad = jnp.sum(key_red, -1) + 2.0 * keys * ksq_grad]
    dot_general x15 -> x14, matrix products: 119 us -> 56 us  [the longest x1 11.1 us: on_device(): lax.dot_general(all_ograd, w_out, (((1,), (1,)), ((), ())), preferred_ele...]
    pallas_call x0 -> x2, Pallas kernels: none -> 51.1 us  [the longest x1 32 us: scan_backward(): pl.pallas_call(lambda *refs: bwd_kernel(chunk, n, *refs), grid=(count,),...]
    reduce_sum x2 -> x3, other arithmetic: 57.4 us -> 8.92 us  [the longest x1 4.07 us: on_device(): query_grad = jnp.sum(query_red, -1)]
    another operation x7 -> x0, local copies, waits for them, and re-layouts: 47.5 us -> none
    mul x7 -> x1, other arithmetic: 43.4 us -> 0.57 us  [on_device(): key_grad = jnp.sum(key_red, -1) + 2.0 * keys * ksq_grad]
  transfers between devices with their start and end apart: 6 -> 7, of which waited for: 3 -> 5; matrix products, arithmetic and copies ran while one was open for 22% -> 8% of each run, Pallas kernels for 0% -> 0%
where the time goes in v1:
time: 801 us; the launch traced here: 793 us
  waiting for transfers between devices  508 us (63%)
  blocking collectives  91 us (11%)
  matrix products  61.9 us (8%)
  Pallas kernels  51.1 us (6%)
  other arithmetic  48 us (6%)
  local copies, waits for them, and re-layouts  16.5 us (2%)
  between operations  16.5 us (2%)
    psum x1, waiting for transfers between devices, sum_over(): return lax.psum(values.astype(jnp.bfloat16), axis).astype(jnp.float32)  377 us
    psum x1, waiting for transfers between devices, on_device(): lax.psum((conv_w_grad, conv_b_grad, w_x_grad, w_dt_grad, b_dt_grad, d_ski...  67.5 us
    psum x1, blocking collectives, on_device(): norm_gain_grad = lax.psum(gain_part, ('dp', 'mp'))  37.9 us
    psum x1, blocking collectives, on_device(): lax.psum((conv_w_grad, conv_b_grad, w_x_grad, w_dt_grad, b_dt_grad, d_ski...  37.7 us
    pallas_call x1, Pallas kernels, scan_backward(): pl.pallas_call(lambda *refs: bwd_kernel(chunk, n, *refs), grid=(count,),...  32 us
    psum x1, waiting for transfers between devices, on_device(): lax.psum(jnp.dot(acts, w_x, preferred_element_type=jnp.float32), 'mp')  30.6 us
    all_gather x1, waiting for transfers between devices, on_device(): all_normed = lax.all_gather(normed, 'mp', axis=0, tiled=True)  19.4 us
    pallas_call x1, Pallas kernels, scan_forward(): pl.pallas_call(lambda *refs: fwd_kernel(chunk, n, *refs), grid=(count,),...  19.1 us
  transfers between devices with their start and end apart: 7, of which 5 were waited for; matrix products, arithmetic and copies ran while one was open for 8% of the time, Pallas kernels for 0%

profile of v1, /device:TPU:0, one launch (start us, length us, event | category | flops | bytes accessed | tf_op | source)
XLA Modules:
  0.0 793.3 jit_solution(302068930126706490)
XLA Ops:
  17.9 19.4 %all-gather.3.cloned.1.call-done = bf16[512,2048]{1,0:T(8,128)(2,1)} async-done(((bf16[128,2048]{1,0:T(8,128)(2,1)}), bf16[512,2048]{1,0:T(8,128)(2,1)}) %all-gather.3.cloned.1.call-update) | async-done | bytes 2097168 | tf_op jit(solution)/shard_map/all_gather | solution.py:245
  37.3 5.3 fusion.6
  42.6 6.9 fusion.2
  49.5 12.0 %all-gather.5.cloned.1.call-done = bf16[512,2048]{1,0:T(8,128)(2,1)} async-done(((bf16[128,2048]{1,0:T(8,128)(2,1)}), bf16[512,2048]{1,0:T(8,128)(2,1)}) %all-gather.5.cloned.1.call-update) | async-done | bytes 2097168 | tf_op jit(solution)/shard_map/all_gather | solution.py:246
  61.5 11.1 %fusion.16 = (f32[1024]{0:T(1024)}, f32[512,1024]{1,0:T(8,128)}, bf16[512,1024]{1,0:T(8,128)(2,1)S(1)}, f32[512,1024]{1,0:T(8,128)}, f32[512,1024]{1,0:T(8,128)}) fusion(f32[512,1024]{1,0:T(8,128)} %fusion.2, f32[509,1024]{1,0:T(8,128)S(1)} %bitcast.109, f32[512]{0:T(512)S(1)} %get-tuple-element.45, f32[1024]{0:T(1024)S(1)} %bitcast.117, ...), kind=kOutput, calls=%fused_computation.28 | convolution fusion | flops 2160065536 | bytes 24123392 | tf_op jit(solution)/shard_map/dot_general | solution.py:275
  75.6 30.6 %all-reduce.15.cloned.1.call-done = f32[512,160]{0,1:T(8,128)} async-done(((f32[512,160]{0,1:T(8,128)}), f32[512,160]{0,1:T(8,128)}) %all-reduce.15.cloned.1.call-update) | async-done | bytes 327696 | tf_op jit(solution)/shard_map/psum | solution.py:254
  109.6 19.1 %shard_map.203 = (f32[64,64,128]{2,1,0:T(8,128)S(1)}, f32[512,16,8,128]{3,2,1,0:T(8,128)}) custom-call(f32[8192]{0:T(1024)S(1)} %reshape.154.refs_0_, f32[8192]{0:T(1024)S(1)} %reshape.155.refs_1_, f32[16]{0:T(128)S(1)} %slice.83.refs_2_, f32[64,64,128]{2,1,0:T(8,128)S(1)} %divide_bitcast_fusion.refs_3_, f32[64,64,128]{2,1,0:T(8,128)} %convert_bitcast_fusion.2.refs_4_), custom_call_target="tpu_custom_call" | custom-call | tf_op jit(solution)/shard_map/pallas_call | solution.py:105
  128.7 32.0 %shard_map.204 = (f32[64,64,128]{2,1,0:T(8,128)S(1)}, f32[64,64,128]{2,1,0:T(8,128)S(1)}, f32[512,16,128]{2,1,0:T(8,128)}, f32[512,16,128]{2,1,0:T(8,128)}) custom-call(f32[8192]{0:T(1024)S(1)} %reshape.154.refs_0_, f32[8192]{0:T(1024)S(1)} %reshape.155.refs_1_, f32[16]{0:T(128)S(1)} %slice.83.refs_2_, f32[64,64,128]{2,1,0:T(8,128)} %copy-done.2, ...), custom_call_target="tpu_custom_call" | custom-call | tf_op jit(solution)/shard_map/pallas_call | solution.py:194
  165.4 4.1 reduce_sum.128
  170.5 4.1 reduce_sum.130
  178.0 15.4 %all-reduce.20 = bf16[512,160]{0,1:T(8,128)(2,1)} all-reduce(f32[512,160]{0,1:T(8,128)} %pad_maximum_fusion), channel_id=1, replica_groups=mesh['dp'=8,'mp'=4] {'mp'}, use_global_device_ids=true, to_apply=%region_7.8 | all-reduce | flops 81920 | bytes 491520 | tf_op jit(solution)/shard_map/psum | solution.py:318
  193.5 3.9 fusion.22
  206.0 2.6 fusion.57
  209.6 4.4 fusion.12
  215.2 5.9 convolution_convert_fusion.1
  221.5 7.2 convert_bitcast_fusion.1
  228.7 4.4 convert_bitcast_fusion
  233.1 4.3 convolution_convert_fusion
  241.1 37.7 %all-reduce.7 = (f32[4,1024]{1,0:T(4,128)}, f32[1024]{0:T(1024)}, f32[1024]{0:T(1024)}, f32[1024]{0:T(1024)}) all-reduce(f32[4,1024]{1,0:T(4,128)S(1)} %pad_maximum_fusion.1, f32[1024]{0:T(1024)S(1)} %get-tuple-element.23, f32[1024]{0:T(1024)S(1)} %copy-done.29, f32[1024]{0:T(1024)S(1)} %copy-done.45), channel_id=1, replica_groups=mesh['dp'=8,'mp'=4] {'dp'}, use_global_device_ids=true, to_apply=%region_18.19 | all-reduce | flops 7168 | bytes 57344 | tf_op jit(solution)/shard_map/psum | solution.py:360
  280.5 37.9 %psum.86 = f32[2048]{0:T(1024)} all-reduce(f32[2048]{0:T(1024)S(1)} %get-tuple-element.28), channel_id=1, replica_groups=mesh['dp'=8,'mp'=4] {'dp','mp'}, use_global_device_ids=true, to_apply=%region_11.12 | all-reduce | flops 2048 | bytes 16384 | tf_op jit(solution)/shard_map/psum | solution.py:359
  320.9 377.4 %all-reduce.19.cloned.1.call-done = (bf16[1,2048,1024]{2,1,0:T(8,128)(2,1)}, bf16[1,2048,1024]{2,1,0:T(8,128)(2,1)}, bf16[1024,2048]{1,0:T(8,128)(2,1)}) async-done(((bf16[1,2048,1024]{2,1,0:T(8,128)(2,1)}, bf16[1,2048,1024]{2,1,0:T(8,128)(2,1)}, bf16[1024,2048]{1,0:T(8,128)(2,1)}), (bf16[1,2048,1024]{2,1,0:T(8,128)(2,1)}, bf16[1,2048,1024]{2,1,0:T(8,128)(2,1)}, ...) | async-done | bytes 12582928 | tf_op jit(solution)/shard_map/psum | solution.py:222
  698.3 6.8 convert_element_type.108
  705.1 9.5 %maximum_convert_fusion = f32[2,2048,1024]{2,1,0:T(8,128)} fusion(bf16[1,2048,1024]{2,1,0:T(8,128)(2,1)S(1)} %copy-done.10, bf16[1,2048,1024]{2,1,0:T(8,128)(2,1)} %get-tuple-element.37), kind=kLoop, calls=%fused_computation | loop fusion | flops 8388608 | bytes 25165824 | tf_op jit(solution)/shard_map/stack | solution.py:367
  714.7 67.5 %all-reduce.17.cloned.1.call-done = (f32[1024,160]{0,1:T(8,128)}, f32[128,1024]{1,0:T(8,128)}) async-done(((f32[1024,160]{0,1:T(8,128)}, f32[128,1024]{1,0:T(8,128)}), (f32[1024,160]{0,1:T(8,128)}, f32[128,1024]{1,0:T(8,128)})) %all-reduce.17.cloned.1.call-update) | async-done | bytes 1179664 | tf_op jit(solution)/shard_map/psum | solution.py:360
  (173 shorter events, 47.4 us)
Async XLA Ops:
  7.2 65.4 %copy-start = (bf16[1024,160]{0,1:T(8,128)(2,1)S(1)}, bf16[1024,160]{0,1:T(8,128)(2,1)}, u32[]{:S(2)}) copy-start(bf16[1024,160]{0,1:T(8,128)(2,1)} %param.17) | copy-start | bytes 983044
  7.2 30.0 %all-gather.3.cloned.1.call-start = ((), (), s32[]{:S(2)}) async-start(), calls=%async_computation.2 | async-start | bytes 2621440 | tf_op jit(solution)/shard_map/all_gather | solution.py:245
  9.1 33.5 %copy-start.43 = (f32[128]{0:T(128)}, f32[128]{0:T(128)S(1)}, u32[]{:S(2)}) copy-start(f32[128]{0:T(128)S(1)} %get-tuple-element.63) | copy-start | bytes 1540
  11.8 49.6 %all-gather.5.cloned.1.call-start = ((), (), s32[]{:S(2)}) async-start(), calls=%async_computation.5 | async-start | bytes 2621440 | tf_op jit(solution)/shard_map/all_gather | solution.py:246
  12.6 93.7 %all-reduce.15.cloned.1.call-start = ((), (), s32[]{:S(2)}) async-start(), calls=%async_computation.3 | async-start | bytes 655360 | tf_op jit(solution)/shard_map/psum | solution.py:254
  16.6 44.9 %copy-start.25 = (f32[512]{0:T(512)}, f32[512]{0:T(512)S(1)}, u32[]{:S(2)}) copy-start(f32[512]{0:T(512)S(1)} %get-tuple-element.45) | copy-start | bytes 6148
  16.6 44.9 %copy-start.27 = (f32[512]{0:T(512)}, f32[512]{0:T(512)S(1)}, u32[]{:S(2)}) copy-start(f32[512]{0:T(512)S(1)} %get-tuple-element.46) | copy-start | bytes 6148
  17.9 43.6 %copy-start.32 = (f32[1,1024]{1,0:T(1,128)}, f32[1,1024]{1,0:T(1,128)S(1)}, u32[]{:S(2)}) copy-start(f32[1,1024]{1,0:T(1,128)S(1)} %get-tuple-element.58) | copy-start | bytes 12292
  17.9 43.6 %copy-start.34 = (f32[1,1024]{1,0:T(1,128)}, f32[1,1024]{1,0:T(1,128)S(1)}, u32[]{:S(2)}) copy-start(f32[1,1024]{1,0:T(1,128)S(1)} %get-tuple-element.57) | copy-start | bytes 12292
  17.9 43.6 %copy-start.36 = (f32[1,1024]{1,0:T(1,128)}, f32[1,1024]{1,0:T(1,128)S(1)}, u32[]{:S(2)}) copy-start(f32[1,1024]{1,0:T(1,128)S(1)} %get-tuple-element.59) | copy-start | bytes 12292
  17.9 43.6 %copy-start.38 = (f32[1,1024]{1,0:T(1,128)}, f32[1,1024]{1,0:T(1,128)S(1)}, u32[]{:S(2)}) copy-start(f32[1,1024]{1,0:T(1,128)S(1)} %get-tuple-element.56) | copy-start | bytes 12292
  73.8 33.8 %copy-start.19 = (bf16[128,1024]{1,0:T(8,128)(2,1)S(1)}, bf16[128,1024]{1,0:T(8,128)(2,1)}, u32[]{:S(2)}) copy-start(bf16[128,1024]{1,0:T(8,128)(2,1)} %param.18) | copy-start | bytes 786436
  73.8 33.8 %copy-start.31 = (f32[1024]{0:T(1024)S(1)}, f32[1024]{0:T(1024)}, u32[]{:S(2)}) copy-start(f32[1024]{0:T(1024)} %convert_element_type.91) | copy-start | bytes 12292
  73.8 205.0 %reduce-scatter.5.cloned.1.call-start = ((), (), s32[]{:S(2)}) async-start(), calls=%async_computation.6 | async-start | bytes 5242880 | tf_op jit(solution)/shard_map/reduce_scatter | solution.py:345
  128.7 32.0 %copy-start.24 = (f32[512]{0:T(512)S(1)}, f32[512]{0:T(512)}, u32[]{:S(2)}) copy-start(f32[512]{0:T(512)} %copy-done.23) | copy-start | bytes 6148
  214.0 104.3 %reduce-scatter.3.cloned.1.call-start = ((), (), s32[]{:S(2)}) async-start(), calls=%async_computation.4 | async-start | bytes 2621440 | tf_op jit(solution)/shard_map/reduce_scatter | solution.py:298
  221.2 477.2 %all-reduce.19.cloned.1.call-start = ((), (), s32[]{:S(2)}) async-start(), calls=%async_computation.8 | async-start | bytes 25165824 | tf_op jit(solution)/shard_map/psum | solution.py:222
  237.5 41.3 %copy-start.8 = (bf16[128,2048]{1,0:T(8,128)(2,1)S(1)}, bf16[128,2048]{1,0:T(8,128)(2,1)}, u32[]{:S(2)}) copy-start(bf16[128,2048]{1,0:T(8,128)(2,1)} %param.12) | copy-start | bytes 1572868
  237.5 41.3 %copy-start.44 = (f32[128]{0:T(128)S(1)}, f32[128]{0:T(128)}, u32[]{:S(2)}) copy-start(f32[128]{0:T(128)} %copy-done.43) | copy-start | bytes 1540
  237.5 544.6 %all-reduce.17.cloned.1.call-start = ((), (), s32[]{:S(2)}) async-start(), calls=%async_computation.7 | async-start | bytes 2359296 | tf_op jit(solution)/shard_map/psum | solution.py:360
  239.9 78.5 %copy-start.11 = (bf16[128,2048]{1,0:T(8,128)(2,1)S(1)}, bf16[128,2048]{1,0:T(8,128)(2,1)}, u32[]{:S(2)}) copy-start(bf16[128,2048]{1,0:T(8,128)(2,1)} %param.22) | copy-start | bytes 1572868
  239.9 78.5 %copy-start.50 = (f32[128]{0:T(128)S(1)}, f32[128]{0:T(128)}, u32[]{:S(2)}) copy-start(f32[128]{0:T(128)} %get-tuple-element.62) | copy-start | bytes 1540
  278.9 39.5 %copy-start.9 = (f32[128,2048]{1,0:T(8,128)S(1)}, f32[128,2048]{1,0:T(8,128)}, u32[]{:S(2)}) copy-start(f32[128,2048]{1,0:T(8,128)} %reduce-scatter.5.cloned.1.call-done) | copy-start | bytes 3145732
  705.1 80.9 %copy-start.1 = (bf16[1024,160]{0,1:T(8,128)(2,1)S(1)}, bf16[1024,160]{0,1:T(8,128)(2,1)}, u32[]{:S(2)}) copy-start(bf16[1024,160]{0,1:T(8,128)(2,1)} %param.17) | copy-start | bytes 983044
  (39 other events, 187.7 us)
Sparse Core Ops, SparseCore 0:
  12.0 25.2 all-gather.2
  38.8 22.5 all-gather.4
  73.9 32.2 all-reduce.14
  214.2 44.5 reduce-scatter.4
  261.3 32.0 reduce-scatter.2
  298.5 399.8 all-reduce.18
  702.8 79.3 all-reduce.16

commit v2 on v1

v2 whole, which is shorter than its diff:
```python
import jax
import jax.numpy as jnp
from jax import lax
from jax.experimental import pallas as pl
from jax.experimental.pallas import tpu as pltpu
from jax.sharding import PartitionSpec as P

R = 128
CHUNK = 64
LINE = 4

def boundaries(bucket_row, length):
    position = jnp.arange(length, dtype=jnp.int32)
    short_len = length // 16
    middle_len = length // 4
    short_end = bucket_row[2] * short_len
    middle_end = short_end + bucket_row[1] * middle_len
    first_short = (position < short_end) & (position % short_len == 0)
    first_middle = (
        (position >= short_end)
        & (position < middle_end)
        & ((position - short_end) % middle_len == 0)
    )
    first_long = (position == middle_end) & (position < length)
    opening = first_short | first_middle | first_long
    return jnp.where(opening, 0.0, 1.0).astype(jnp.float32)


def shift_down(values, lag):
    return jnp.concatenate([jnp.zeros((lag,) + values.shape[1:], values.dtype), values[:-lag]], 0)


def estimate(micros):
    return pl.CostEstimate(flops=0, bytes_accessed=int(micros * 3.3e6), transcendentals=0)


TOKENS = (((0,), (0,)), ((), ()))
ACROSS = (((1,), (1,)), ((), ()))


def product(left, right, dims=(((1,), (0,)), ((), ()))):
    return lax.dot_general(left, right, dims, preferred_element_type=jnp.float32)


def fixed(shape):
    return pl.BlockSpec(shape, lambda *_: (0,) * len(shape), pipeline_mode=pl.Buffered(1))


def anywhere():
    return pl.BlockSpec(memory_space=pl.ANY)


def whole(shape):
    return pl.BlockSpec(shape, lambda *_: (0,) * len(shape))


def row_sums(values):
    if values[0].shape[0] != 8:
        return jnp.concatenate([jnp.sum(value, 0, keepdims=True) for value in values], 0)
    row = lax.broadcasted_iota(jnp.int32, (8, 128), 0)
    span = 1
    while len(values) > 1:
        low = (row // span) % 2 == 0
        values = [
            jnp.where(low, a, b) + pltpu.roll(jnp.where(low, b, a), 8 - span, axis=0)
            for a, b in zip(values[0::2], values[1::2])
        ]
        span *= 2
    return values[0]


def forward_kernel(chunk, n, length, scalars, step_ref, acts_ref, mix_ref, states_ref, carry):
    index = pl.program_id(0)
    tiles = carry.shape[1]

    @pl.when(index == 0)
    def _():
        carry[...] = jnp.zeros_like(carry)

    def eight(block, state):
        keep = scalars[(2 * n + 1) * length + index * (chunk // 8) + block]
        state = [value * keep for value in state]
        for i in range(8):
            rows = pl.ds(i, tiles, stride=8)
            step = step_ref[block, rows, :]
            act = acts_ref[block, rows, :]
            token = block * 8 + i
            base = (index * chunk + token) * n
            total = None
            for j in range(n):
                k = scalars[base + j]
                state[j] = state[j] + (step * k) * (act - state[j] * k)
                states_ref[token, j] = state[j]
                part = state[j] * scalars[n * length + base + j]
                total = part if total is None else total + part
            mix_ref[block, rows, :] = total
        return tuple(state)

    final = lax.fori_loop(0, chunk // 8, eight, tuple(carry[j] for j in range(n)))
    for j in range(n):
        carry[j] = final[j]


def scan_forward(values, step, acts, chunk, n, after):
    blocks, height, _ = step.shape
    tiles = height // 8
    length = blocks * 8
    wide = pl.BlockSpec((chunk // 8, height, 128), lambda c: (c, 0, 0))
    scalars = pl.BlockSpec(memory_space=pltpu.SMEM)
    return pl.pallas_call(
        lambda *refs: forward_kernel(
            chunk, n, length, *refs[:3], *refs[3 + len(after) :]
        ),
        grid=(length // chunk,),
        in_specs=[scalars, wide, wide] + [anywhere()] * len(after),
        out_specs=[wide, pl.BlockSpec((chunk, n, tiles, 128), lambda c: (c, 0, 0, 0))],
        out_shape=[
            jax.ShapeDtypeStruct(step.shape, jnp.float32),
            jax.ShapeDtypeStruct((length, n, tiles, 128), jnp.float32),
        ],
        scratch_shapes=[pltpu.VMEM((n, tiles, 128), jnp.float32)],
        compiler_params=pltpu.CompilerParams(vmem_limit_bytes=48 << 20),
        cost_estimate=estimate(16),
        name="scan_forward",
    )(values, step, acts, *after)


def backward_kernel(
    chunk,
    n,
    last,
    carry_in,
    sums_in,
    length,
    scalars,
    step_ref,
    acts_ref,
    ygrad_ref,
    states_ref,
    prior_ref,
    skip_ref,
    pre_ref,
    agrad_ref,
    kgrad_ref,
    qgrad_ref,
    fade_ref,
    sums_ref,
    carry,
    kred,
    qred,
):
    order = pl.program_id(0)
    index = last - order
    tiles = carry.shape[1]

    @pl.when(order == 0)
    def _():
        if carry_in is None:
            carry[...] = jnp.zeros_like(carry)
            sums_ref[...] = jnp.zeros_like(sums_ref)
        else:
            carry[...] = carry_in[...]
            sums_ref[...] = sums_in[...]

    skip = skip_ref[...]

    def token_step(block, i, adjoint, prior_of):
        rows = pl.ds(i, tiles, stride=8)
        step = step_ref[block, rows, :]
        act = acts_ref[block, rows, :]
        ygrad = ygrad_ref[block, rows, :]
        token = block * 8 + i
        where = index * chunk + token
        base = where * n
        drive = None
        loss = None
        kparts = []
        qparts = []
        for j in range(n):
            k = scalars[base + j]
            adj = adjoint[j] + ygrad * scalars[n * length + base + j]
            prior = prior_of(token, j)
            ka = adj * k
            kp = prior * k
            kparts.append((step * adj) * (act - (kp + kp)))
            qparts.append(states_ref[token, j] * ygrad)
            part = ka * kp
            drive = ka if drive is None else drive + ka
            loss = part if loss is None else loss + part
            adjoint[j] = adj - (step * k) * ka
        step_grad = act * drive - loss
        scaled = step_grad * step
        pre = scaled * (1.0 - step * (1.0 + scalars[2 * n * length + where]))
        pre_ref[block, rows, :] = pre
        agrad_ref[block, rows, :] = step * drive + ygrad * skip
        sums_ref[0] += pre.astype(jnp.bfloat16).astype(jnp.float32)
        sums_ref[1] += ygrad * act
        for first in range(0, n, 8):
            kred[token, first : first + 8, :] = row_sums(kparts[first : first + 8])
            qred[token, first : first + 8, :] = row_sums(qparts[first : first + 8])
        return scaled * step

    def eight(turn, adjoint):
        block = chunk // 8 - 1 - turn
        adjoint = list(adjoint)
        keep = scalars[(2 * n + 1) * length + index * (chunk // 8) + block]
        fades = [None] * 8
        for i in range(7, 0, -1):
            fades[i] = token_step(block, i, adjoint, lambda token, j: states_ref[token - 1, j])
        first = block == 0
        back = jnp.maximum(block * 8 - 1, 0)
        fades[0] = token_step(
            block,
            0,
            adjoint,
            lambda token, j: jnp.where(first, prior_ref[0, j], states_ref[back, j]) * keep,
        )
        fade_ref[pl.ds(pl.multiple_of(block * 8, 8), 8), :] = row_sums(fades)
        return tuple(value * keep for value in adjoint)

    final = lax.fori_loop(0, chunk // 8, eight, tuple(carry[j] for j in range(n)))
    for j in range(n):
        carry[j] = final[j]
    kgrad_ref[...] = jnp.sum(kred[...], -1)
    qgrad_ref[...] = jnp.sum(qred[...], -1)


def scan_backward(
    values, step, acts, ygrad, states, skip, chunk, n, span, before, after
):
    blocks, height, _ = step.shape
    tiles = height // 8
    length = blocks * 8
    last = span[1] - 1
    wide = pl.BlockSpec((chunk // 8, height, 128), lambda c: (last - c, 0, 0))
    scalars = pl.BlockSpec(memory_space=pltpu.SMEM)
    narrow = pl.BlockSpec((chunk, n), lambda c: (last - c, 0))
    kept = pl.BlockSpec((n, tiles, 128), lambda c: (0, 0, 0))
    pair = pl.BlockSpec((2, tiles, 128), lambda c: (0, 0, 0))
    in_specs = [
        scalars,
        wide,
        wide,
        wide,
        pl.BlockSpec((chunk, n, tiles, 128), lambda c: (last - c, 0, 0, 0)),
        pl.BlockSpec(
            (1, n, tiles, 128), lambda c: (jnp.maximum((last - c) * chunk - 1, 0), 0, 0, 0)
        ),
        pl.BlockSpec((tiles, 128), lambda c: (0, 0)),
    ]
    operands = [values, step, acts, ygrad, states, states, skip]
    aliases = {}
    base = len(operands)
    if before is not None:
        in_specs += [pair, kept] + [anywhere()] * 5
        operands += [before[5], before[6]] + list(before[:5])
        aliases = {base + 2 + turn: turn for turn in range(5)}
    in_specs += [anywhere()] * len(after)
    operands += list(after)

    def kernel(*refs):
        sums_in, carry_in = refs[base : base + 2] if before is not None else (None, None)
        outs = refs[len(operands) :]
        backward_kernel(
            chunk, n, last, carry_in, sums_in, length, *refs[:base], *outs[:6], *outs[6:]
        )

    return pl.pallas_call(
        kernel,
        grid=(span[1] - span[0],),
        in_specs=in_specs,
        out_specs=[
            wide,
            wide,
            narrow,
            narrow,
            pl.BlockSpec((chunk, 128), lambda c: (last - c, 0)),
            pair,
            kept,
        ],
        out_shape=[jax.ShapeDtypeStruct(step.shape, jnp.float32)] * 2
        + [jax.ShapeDtypeStruct((length, n), jnp.float32)] * 2
        + [
            jax.ShapeDtypeStruct((length, 128), jnp.float32),
            jax.ShapeDtypeStruct((2, tiles, 128), jnp.float32),
            jax.ShapeDtypeStruct((n, tiles, 128), jnp.float32),
        ],
        scratch_shapes=[
            pltpu.VMEM((chunk, n, 128), jnp.float32),
            pltpu.VMEM((chunk, n, 128), jnp.float32),
        ],
        input_output_aliases=aliases,
        compiler_params=pltpu.CompilerParams(vmem_limit_bytes=48 << 20),
        cost_estimate=estimate(32 * chunk * (span[1] - span[0]) / length),
        name="scan_backward",
    )(*operands)


def taps_of(inner, allows):
    return [inner] + [
        pltpu.roll(inner, lag, axis=0) * allows[:, lag - 1 : lag] for lag in range(1, 4)
    ]


def project_in(pieces, masks, w_in, allows, conv_w, conv_b, w_x_rows):
    rank = lax.axis_index("mp")
    rows, depth = pieces[0].shape
    count = len(pieces)
    length = rows * count
    channels = w_in.shape[2]
    tile = min(256, channels)
    width = w_x_rows.shape[0]
    places = jnp.stack([(rank ^ mask) * rows for mask in masks]).astype(jnp.int32)

    def kernel(places_ref, *refs):
        sources = refs[:count]
        w_ref, allow_ref, cw_ref, cb_ref, wx_ref = refs[count : count + 5]
        normed_ref, inner_ref, acts_ref, proj_ref = refs[count + 5 :]
        step = pl.program_id(0)

        @pl.when(step == 0)
        def _():
            for turn in range(count):
                at = pl.multiple_of(places_ref[turn], rows)
                normed_ref[pl.ds(at, rows), :] = sources[turn][...]
            proj_ref[...] = jnp.zeros_like(proj_ref)

        inner = jnp.dot(normed_ref[...], w_ref[0], preferred_element_type=jnp.float32)
        inner_ref[...] = inner
        weights = cw_ref[...].astype(jnp.float32)
        pre = cb_ref[...].astype(jnp.float32)
        for lag, tap in enumerate(taps_of(inner, allow_ref[...])):
            pre = pre + weights[lag : lag + 1] * tap
        acts = (pre * jax.nn.sigmoid(pre)).astype(jnp.bfloat16)
        acts_ref[...] = acts.astype(jnp.float32)
        proj_ref[...] += product(acts, wx_ref[...], ACROSS)

    column = pl.BlockSpec((length, tile), lambda c, places_ref: (0, c))
    return pl.pallas_call(
        kernel,
        grid_spec=pltpu.PrefetchScalarGridSpec(
            num_scalar_prefetch=1,
            grid=(channels // tile,),
            in_specs=[fixed((rows, depth))] * count
            + [
                pl.BlockSpec((1, depth, tile), lambda c, places_ref: (0, 0, c)),
                fixed(allows.shape),
                pl.BlockSpec((4, tile), lambda c, places_ref: (0, c)),
                pl.BlockSpec((1, tile), lambda c, places_ref: (0, c)),
                pl.BlockSpec((width, tile), lambda c, places_ref: (0, c)),
            ],
            out_specs=[whole((length, depth)), column, column, whole((length, width))],
        ),
        out_shape=[
            jax.ShapeDtypeStruct((length, depth), jnp.bfloat16),
            jax.ShapeDtypeStruct((length, channels), jnp.float32),
            jax.ShapeDtypeStruct((length, channels), jnp.float32),
            jax.ShapeDtypeStruct((length, width), jnp.float32),
        ],
        compiler_params=pltpu.CompilerParams(vmem_limit_bytes=56 << 20),
        cost_estimate=estimate(8),
        name="project_in",
    )(places, *pieces, w_in, allows, conv_w, conv_b.reshape(1, -1), w_x_rows)


def project_gate(pieces, masks, normed, w_in, w_out, after):
    rank = lax.axis_index("mp")
    rows, depth = pieces[0].shape
    count = len(pieces)
    length = rows * count
    channels = w_in.shape[2]
    tile = min(256, channels)
    places = jnp.stack([(rank ^ mask) * rows for mask in masks]).astype(jnp.int32)

    def kernel(places_ref, *refs):
        sources = refs[:count]
        normed_ref, w_ref, wo_ref = refs[count : count + 3]
        ograd_ref, silu_ref, grad_ref, slope_ref = refs[-4:]

        @pl.when(pl.program_id(0) == 0)
        def _():
            for turn in range(count):
                at = pl.multiple_of(places_ref[turn], rows)
                ograd_ref[pl.ds(at, rows), :] = sources[turn][...]

        gate = product(normed_ref[...], w_ref[0])
        gated_rows = product(ograd_ref[...], wo_ref[...], ACROSS)
        sig = jax.nn.sigmoid(gate)
        silu = gate * sig
        silu_ref[...] = silu
        grad_ref[...] = gated_rows * silu
        slope_ref[...] = gated_rows * sig * (1.0 + gate * (1.0 - sig))

    column = pl.BlockSpec((length, tile), lambda c, places_ref: (0, c))
    return pl.pallas_call(
        kernel,
        grid_spec=pltpu.PrefetchScalarGridSpec(
            num_scalar_prefetch=1,
            grid=(channels // tile,),
            in_specs=[fixed((rows, depth))] * count
            + [
                fixed((length, depth)),
                pl.BlockSpec((1, depth, tile), lambda c, places_ref: (1, 0, c)),
                pl.BlockSpec((tile, depth), lambda c, places_ref: (c, 0)),
            ]
            + [anywhere()] * len(after),
            out_specs=[whole((length, depth)), column, column, column],
        ),
        out_shape=[jax.ShapeDtypeStruct((length, depth), jnp.bfloat16)]
        + [jax.ShapeDtypeStruct((length, channels), jnp.float32)] * 3,
        compiler_params=pltpu.CompilerParams(vmem_limit_bytes=60 << 20),
        cost_estimate=estimate(11),
        name="project_gate",
    )(places, *pieces, normed, w_in, w_out, *after)


def finish_inner(agrad, proj_grad, w_x_rows, inner, allows, conv_w, conv_b, after):
    length, channels = inner.shape
    tile = min(256, channels)
    width = w_x_rows.shape[0]

    def kernel(ag_ref, pg_ref, wx_ref, inner_ref, allow_ref, cw_ref, cb_ref, *refs):
        out_ref, sums_ref = refs[-2:]
        acts_grad = ag_ref[...] + product(pg_ref[...], wx_ref[...])
        allow = allow_ref[...]
        taps = taps_of(inner_ref[...], allow)
        weights = cw_ref[...].astype(jnp.float32)
        pre = cb_ref[...].astype(jnp.float32)
        for lag, tap in enumerate(taps):
            pre = pre + weights[lag : lag + 1] * tap
        sig = jax.nn.sigmoid(pre)
        conv_grad = acts_grad * sig * (1.0 + pre * (1.0 - sig))
        rows = [jnp.sum(conv_grad * tap, 0, keepdims=True) for tap in taps]
        rows.append(jnp.sum(conv_grad, 0, keepdims=True))
        sums_ref[...] = jnp.concatenate(rows + [jnp.zeros((3, tile), jnp.float32)], 0)
        total = weights[0:1] * conv_grad
        for lag in range(1, 4):
            sent = conv_grad * allow[:, lag - 1 : lag] * weights[lag : lag + 1]
            total = total + pltpu.roll(sent, length - lag, axis=0)
        out_ref[...] = total.astype(jnp.bfloat16)

    column = pl.BlockSpec((length, tile), lambda c: (0, c))
    return pl.pallas_call(
        kernel,
        grid=(channels // tile,),
        in_specs=[
            column,
            fixed((length, width)),
            pl.BlockSpec((width, tile), lambda c: (0, c)),
            column,
            fixed(allows.shape),
            pl.BlockSpec((4, tile), lambda c: (0, c)),
            pl.BlockSpec((1, tile), lambda c: (0, c)),
        ]
        + [anywhere()] * len(after),
        out_specs=[column, pl.BlockSpec((8, tile), lambda c: (0, c))],
        out_shape=[
            jax.ShapeDtypeStruct((length, channels), jnp.bfloat16),
            jax.ShapeDtypeStruct((8, channels), jnp.float32),
        ],
        compiler_params=pltpu.CompilerParams(vmem_limit_bytes=56 << 20),
        cost_estimate=estimate(6),
        name="finish_inner",
    )(agrad, proj_grad, w_x_rows, inner, allows, conv_w, conv_b.reshape(1, -1), *after)


def factor_products(jobs, others, masks, depth, extra=None, after=()):
    rank = lax.axis_index("mp")
    count = len(masks)
    length = jobs[0][0].shape[0]
    rows = length // count
    part = depth // LINE
    channels = jobs[0][2][0].shape[1]
    factors_first = [job[3] for job in jobs]
    sizes = [(channels, part) if first else (part, channels) for first in factors_first]
    more = 0 if extra is None else extra.shape[1]
    own = line_place() % 2
    order = jnp.stack([1 - own, 3 - own, own, 2 + own])
    places = jnp.stack([(rank ^ mask) * rows for mask in masks])
    numbers = jnp.concatenate([order, places]).astype(jnp.int32)
    in_specs = []
    operands = [numbers]
    for rows_of, half, factors, _ in jobs:
        in_specs.append(pl.BlockSpec((length, part), lambda b, numbers_ref: (0, numbers_ref[b])))
        operands.append(rows_of)
        for other in others:
            for mask in masks:
                in_specs.append(
                    pl.BlockSpec(
                        (rows, part),
                        lambda b, numbers_ref, half=half: (0, half * LINE + numbers_ref[b]),
                    )
                )
                operands.append(other[mask])
        for factor in factors:
            in_specs.append(fixed(factor.shape))
            operands.append(factor)
    if more:
        in_specs.append(
            pl.BlockSpec((1, more, channels), lambda b, numbers_ref: (numbers_ref[b], 0, 0))
        )
        operands.append(extra)
    in_specs += [anywhere()] * len(after)
    operands += list(after)

    def kernel(numbers_ref, *refs):
        scratch = refs[-1]
        outs = refs[len(operands) - 1 : -1]
        step = pl.program_id(0)
        at = 0
        for turn, first in enumerate(factors_first):
            source = refs[at]
            at += 1
            total = None
            groups = [refs[at + g * count : at + (g + 1) * count] for g in range(len(others))]
            at += len(others) * count
            for g in range(len(others) + 1):
                if g:
                    for piece, ref in enumerate(groups[g - 1]):
                        place = pl.multiple_of(numbers_ref[LINE + piece], rows)
                        scratch[pl.ds(place, rows), :] = ref[...]
                    value = scratch[...]
                else:
                    value = source[...]
                factor = refs[at + g][...]
                pair = (factor, value) if first else (value, factor)
                term = product(*pair, TOKENS)
                total = term if total is None else total + term
            at += len(others) + 1
            total = total.astype(jnp.bfloat16)
            height = sizes[turn][0]

            @pl.when(step < LINE // 2)
            def _():
                outs[2 * turn][0, :height, :] = total

            @pl.when(step >= LINE // 2)
            def _():
                outs[2 * turn + 1][0, :height, :] = total

        if more:

            @pl.when(step < LINE // 2)
            def _():
                outs[0][0, sizes[0][0] :, :] = refs[at][0]

            @pl.when(step >= LINE // 2)
            def _():
                outs[1][0, sizes[0][0] :, :] = refs[at][0]

    early = lambda b, numbers_ref: (jnp.minimum(b, LINE // 2 - 1), 0, 0)
    late = lambda b, numbers_ref: (jnp.maximum(b - LINE // 2, 0), 0, 0)
    return pl.pallas_call(
        kernel,
        grid_spec=pltpu.PrefetchScalarGridSpec(
            num_scalar_prefetch=1,
            grid=(LINE,),
            in_specs=in_specs,
            out_specs=[
                pl.BlockSpec((1, height + more, width), index)
                for height, width in sizes
                for index in (early, late)
            ],
            scratch_shapes=[pltpu.VMEM((length, part), jnp.bfloat16)],
        ),
        out_shape=[
            jax.ShapeDtypeStruct((LINE // 2, height + more, width), jnp.bfloat16)
            for height, width in sizes
            for _ in range(2)
        ],
        compiler_params=pltpu.CompilerParams(vmem_limit_bytes=56 << 20),
        cost_estimate=estimate(4 * len(jobs)),
        name="factor_products",
    )(*operands)


def add_blocks(kept, got, bit, after):
    count, rows, width = kept.shape
    own = (line_place() // bit) % 2
    order = jnp.stack([1 - own, own]) if count == 2 else jnp.zeros((1,), jnp.int32)

    def kernel(order_ref, kept_ref, got_ref, *refs):
        total = kept_ref[...].astype(jnp.float32) + got_ref[...].astype(jnp.float32)
        total = total.astype(jnp.bfloat16)
        if count == 1:
            refs[-1][...] = total
            return
        step = pl.program_id(0)

        @pl.when(step == 0)
        def _():
            refs[-2][...] = total

        @pl.when(step == 1)
        def _():
            refs[-1][...] = total

    block = pl.BlockSpec((1, rows, width), lambda b, order_ref: (order_ref[b], 0, 0))
    result = pl.BlockSpec((1, rows, width), lambda b, order_ref: (0, 0, 0))
    return pl.pallas_call(
        kernel,
        grid_spec=pltpu.PrefetchScalarGridSpec(
            num_scalar_prefetch=1,
            grid=(count,),
            in_specs=[block, block] + [anywhere()] * len(after),
            out_specs=[result] * count,
        ),
        out_shape=[jax.ShapeDtypeStruct((1, rows, width), jnp.bfloat16)] * count,
        compiler_params=pltpu.CompilerParams(vmem_limit_bytes=40 << 20),
        cost_estimate=estimate(1),
        name="add_blocks",
    )(order.astype(jnp.int32), kept, got, *after)


def project_back(pre, w_dt, key_grad, query_grad, keys, fade, after):
    length, channels = pre.shape
    rank_width = w_dt.shape[0]
    n = keys.shape[1]
    tile = min(256, length)

    def kernel(pre_ref, w_ref, kg_ref, qg_ref, keys_ref, fade_ref, *refs):
        out_ref = refs[-1]
        out_ref[:, :rank_width] = product(pre_ref[...].astype(jnp.bfloat16), w_ref[...], ACROSS)
        spread = jnp.sum(fade_ref[...], 1, keepdims=True)
        out_ref[:, rank_width : rank_width + n] = kg_ref[...] - 2.0 * keys_ref[...] * spread
        out_ref[:, rank_width + n :] = qg_ref[...]

    rows = lambda width: pl.BlockSpec((tile, width), lambda c: (c, 0))
    return pl.pallas_call(
        kernel,
        grid=(length // tile,),
        in_specs=[rows(channels), fixed(w_dt.shape), rows(n), rows(n), rows(n), rows(128)]
        + [anywhere()] * len(after),
        out_specs=rows(rank_width + 2 * n),
        out_shape=jax.ShapeDtypeStruct((length, rank_width + 2 * n), jnp.float32),
        compiler_params=pltpu.CompilerParams(vmem_limit_bytes=40 << 20),
        cost_estimate=estimate(3),
        name="project_back",
    )(pre, w_dt, key_grad, query_grad, keys, fade, *after)


def narrow_products(low_rank, pre, proj_grad, acts, after):
    length, channels = pre.shape
    tile = min(256, channels)
    rank_width, width = low_rank.shape[1], proj_grad.shape[1]
    padding = -(rank_width + width) % (16 * LINE)
    total = rank_width + width + padding

    def kernel(low_ref, pre_ref, pg_ref, acts_ref, *refs):
        out_ref = refs[-1]
        first = product(low_ref[...], pre_ref[...].astype(jnp.bfloat16), TOKENS)
        out_ref[:rank_width, :] = first.astype(jnp.bfloat16)
        second = product(pg_ref[...], acts_ref[...].astype(jnp.bfloat16), TOKENS)
        out_ref[rank_width : rank_width + width, :] = second.astype(jnp.bfloat16)
        if padding:
            out_ref[rank_width + width :, :] = jnp.zeros((padding, tile), jnp.bfloat16)

    column = pl.BlockSpec((length, tile), lambda c: (0, c))
    return pl.pallas_call(
        kernel,
        grid=(channels // tile,),
        in_specs=[fixed(low_rank.shape), column, fixed(proj_grad.shape), column]
        + [anywhere()] * len(after),
        out_specs=pl.BlockSpec((total, tile), lambda c: (0, c)),
        out_shape=jax.ShapeDtypeStruct((total, channels), jnp.bfloat16),
        compiler_params=pltpu.CompilerParams(vmem_limit_bytes=48 << 20),
        cost_estimate=estimate(4),
        name="narrow_products",
    )(low_rank, pre, proj_grad, acts, *after)


def to_tiles(values):
    length, channels = values.shape
    parts = values.reshape(length // 8, 8, channels // 128, 128).transpose(0, 2, 1, 3)
    return parts.reshape(length // 8, channels // 16, 128)


def from_tiles(values):
    blocks, height, _ = values.shape
    parts = values.reshape(blocks, height // 8, 8, 128).transpose(0, 2, 1, 3)
    return parts.reshape(blocks * 8, height * 16)


def swap(values, axis, offset):
    size = lax.axis_size(axis)
    return lax.ppermute(values, axis, [(i, i ^ offset) for i in range(size)])


def bits_down(size):
    bits = []
    bit = size // 2
    while bit:
        bits.append(bit)
        bit //= 2
    return bits


def gather_pieces(values, axis):
    pieces = {0: values}
    for bit in bits_down(lax.axis_size(axis)):
        for mask in list(pieces):
            pieces[mask | bit] = swap(pieces[mask], axis, bit)
    return pieces


def nothing(other):
    return other[(slice(0, 1),) * other.ndim].reshape(()).astype(jnp.float32) * 0.0


def sum_mp(values, after=None):
    rank = lax.axis_index("mp")
    half = values.shape[0] // 2
    odd = rank % 2
    mine = lax.dynamic_slice_in_dim(values, odd * half, half, 0)
    other = lax.dynamic_slice_in_dim(values, (1 - odd) * half, half, 0)
    mine = mine + swap(other, "mp", 1)
    bit = 2
    while bit < lax.axis_size("mp"):
        mine = mine + swap(mine, "mp", bit)
        bit *= 2
    if after is not None:
        mine = mine + nothing(after)
    other = swap(mine, "mp", 1)
    whole = jnp.zeros(values.shape, values.dtype)
    whole = lax.dynamic_update_slice_in_dim(whole, mine, odd * half, 0)
    return lax.dynamic_update_slice_in_dim(whole, other, (1 - odd) * half, 0)


def scatter_mp(values):
    rank = lax.axis_index("mp")
    size = lax.axis_size("mp")
    rows = values.shape[0] // size
    blocks = values.reshape(1, size, rows, values.shape[1])
    bit = 1
    while bit < size:
        left, here, _, width = blocks.shape
        pairs = blocks.reshape(left, here // 2, 2, rows, width)
        own = (rank // bit) % 2
        keep = lax.dynamic_index_in_dim(pairs, own, 2, keepdims=False)
        give = lax.dynamic_index_in_dim(pairs, 1 - own, 2, keepdims=False).astype(jnp.bfloat16)
        blocks = keep.astype(jnp.float32) + swap(give, "mp", bit).astype(jnp.float32)
        bit *= 2
    return blocks.reshape(rows, values.shape[1])


def trade_side(values):
    side = lax.axis_size("dp") // LINE
    rank = lax.axis_index("dp") % side
    width = values.shape[1] // side
    parts = []
    for mask in range(side):
        part = lax.dynamic_slice_in_dim(values, (rank ^ mask) * width, width, 1)
        parts.append(swap(part, "dp", mask) if mask else part)
    return parts


def line_place():
    return lax.axis_index("dp") // (lax.axis_size("dp") // LINE)


def near_step(give, keep, after):
    side = lax.axis_size("dp") // LINE
    return add_blocks(keep, swap(give, "dp", side), 2, after)


def far_step(give, keep, after):
    side = lax.axis_size("dp") // LINE
    return add_blocks(keep, swap(give, "dp", 2 * side), 2, after)[0][0]


def spread(piece, apart=False):
    rows = piece.shape[0]
    held = [(piece, [0])]
    for bit in bits_down(lax.axis_size("dp")):
        if apart:
            parts = [[one] for one in held]
        elif len(held) > 1:
            parts = [held[:-1], held[-1:]] if bit == 1 else [held]
        else:
            parts = [held]
        for part in parts:
            masks = [mask for _, group in part for mask in group]
            arrays = [array for array, _ in part]
            sent = arrays[0] if len(arrays) == 1 else jnp.concatenate(arrays, 0)
            held.append((swap(sent, "dp", bit), [mask | bit for mask in masks]))
    table = {mask: (array, which) for array, masks in held for which, mask in enumerate(masks)}
    return table, [array for array, _ in held[1:]]


def join(pieces, rows, height, lines_first, target=None, buffer=None):
    side = lax.axis_size("dp") // LINE
    rank = lax.axis_index("dp")
    masks = list(pieces)
    count = len(masks)
    width = pieces[masks[0]][0].shape[1]
    more = rows - height
    origin = jnp.stack([rank ^ mask for mask in masks])
    line, flank = origin // side, origin % side
    down, right = (line, flank) if lines_first else (flank, line)
    grid_down, grid_right = (LINE, side) if lines_first else (side, LINE)
    shape = (height * grid_down, width * grid_right)
    low_shape = (more * grid_down, width * grid_right)
    if width % 128:
        total = jnp.zeros(shape, jnp.float32)
        low = jnp.zeros(low_shape, jnp.float32)
        for step, mask in enumerate(masks):
            array, which = pieces[mask]
            value = array[which * rows : (which + 1) * rows].astype(jnp.float32)
            right_at = right[step] * width
            total = lax.dynamic_update_slice(total, value[:height], (down[step] * height, right_at))
            if more:
                low = lax.dynamic_update_slice(low, value[height:], (down[step] * more, right_at))
        if target is not None:
            if buffer is None:
                buffer = jnp.zeros((2,) + shape, jnp.float32)
            total = lax.dynamic_update_slice(buffer, total[None], (target, 0, 0))
        return (total, low) if more else total
    places = jnp.stack([down, right]).astype(jnp.int32)

    def kernel(places_ref, *refs):
        outs = refs[-2:] if more else refs[-1:]
        step = pl.program_id(0)
        for turn in range(count):

            @pl.when(step == turn)
            def _():
                value = refs[turn][:height, :].astype(jnp.float32)
                outs[0][...] = value if target is None else value[None]
                if more:
                    outs[1][...] = refs[turn][height:, :].astype(jnp.float32)

    in_specs = [
        pl.BlockSpec((rows, width), lambda step, places_ref, which=pieces[mask][1]: (which, 0))
        for mask in masks
    ]
    operands = [places] + [pieces[mask][0] for mask in masks]
    aliases = {}
    if target is None:
        out_shapes = [jax.ShapeDtypeStruct(shape, jnp.float32)]
        out_specs = [
            pl.BlockSpec(
                (height, width),
                lambda step, places_ref: (places_ref[0, step], places_ref[1, step]),
            )
        ]
    else:
        out_shapes = [jax.ShapeDtypeStruct((2,) + shape, jnp.float32)]
        out_specs = [
            pl.BlockSpec(
                (1, height, width),
                lambda step, places_ref: (target, places_ref[0, step], places_ref[1, step]),
            )
        ]
        if buffer is not None:
            in_specs.append(pl.BlockSpec(memory_space=pl.ANY))
            operands.append(buffer)
            aliases = {len(operands) - 1: 0}
    if more:
        out_shapes.append(jax.ShapeDtypeStruct(low_shape, jnp.float32))
        out_specs.append(
            pl.BlockSpec(
                (more, width), lambda step, places_ref: (places_ref[0, step], places_ref[1, step])
            )
        )
    results = pl.pallas_call(
        kernel,
        grid_spec=pltpu.PrefetchScalarGridSpec(
            num_scalar_prefetch=1,
            grid=(count,),
            in_specs=in_specs,
            out_specs=out_specs,
        ),
        out_shape=out_shapes,
        input_output_aliases=aliases,
        compiler_params=pltpu.CompilerParams(vmem_limit_bytes=40 << 20),
        cost_estimate=estimate(count * 0.6),
        name="join",
    )(*operands)
    return results if more else results[0]


def tie(values, other):
    return values + nothing(other).astype(values.dtype)


def on_device(
    block_input,
    norm_gain,
    w_in,
    conv_w,
    conv_b,
    w_x,
    w_dt,
    b_dt,
    d_skip,
    w_out,
    out_grad,
    seq_counts,
):
    row_count, depth = block_input.shape
    size = lax.axis_size("mp")
    side = lax.axis_size("dp") // LINE
    length = row_count * size
    channels = w_in.shape[2]
    state_size = (w_x.shape[1] - R) // 2
    source_rows = block_input.astype(jnp.float32)
    inv_root = lax.rsqrt(jnp.mean(source_rows * source_rows, -1, keepdims=True) + 1e-05)
    normed = (source_rows * inv_root * norm_gain).astype(jnp.bfloat16)
    normed_pieces = gather_pieces(normed, "mp")
    masks = list(normed_pieces)
    ograd_pieces = gather_pieces(tie(out_grad, normed_pieces[masks[1]]), "mp")
    both = jnp.concatenate([normed, out_grad], 1)
    beside = [swap(both, "dp", mask) for mask in range(1, side)]
    keep_mask = boundaries(seq_counts[0], length)
    allow_two = keep_mask * shift_down(keep_mask, 1)
    allow_three = allow_two * shift_down(keep_mask, 2)
    allows = jnp.stack([keep_mask, allow_two, allow_three], 1)
    w_x_rows = w_x.T
    group_normed, inner, acts, proj_part = project_in(
        list(normed_pieces.values()),
        masks,
        w_in,
        allows,
        conv_w,
        conv_b,
        w_x_rows,
    )
    group_ograd, gate_silu, mixer_grad, gate_slope = project_gate(
        list(ograd_pieces.values()), list(ograd_pieces), group_normed, w_in, w_out, beside
    )
    proj = sum_mp(proj_part, gate_silu)
    others = []
    for rows in beside:
        others.append(gather_pieces(tie(rows, proj), "mp"))
    low_rank = proj[:, :R].astype(jnp.bfloat16)
    keys = proj[:, R : R + state_size]
    queries = proj[:, R + state_size :]
    beta = jax.nn.sigmoid(product(low_rank, w_dt) + b_dt)
    key_square = jnp.sum(keys * keys, 1)
    step_size = beta / (1.0 + beta * key_square[:, None])
    scalars = jnp.concatenate(
        [keys.reshape(-1), queries.reshape(-1), key_square, keep_mask[::8]]
    )
    step_tiles = to_tiles(step_size)
    acts_tiles = to_tiles(acts)
    mix_tiles, states = scan_forward(
        scalars,
        step_tiles,
        acts_tiles,
        CHUNK,
        state_size,
        (gate_silu, gate_slope),
    )
    mixer = from_tiles(mix_tiles) + d_skip * acts
    gated = (mixer * gate_silu).astype(jnp.bfloat16)
    gate_grad = (mixer * gate_slope).astype(jnp.bfloat16)
    back_args = (
        scalars,
        step_tiles,
        acts_tiles,
        to_tiles(mixer_grad),
        states,
        d_skip.astype(jnp.float32).reshape(channels // 128, 128),
        CHUNK,
        state_size,
    )
    chunks = length // CHUNK
    fetched = [rows[masks[1]] for rows in others]
    later = scan_backward(*back_args, (chunks // 2, chunks), None, [gated, gate_grad] + fetched)
    gate_job = (group_normed, 0, trade_side(gate_grad), False)
    out_job = (group_ograd, 1, trade_side(gated), True)
    gate_give, gate_keep, out_give, out_keep = factor_products(
        [gate_job, out_job], others, masks, depth, None, (later[6],)
    )
    pre_tiles, agrad_tiles, key_grad, query_grad, fade, sums, _ = scan_backward(
        *back_args, (0, chunks // 2), later, (gate_give, out_give)
    )
    pre_full = from_tiles(pre_tiles)
    gate_give, gate_keep = near_step(gate_give, gate_keep, (fade,))
    proj_back = project_back(pre_full, w_dt, key_grad, query_grad, keys, fade, (gate_give,))
    out_give, out_keep = near_step(out_give, out_keep, (proj_back,))
    proj_grad = sum_mp(proj_back).astype(jnp.bfloat16)
    gate_piece = far_step(gate_give, gate_keep, ())
    gate_pieces, gate_came = spread(gate_piece)
    inner_grad, conv_sums = finish_inner(
        from_tiles(agrad_tiles),
        proj_grad,
        w_x_rows,
        inner,
        allows,
        conv_w,
        conv_b,
        (out_give, gate_piece),
    )
    inner_parts = trade_side(inner_grad)
    out_piece = far_step(out_give, out_keep, (inner_grad,))
    out_pieces, out_came = spread(out_piece)
    narrow = narrow_products(low_rank, pre_full, proj_grad, acts, (inner_grad,))
    branch_out = scatter_mp(product(tie(gated, inner_grad), w_out))
    block_out = (source_rows + branch_out).astype(jnp.bfloat16)
    extra = sum((part.astype(jnp.float32) for part in trade_side(narrow))).astype(jnp.bfloat16)
    width = channels // side
    tall = narrow.shape[0] // LINE
    extra = extra.reshape(LINE, tall, width)
    inner_job = (group_normed, 0, inner_parts, False)
    inner_give, inner_keep = factor_products([inner_job], others, masks, depth, extra)
    w_in_grad = join(gate_pieces, depth // LINE, depth // LINE, True, 1)
    w_out_grad = join(out_pieces, width, width, False)
    inner_give, inner_keep = near_step(inner_give, inner_keep, (out_piece, gate_came[0]))
    inner_piece = far_step(inner_give, inner_keep, gate_came[1:3] + out_came[:1])
    normed_grad = scatter_mp(
        product(inner_grad, w_in[0], ACROSS) + product(gate_grad, w_in[1], ACROSS)
    )
    scaled = normed_grad * norm_gain
    gain_part = jnp.sum(normed_grad * source_rows * inv_root, 0)
    cubed = inv_root * inv_root * inv_root
    input_grad = inv_root * scaled - source_rows * cubed * jnp.mean(
        scaled * source_rows, -1, keepdims=True
    )
    input_grad = (out_grad.astype(jnp.float32) + input_grad).astype(jnp.bfloat16)
    for bit in bits_down(size):
        gain_part = gain_part + swap(gain_part, "mp", bit)
    partial = [conv_sums[:5].reshape(-1), sums.reshape(-1), gain_part]
    partial = jnp.concatenate([value.astype(jnp.bfloat16) for value in partial])
    used = partial.shape[0]
    count = -(-used // (16 * width)) * 16
    partial = jnp.concatenate([partial, jnp.zeros(count * width - used, jnp.bfloat16)])
    tail = jnp.concatenate([inner_piece, partial.reshape(count, width)], 0)
    pieces, _ = spread(tail, True)
    w_in_grad, low = join(pieces, tail.shape[0], depth // LINE, True, 0, w_in_grad)
    low = low.reshape(LINE, -1, channels)
    narrow = low[:, :tall].reshape(LINE * tall, channels)
    total = low[:, tall : tall + count].reshape(LINE, count, side, width)
    total = jnp.sum(total, (0, 2)).reshape(-1)
    return (
        block_out,
        input_grad,
        total[7 * channels : used],
        w_in_grad,
        total[: 4 * channels].reshape(4, channels),
        total[4 * channels : 5 * channels],
        narrow[R : 2 * R + 2 * state_size].T,
        narrow[:R],
        total[5 * channels : 6 * channels],
        total[6 * channels : 7 * channels],
        w_out_grad,
    )


def solution(mesh):
    in_specs = (
        P(("dp", "mp"), None),
        P(),
        P(None, None, "mp"),
        P(None, "mp"),
        P("mp"),
        P("mp", None),
        P(None, "mp"),
        P("mp"),
        P("mp"),
        P("mp", None),
        P(("dp", "mp"), None),
        P("dp", None),
    )
    out_specs = (
        P(("dp", "mp"), None),
        P(("dp", "mp"), None),
        P(),
        P(None, None, "mp"),
        P(None, "mp"),
        P("mp"),
        P("mp", None),
        P(None, "mp"),
        P("mp"),
        P("mp"),
        P("mp", None),
    )
    return jax.shard_map(
        on_device, mesh=mesh, in_specs=in_specs, out_specs=out_specs, check_vma=False
    )
```

time: 801 us -> 481 us (0.60)
  waiting for transfers between devices: 508 us -> 221 us
  blocking collectives: 91 us -> 0 us
  Pallas kernels: 51.1 us -> 137 us
  matrix products: 61.9 us -> 12.9 us
  starting transfers between devices: 0.71 us -> 49.6 us
  other arithmetic: 48 us -> 23.7 us
  local copies, waits for them, and re-layouts: 16.5 us -> 30.1 us
  between operations: 16.5 us -> 5.49 us
    psum x3 -> x0, waiting for transfers between devices: 476 us -> none  [the longest x1 377 us: sum_over(): return lax.psum(values.astype(jnp.bfloat16), axis).astype(jnp.float32)]
    ppermute x0 -> x47, waiting for transfers between devices: none -> 221 us  [swap(): return lax.ppermute(values, axis, [(i, i ^ offset) for i in range(size)])]
    psum x3 -> x0, blocking collectives: 91 us -> none  [the longest x1 37.9 us: on_device(): norm_gain_grad = lax.psum(gain_part, ('dp', 'mp'))]
    pallas_call x2 -> x19, Pallas kernels: 51.1 us -> 137 us  [the longest x2 38.6 us: scan_backward(): pl.pallas_call(kernel, grid=(span[1] - span[0],), in_specs=in_specs, out_...]
    ppermute x0 -> x47, starting transfers between devices: none -> 49.6 us  [swap(): return lax.ppermute(values, axis, [(i, i ^ offset) for i in range(size)])]
    dot_general x15 -> x4, matrix products: 61.9 us -> 12.9 us  [product(): lax.dot_general(left, right, dims, preferred_element_type=jnp.float32)]
    all_gather x2 -> x0, waiting for transfers between devices: 31.3 us -> none  [the longest x1 19.4 us: on_device(): all_normed = lax.all_gather(normed, 'mp', axis=0, tiled=True)]
    reduce_sum x5 -> x2, other arithmetic: 13.4 us -> 0.18 us  [on_device(): total = jnp.sum(total, (0, 2)).reshape(-1)]
  transfers between devices with their start and end apart: 7 -> 47, of which waited for: 5 -> 21; matrix products, arithmetic and copies ran while one was open for 8% -> 9% of each run, Pallas kernels for 0% -> 23%
where the time goes in v2:
time: 481 us; the launch traced here: 480 us
  waiting for transfers between devices  221 us (46%)
  Pallas kernels  137 us (28%)
  starting transfers between devices  49.6 us (10%)
  local copies, waits for them, and re-layouts  30.1 us (6%)
  other arithmetic  23.7 us (5%)
  matrix products  12.9 us (3%)
  between operations  5.49 us (1%)
    ppermute x47, waiting for transfers between devices, swap(): return lax.ppermute(values, axis, [(i, i ^ offset) for i in range(size)])  221 us
    ppermute x47, starting transfers between devices, swap(): return lax.ppermute(values, axis, [(i, i ^ offset) for i in range(size)])  49.6 us
    pallas_call x2, Pallas kernels, scan_backward(): pl.pallas_call(kernel, grid=(span[1] - span[0],), in_specs=in_specs, out_...  38.6 us
    pallas_call x3, Pallas kernels, join(): pl.pallas_call(kernel, grid_spec=pltpu.PrefetchScalarGridSpec(num_scalar_...  19.9 us
    pallas_call x2, Pallas kernels, factor_products(): pl.pallas_call(kernel, grid_spec=pltpu.PrefetchScalarGridSpec(num_scalar_...  19.4 us
    pallas_call x1, Pallas kernels, scan_forward(): pl.pallas_call(lambda *refs: forward_kernel(chunk, n, length, *refs[:3],...  16.7 us
    dot_general x4, matrix products, product(): lax.dot_general(left, right, dims, preferred_element_type=jnp.float32)  12.9 us
    unnamed x130, local copies, waits for them, and re-layouts  12.3 us
  transfers between devices with their start and end apart: 47, of which 21 were waited for; matrix products, arithmetic and copies ran while one was open for 9% of the time, Pallas kernels for 23%

profile of v2, /device:TPU:0, one launch (start us, length us, event | category | flops | bytes accessed | tf_op | source)
XLA Modules:
  0.0 479.5 jit_solution(12842161900964679300)
XLA Ops:
  12.5 6.5 %collective-permute-done.refs_1_ = bf16[128,2048]{1,0:T(8,128)(2,1)} collective-permute-done((bf16[128,2048]{1,0:T(8,128)(2,1)S(1)}, bf16[128,2048]{1,0:T(8,128)(2,1)}, u32[]{:S(2)}, u32[]{:S(2)}) %collective-permute-start) | collective-permute-done | bytes 524320 | tf_op jit(solution)/shard_map/ppermute | solution.py:686
  25.0 9.1 %project_in.1 = (bf16[512,2048]{1,0:T(8,128)(2,1)}, f32[512,1024]{1,0:T(8,128)}, f32[512,1024]{1,0:T(8,128)}, f32[512,160]{1,0:T(8,128)}) custom-call(s32[4]{0:T(128)} %pad_add_fusion.2.places_ref, bf16[128,2048]{1,0:T(8,128)(2,1)} %copy-done.45, bf16[128,2048]{1,0:T(8,128)(2,1)} %collective-permute-done.refs_1_, ...), custom_call_target="tpu_custom_call" | custom-call | bytes 26400000 | tf_op jit(solution)/shard_map/project_in/pallas_call | solution.py:339
  39.7 11.6 %project_gate.1 = (bf16[512,2048]{1,0:T(8,128)(2,1)}, f32[512,1024]{1,0:T(8,128)}, f32[512,1024]{1,0:T(8,128)}, f32[512,1024]{1,0:T(8,128)}) custom-call(s32[4]{0:T(128)} %pad_add_fusion.2.places_ref, bf16[128,2048]{1,0:T(8,128)(2,1)} %copy-done.53, bf16[128,2048]{1,0:T(8,128)(2,1)} %copy-done.55, bf16[128,2048]{1,0:T(8,128)(2,1)} %copy-done.56, ...), custom_call_target="tpu_custom_call" | custom-call | bytes 36300000 | tf_op jit(solution)/shard_map/project_gate/pallas_call | solution.py:395
  60.3 16.7 %scan_forward.1 = (f32[64,64,128]{2,1,0:T(8,128)S(1)}, f32[512,16,8,128]{3,2,1,0:T(8,128)}) custom-call(f32[16960]{0:T(1024)S(1)} %pad_maximum_fusion.4.refs_0_, f32[64,64,128]{2,1,0:T(8,128)S(1)} %divide_bitcast_fusion.refs_1_, f32[64,64,128]{2,1,0:T(8,128)} %bitcast.138, f32[512,1024]{1,0:T(8,128)} %get-tuple-element.52.refs_3_, ...), custom_call_target="tpu_custom_call" | custom-call | bytes 52800000 | tf_op jit(solution)/shard_map/scan_forward/pallas_call | solution.py:110
  77.0 5.6 %collective-permute-done.10.refs_9_.refs_2_ = bf16[128,4096]{1,0:T(8,128)(2,1)S(1)} collective-permute-done((bf16[128,4096]{1,0:T(8,128)(2,1)}, bf16[128,4096]{1,0:T(8,128)(2,1)S(1)}, u32[]{:S(2)}, u32[]{:S(2)}) %collective-permute-start.10) | collective-permute-done | bytes 1048608 | tf_op jit(solution)/shard_map/ppermute | solution.py:686
  91.2 19.3 %scan_backward.2 = (f32[64,64,128]{2,1,0:T(8,128)S(1)}, f32[64,64,128]{2,1,0:T(8,128)}, f32[512,16]{1,0:T(8,128)S(1)}, f32[512,16]{1,0:T(8,128)S(1)}, f32[512,12...) custom-call(f32[16960]{0:T(1024)S(1)} %pad_maximum_fusion.4.refs_0_, f32[64,64,128]{2,1,0:T(8,128)} %copy-done, ...), custom_call_target="tpu_custom_call" | custom-call | bytes 52800000 | tf_op jit(solution)/shard_map/scan_backward/pallas_call | solution.py:268
  112.5 11.8 %factor_products.2 = (bf16[2,512,512]{2,1,0:T(8,128)(2,1)}, bf16[2,512,512]{2,1,0:T(8,128)(2,1)}, bf16[2,512,512]{2,1,0:T(8,128)(2,1)}, bf16[2,512,512]{2,1,0:T(8,128)(2,1)}) custom-call(s32[8]{0:T(128)} %concatenate.85.numbers_ref, bf16[512,2048]{1,0:T(8,128)(2,1)} %get-tuple-element.51.refs_4_.refs_0_, ...), custom_call_target="tpu_custom_call" | custom-call | bytes 26400000 | tf_op jit(solution)/shard_map/factor_products/pallas_call | solution.py:553
  127.3 19.4 %scan_backward.3 = (f32[64,64,128]{2,1,0:T(8,128)S(1)}, f32[64,64,128]{2,1,0:T(8,128)}, f32[512,16]{1,0:T(8,128)S(1)}, f32[512,16]{1,0:T(8,128)S(1)}, f32[512,12...) custom-call(f32[16960]{0:T(1024)S(1)} %pad_maximum_fusion.4.refs_0_,, ...), custom_call_target="tpu_custom_call", output_to_operand_aliasing={{0}: (9, {}), {1}: (10, {}), {2}: (11, {}), {3}: (12, {}), ... | custom-call | bytes 52800000 | tf_op jit(solution)/shard_map/scan_backward/pallas_call | solution.py:268
  169.0 21.1 %collective-permute-done.19.got_ref = bf16[2,512,512]{2,1,0:T(8,128)(2,1)} collective-permute-done((bf16[2,512,512]{2,1,0:T(8,128)(2,1)}, bf16[2,512,512]{2,1,0:T(8,128)(2,1)}, u32[]{:S(2)}, u32[]{:S(2)}) %collective-permute-start.19) | collective-permute-done | bytes 1048608 | tf_op jit(solution)/shard_map/ppermute | solution.py:686
  194.8 6.8 %finish_inner.1 = (bf16[512,1024]{1,0:T(8,128)(2,1)}, f32[8,1024]{1,0:T(8,128)}) custom-call(f32[512,1024]{1,0:T(8,128)} %bitcast.143, bf16[512,160]{1,0:T(8,128)(2,1)} %convert_element_type.146.pg_ref, bf16[160,1024]{1,0:T(8,128)(2,1)} %bitcast.152, f32[512,1024]{1,0:T(8,128)} %get-tuple-element.75.inner_ref, f32[512,3]{1,0:T(8,128)} %copy.44.refs_5_.allow_ref, ...), custom_call_target="tpu_custom_call" | custom-call | bytes 19800000 | tf_op jit(solution)/shard_map/finish_inner/pallas_call | solution.py:443
  220.5 27.8 %collective-permute-done.28.got_ref = bf16[1,512,512]{2,1,0:T(8,128)(2,1)} collective-permute-done((bf16[1,512,512]{2,1,0:T(8,128)(2,1)}, bf16[1,512,512]{2,1,0:T(8,128)(2,1)}, u32[]{:S(2)}, u32[]{:S(2)}) %collective-permute-start.28) | collective-permute-done | bytes 524320 | tf_op jit(solution)/shard_map/ppermute | solution.py:686
  251.8 7.6 %factor_products.3 = (bf16[2,592,512]{2,1,0:T(8,128)(2,1)}, bf16[2,592,512]{2,1,0:T(8,128)(2,1)}) custom-call(s32[8]{0:T(128)} %concatenate.85.numbers_ref, bf16[512,2048]{1,0:T(8,128)(2,1)} %get-tuple-element.51.refs_4_.refs_0_, bf16[128,4096]{1,0:T(8,128)(2,1)} %broadcast_add_fusion.refs_1_.refs_8_, bf16[128,4096]{1,0:T(8,128)(2,1)} %copy-done.1, ...), custom_call_target="tpu_custom_call" | custom-call | bytes 13200000 | tf_op jit(solution)/shard_map/factor_products/pallas_call | solution.py:553
  281.0 25.5 %collective-permute-done.27.got_ref = bf16[2,592,512]{2,1,0:T(8,128)(2,1)S(1)} collective-permute-done((bf16[2,592,512]{2,1,0:T(8,128)(2,1)}, bf16[2,592,512]{2,1,0:T(8,128)(2,1)S(1)}, u32[]{:S(2)}, u32[]{:S(2)}) %collective-permute-start.27) | collective-permute-done | bytes 1212448 | tf_op jit(solution)/shard_map/ppermute | solution.py:686
  315.2 26.8 %collective-permute-done.31.refs_0_.refs_2_.refs_3_ = bf16[1024,512]{1,0:T(8,128)(2,1)S(1)} collective-permute-done((bf16[1024,512]{1,0:T(8,128)(2,1)}, bf16[1024,512]{1,0:T(8,128)(2,1)S(1)}, u32[]{:S(2)}, u32[]{:S(2)}) %collective-permute-start.31) | collective-permute-done | bytes 1048608 | tf_op jit(solution)/shard_map/ppermute | solution.py:686
  351.0 21.9 %collective-permute-done.36.refs_1_ = bf16[624,512]{1,0:T(8,128)(2,1)} collective-permute-done((bf16[624,512]{1,0:T(8,128)(2,1)S(1)}, bf16[624,512]{1,0:T(8,128)(2,1)}, u32[]{:S(2)}, u32[]{:S(2)}) %collective-permute-start.36) | collective-permute-done | bytes 639008 | tf_op jit(solution)/shard_map/ppermute | solution.py:686
  381.4 9.3 %collective-permute-done.22 = bf16[1,1,128,2048]{3,2,1,0:T(8,128)(2,1)} collective-permute-done((bf16[1,1,128,2048]{3,2,1,0:T(8,128)(2,1)}, bf16[1,1,128,2048]{3,2,1,0:T(8,128)(2,1)}, u32[]{:S(2)}, u32[]{:S(2)}) %collective-permute-start.22) | collective-permute-done | bytes 524320 | tf_op jit(solution)/shard_map/ppermute | solution.py:686
  395.9 8.8 %collective-permute-done.38.refs_3_ = bf16[624,512]{1,0:T(8,128)(2,1)} collective-permute-done((bf16[624,512]{1,0:T(8,128)(2,1)}, bf16[624,512]{1,0:T(8,128)(2,1)}, u32[]{:S(2)}, u32[]{:S(2)}) %collective-permute-start.38) | collective-permute-done | bytes 639008 | tf_op jit(solution)/shard_map/ppermute | solution.py:686
  410.0 6.4 %join.3.refs_8_ = f32[2,2048,1024]{2,1,0:T(8,128)} custom-call(s32[2,8]{1,0:T(2,128)S(1)} %get-tuple-element.114.places_ref, bf16[512,512]{1,0:T(8,128)(2,1)S(1)} %bitcast.134, bf16[512,512]{1,0:T(8,128)(2,1)S(1)} %copy-done.15, bf16[1024,512]{1,0:T(8,128)(2,1)S(1)} %collective-permute-done.31.refs_0_.refs_2_.refs_3_, ...), custom_call_target="tpu_custom_call" | custom-call | bytes 15840000 | tf_op jit(solution)/shard_map/join/pallas_call | solution.py:865
  416.4 6.8 %join.5 = f32[1024,2048]{1,0:T(8,128)} custom-call(s32[2,8]{1,0:T(2,128)S(1)} %get-tuple-element.113.places_ref, bf16[512,512]{1,0:T(8,128)(2,1)} %bitcast.67.refs_0_, bf16[512,512]{1,0:T(8,128)(2,1)S(1)} %collective-permute-done.33.refs_2_.refs_1_, bf16[1024,512]{1,0:T(8,128)(2,1)} %collective-permute-done.44.refs_2_.refs_3_, ...), custom_call_target="tpu_custom_call" | custom-call | bytes 15840000 | tf_op jit(solution)/shard_map/join/pallas_call | solution.py:865
  423.2 6.7 %collective-permute-done.39.refs_4_ = bf16[624,512]{1,0:T(8,128)(2,1)S(1)} collective-permute-done((bf16[624,512]{1,0:T(8,128)(2,1)S(1)}, bf16[624,512]{1,0:T(8,128)(2,1)S(1)}, u32[]{:S(2)}, u32[]{:S(2)}) %collective-permute-start.39) | collective-permute-done | bytes 639008 | tf_op jit(solution)/shard_map/ppermute | solution.py:686
  429.9 13.7 %collective-permute-done.40.refs_5_ = bf16[624,512]{1,0:T(8,128)(2,1)S(1)} collective-permute-done((bf16[624,512]{1,0:T(8,128)(2,1)}, bf16[624,512]{1,0:T(8,128)(2,1)S(1)}, u32[]{:S(2)}, u32[]{:S(2)}) %collective-permute-start.40) | collective-permute-done | bytes 639008 | tf_op jit(solution)/shard_map/ppermute | solution.py:686
  443.6 13.7 %collective-permute-done.41.refs_6_ = bf16[624,512]{1,0:T(8,128)(2,1)S(1)} collective-permute-done((bf16[624,512]{1,0:T(8,128)(2,1)}, bf16[624,512]{1,0:T(8,128)(2,1)S(1)}, u32[]{:S(2)}, u32[]{:S(2)}) %collective-permute-start.41) | collective-permute-done | bytes 639008 | tf_op jit(solution)/shard_map/ppermute | solution.py:686
  457.3 10.3 %collective-permute-done.42.refs_7_ = bf16[624,512]{1,0:T(8,128)(2,1)S(1)} collective-permute-done((bf16[624,512]{1,0:T(8,128)(2,1)}, bf16[624,512]{1,0:T(8,128)(2,1)S(1)}, u32[]{:S(2)}, u32[]{:S(2)}) %collective-permute-start.42) | collective-permute-done | bytes 639008 | tf_op jit(solution)/shard_map/ppermute | solution.py:686
  467.6 6.7 %join.4 = (f32[2,2048,1024]{2,1,0:T(8,128)}, f32[448,1024]{1,0:T(8,128)S(1)}) custom-call(s32[2,8]{1,0:T(2,128)S(1)} %get-tuple-element.114.places_ref, bf16[624,512]{1,0:T(8,128)(2,1)S(1)} %pad_maximum_fusion.3.refs_0_, bf16[624,512]{1,0:T(8,128)(2,1)} %collective-permute-done.36.refs_1_, ...), custom_call_target="tpu_custom_call", output_to_operand_aliasing={{0}: (9, {})} | custom-call | bytes 15840000 | tf_op jit(solution)/shard_map/join/pallas_call | solution.py:865
  (300 shorter events, 154.0 us)
Async XLA Ops:
  58.7 53.8 %collective-permute-start.11 = (bf16[128,4096]{1,0:T(8,128)(2,1)}, bf16[128,4096]{1,0:T(8,128)(2,1)}, u32[]{:S(2)}, u32[]{:S(2)}) collective-permute-start(bf16[128,4096]{1,0:T(8,128)(2,1)} %broadcast_add_fusion.refs_1_.refs_8_), channel_id=1, source_target_pairs={{0,1},{1,0},{2,3},{3,2},{4,5},{5,4},{6,7},{7,6},{8,9},{9,8},{10,11... | collective-permute-start | bytes 3145736 | tf_op jit(solution)/shard_map/ppermute | solution.py:686
  153.0 37.1 %collective-permute-start.19 = (bf16[2,512,512]{2,1,0:T(8,128)(2,1)}, bf16[2,512,512]{2,1,0:T(8,128)(2,1)}, u32[]{:S(2)}, u32[]{:S(2)}) collective-permute-start(bf16[2,512,512]{2,1,0:T(8,128)(2,1)} %get-tuple-element.67.refs_15_), channel_id=1, source_target_pairs={{0,8},{4,12},{8,0},{12,4},{16,24},{20,28},{24,16},{28,20},{1,9},{5... | collective-permute-start | bytes 3145736 | tf_op jit(solution)/shard_map/ppermute | solution.py:686
  156.2 37.7 %collective-permute-start.20 = (bf16[1,512,512]{2,1,0:T(8,128)(2,1)}, bf16[1,512,512]{2,1,0:T(8,128)(2,1)S(1)}, u32[]{:S(2)}, u32[]{:S(2)}) collective-permute-start(bf16[1,512,512]{2,1,0:T(8,128)(2,1)} %copy-done.29), channel_id=1, source_target_pairs={{0,16},{4,20},{8,24},{12,28},{16,0},{20,4},{24,8},{28,12},{1,17},{... | collective-permute-start | bytes 1572872 | tf_op jit(solution)/shard_map/ppermute | solution.py:686
  208.8 53.4 %collective-permute-start.23 = (bf16[1,2,128,2048]{3,2,1,0:T(8,128)(2,1)}, bf16[1,2,128,2048]{3,2,1,0:T(8,128)(2,1)}, u32[]{:S(2)}, u32[]{:S(2)}) collective-permute-start(bf16[1,2,128,2048]{3,2,1,0:T(8,128)(2,1)} %fusion.9), channel_id=1, source_target_pairs={{0,1},{1,0},{2,3},{3,2},{4,5},{5,4},{6,7},{7,6},{8,9},{9,8},{10,11... | collective-permute-start | bytes 3145736 | tf_op jit(solution)/shard_map/ppermute | solution.py:686
  209.8 38.5 %collective-permute-start.28 = (bf16[1,512,512]{2,1,0:T(8,128)(2,1)}, bf16[1,512,512]{2,1,0:T(8,128)(2,1)}, u32[]{:S(2)}, u32[]{:S(2)}) collective-permute-start(bf16[1,512,512]{2,1,0:T(8,128)(2,1)} %get-tuple-element.77.refs_0_), channel_id=1, source_target_pairs={{0,16},{4,20},{8,24},{12,28},{16,0},{20,4},{24,8},{28,12},{1,17},{... | collective-permute-start | bytes 1572872 | tf_op jit(solution)/shard_map/ppermute | solution.py:686
  215.6 35.3 %collective-permute-start.26 = (bf16[320,512]{1,0:T(8,128)(2,1)S(1)}, bf16[320,512]{1,0:T(8,128)(2,1)S(1)}, u32[]{:S(2)}, u32[]{:S(2)}) collective-permute-start(bf16[320,512]{1,0:T(8,128)(2,1)S(1)} %constant_dynamic-slice_fusion), channel_id=1, source_target_pairs={{0,4},{4,0},{8,12},{12,8},{16,20},{20,16},{24,28},{28,24},{1,5},{5... | collective-permute-start | bytes 983048 | tf_op jit(solution)/shard_map/ppermute | solution.py:686
  218.2 33.6 %collective-permute-start.25 = (bf16[512,512]{1,0:T(8,128)(2,1)}, bf16[512,512]{1,0:T(8,128)(2,1)}, u32[]{:S(2)}, u32[]{:S(2)}) collective-permute-start(bf16[512,512]{1,0:T(8,128)(2,1)} %get-tuple-element.97), channel_id=1, source_target_pairs={{0,4},{4,0},{8,12},{12,8},{16,20},{20,16},{24,28},{28,24},{1,5},{5... | collective-permute-start | bytes 1572872 | tf_op jit(solution)/shard_map/ppermute | solution.py:686
  218.8 52.0 %collective-permute-start.29 = (bf16[512,512]{1,0:T(8,128)(2,1)S(1)}, bf16[512,512]{1,0:T(8,128)(2,1)S(1)}, u32[]{:S(2)}, u32[]{:S(2)}) collective-permute-start(bf16[512,512]{1,0:T(8,128)(2,1)S(1)} %bitcast.132), channel_id=1, source_target_pairs={{0,16},{4,20},{8,24},{12,28},{16,0},{20,4},{24,8},{28,12},{1,17},{... | collective-permute-start | bytes 1572872 | tf_op jit(solution)/shard_map/ppermute | solution.py:686
  250.3 60.0 %collective-permute-start.33 = (bf16[512,512]{1,0:T(8,128)(2,1)}, bf16[512,512]{1,0:T(8,128)(2,1)S(1)}, u32[]{:S(2)}, u32[]{:S(2)}) collective-permute-start(bf16[512,512]{1,0:T(8,128)(2,1)} %bitcast.67.refs_0_), channel_id=1, source_target_pairs={{0,16},{4,20},{8,24},{12,28},{16,0},{20,4},{24,8},{28,12},{1,17},{... | collective-permute-start | bytes 1572872 | tf_op jit(solution)/shard_map/ppermute | solution.py:686
  259.4 47.1 %collective-permute-start.27 = (bf16[2,592,512]{2,1,0:T(8,128)(2,1)}, bf16[2,592,512]{2,1,0:T(8,128)(2,1)S(1)}, u32[]{:S(2)}, u32[]{:S(2)}) collective-permute-start(bf16[2,592,512]{2,1,0:T(8,128)(2,1)} %get-tuple-element.81), channel_id=1, source_target_pairs={{0,8},{4,12},{8,0},{12,4},{16,24},{20,28},{24,16},{28,20},{1,9},{5... | collective-permute-start | bytes 3637256 | tf_op jit(solution)/shard_map/ppermute | solution.py:686
  271.9 70.1 %collective-permute-start.31 = (bf16[1024,512]{1,0:T(8,128)(2,1)}, bf16[1024,512]{1,0:T(8,128)(2,1)S(1)}, u32[]{:S(2)}, u32[]{:S(2)}) collective-permute-start(bf16[1024,512]{1,0:T(8,128)(2,1)} %pad_maximum_fusion.1), channel_id=1, source_target_pairs={{0,8},{4,12},{8,0},{12,4},{16,24},{20,28},{24,16},{28,20},{1,9},{5... | collective-permute-start | bytes 3145736 | tf_op jit(solution)/shard_map/ppermute | solution.py:686
  271.9 70.1 %collective-permute-start.32 = (bf16[1024,512]{1,0:T(8,128)(2,1)}, bf16[1024,512]{1,0:T(8,128)(2,1)S(1)}, u32[]{:S(2)}, u32[]{:S(2)}) collective-permute-start(bf16[1024,512]{1,0:T(8,128)(2,1)} %pad_maximum_fusion.1), channel_id=1, source_target_pairs={{0,4},{4,0},{8,12},{12,8},{16,20},{20,16},{24,28},{28,24},{1,5},{5... | collective-permute-start | bytes 3145736 | tf_op jit(solution)/shard_map/ppermute | solution.py:686
  306.5 40.5 %collective-permute-start.21 = (bf16[1,2,128,2048]{3,2,1,0:T(8,128)(2,1)}, bf16[1,2,128,2048]{3,2,1,0:T(8,128)(2,1)}, u32[]{:S(2)}, u32[]{:S(2)}) collective-permute-start(bf16[1,2,128,2048]{3,2,1,0:T(8,128)(2,1)} %fusion.10), channel_id=1, source_target_pairs={{0,1},{1,0},{2,3},{3,2},{4,5},{5,4},{6,7},{7,6},{8,9},{9,8},{10,11... | collective-permute-start | bytes 3145736 | tf_op jit(solution)/shard_map/ppermute | solution.py:686
  308.8 33.2 %collective-permute-start.30 = (bf16[1,592,512]{2,1,0:T(8,128)(2,1)}, bf16[1,592,512]{2,1,0:T(8,128)(2,1)}, u32[]{:S(2)}, u32[]{:S(2)}) collective-permute-start(bf16[1,592,512]{2,1,0:T(8,128)(2,1)} %get-tuple-element.84), channel_id=1, source_target_pairs={{0,16},{4,20},{8,24},{12,28},{16,0},{20,4},{24,8},{28,12},{1,17},{... | collective-permute-start | bytes 1818632 | tf_op jit(solution)/shard_map/ppermute | solution.py:686
  312.7 65.5 %collective-permute-start.44 = (bf16[1024,512]{1,0:T(8,128)(2,1)}, bf16[1024,512]{1,0:T(8,128)(2,1)}, u32[]{:S(2)}, u32[]{:S(2)}) collective-permute-start(bf16[1024,512]{1,0:T(8,128)(2,1)} %pad_maximum_fusion.2), channel_id=1, source_target_pairs={{0,8},{4,12},{8,0},{12,4},{16,24},{20,28},{24,16},{28,20},{1,9},{5... | collective-permute-start | bytes 3145736 | tf_op jit(solution)/shard_map/ppermute | solution.py:686
  345.0 34.9 %collective-permute-start.45 = (bf16[1024,512]{1,0:T(8,128)(2,1)}, bf16[1024,512]{1,0:T(8,128)(2,1)}, u32[]{:S(2)}, u32[]{:S(2)}) collective-permute-start(bf16[1024,512]{1,0:T(8,128)(2,1)} %pad_maximum_fusion.2), channel_id=1, source_target_pairs={{0,4},{4,0},{8,12},{12,8},{16,20},{20,16},{24,28},{28,24},{1,5},{5... | collective-permute-start | bytes 3145736 | tf_op jit(solution)/shard_map/ppermute | solution.py:686
  346.5 47.4 %collective-permute-start.43 = (bf16[1024,512]{1,0:T(8,128)(2,1)S(1)}, bf16[1024,512]{1,0:T(8,128)(2,1)}, u32[]{:S(2)}, u32[]{:S(2)}) collective-permute-start(bf16[1024,512]{1,0:T(8,128)(2,1)S(1)} %collective-permute-done.31.refs_0_.refs_2_.refs_3_), channel_id=1, source_target_pairs={{0,4},{4,0},{8,12},{12,8},{16,20},{20,16},{24,28},{28,24},{1,5},{5... | collective-permute-start | bytes 3145736 | tf_op jit(solution)/shard_map/ppermute | solution.py:686
  348.5 46.8 %collective-permute-start.37 = (bf16[624,512]{1,0:T(8,128)(2,1)S(1)}, bf16[624,512]{1,0:T(8,128)(2,1)}, u32[]{:S(2)}, u32[]{:S(2)}) collective-permute-start(bf16[624,512]{1,0:T(8,128)(2,1)S(1)} %pad_maximum_fusion.3.refs_0_), channel_id=1, source_target_pairs={{0,8},{4,12},{8,0},{12,4},{16,24},{20,28},{24,16},{28,20},{1,9},{5... | collective-permute-start | bytes 1916936 | tf_op jit(solution)/shard_map/ppermute | solution.py:686
  372.9 31.8 %collective-permute-start.38 = (bf16[624,512]{1,0:T(8,128)(2,1)}, bf16[624,512]{1,0:T(8,128)(2,1)}, u32[]{:S(2)}, u32[]{:S(2)}) collective-permute-start(bf16[624,512]{1,0:T(8,128)(2,1)} %collective-permute-done.36.refs_1_), channel_id=1, source_target_pairs={{0,8},{4,12},{8,0},{12,4},{16,24},{20,28},{24,16},{28,20},{1,9},{5... | collective-permute-start | bytes 1916936 | tf_op jit(solution)/shard_map/ppermute | solution.py:686
  379.8 36.5 %collective-permute-start.46 = (bf16[1024,512]{1,0:T(8,128)(2,1)}, bf16[1024,512]{1,0:T(8,128)(2,1)S(1)}, u32[]{:S(2)}, u32[]{:S(2)}) collective-permute-start(bf16[1024,512]{1,0:T(8,128)(2,1)} %collective-permute-done.44.refs_2_.refs_3_), channel_id=1, source_target_pairs={{0,4},{4,0},{8,12},{12,8},{16,20},{20,16},{24,28},{28,24},{1,5},{5... | collective-permute-start | bytes 3145736 | tf_op jit(solution)/shard_map/ppermute | solution.py:686
  390.7 39.2 %collective-permute-start.39 = (bf16[624,512]{1,0:T(8,128)(2,1)S(1)}, bf16[624,512]{1,0:T(8,128)(2,1)S(1)}, u32[]{:S(2)}, u32[]{:S(2)}) collective-permute-start(bf16[624,512]{1,0:T(8,128)(2,1)S(1)} %pad_maximum_fusion.3.refs_0_), channel_id=1, source_target_pairs={{0,4},{4,0},{8,12},{12,8},{16,20},{20,16},{24,28},{28,24},{1,5},{5... | collective-permute-start | bytes 1916936 | tf_op jit(solution)/shard_map/ppermute | solution.py:686
  393.9 49.8 %collective-permute-start.40 = (bf16[624,512]{1,0:T(8,128)(2,1)}, bf16[624,512]{1,0:T(8,128)(2,1)S(1)}, u32[]{:S(2)}, u32[]{:S(2)}) collective-permute-start(bf16[624,512]{1,0:T(8,128)(2,1)} %collective-permute-done.36.refs_1_), channel_id=1, source_target_pairs={{0,4},{4,0},{8,12},{12,8},{16,20},{20,16},{24,28},{28,24},{1,5},{5... | collective-permute-start | bytes 1916936 | tf_op jit(solution)/shard_map/ppermute | solution.py:686
  395.4 61.9 %collective-permute-start.41 = (bf16[624,512]{1,0:T(8,128)(2,1)}, bf16[624,512]{1,0:T(8,128)(2,1)S(1)}, u32[]{:S(2)}, u32[]{:S(2)}) collective-permute-start(bf16[624,512]{1,0:T(8,128)(2,1)} %collective-permute-done.37.refs_2_), channel_id=1, source_target_pairs={{0,4},{4,0},{8,12},{12,8},{16,20},{20,16},{24,28},{28,24},{1,5},{5... | collective-permute-start | bytes 1916936 | tf_op jit(solution)/shard_map/ppermute | solution.py:686
  404.7 62.9 %collective-permute-start.42 = (bf16[624,512]{1,0:T(8,128)(2,1)}, bf16[624,512]{1,0:T(8,128)(2,1)S(1)}, u32[]{:S(2)}, u32[]{:S(2)}) collective-permute-start(bf16[624,512]{1,0:T(8,128)(2,1)} %collective-permute-done.38.refs_3_), channel_id=1, source_target_pairs={{0,4},{4,0},{8,12},{12,8},{16,20},{20,16},{24,28},{28,24},{1,5},{5... | collective-permute-start | bytes 1916936 | tf_op jit(solution)/shard_map/ppermute | solution.py:686
  (85 other events, 1043.3 us)

commit v3 on v2

--- a/solution.py
+++ b/solution.py
@@ -31,7 +31,7 @@
 
 
 def estimate(micros):
-    return pl.CostEstimate(flops=0, bytes_accessed=int(micros * 3.3e6), transcendentals=0)
+    return pl.CostEstimate(flops=1, bytes_accessed=1, transcendentals=0)
 
 
 TOKENS = (((0,), (0,)), ((), ()))
@@ -464,7 +464,7 @@
     )(agrad, proj_grad, w_x_rows, inner, allows, conv_w, conv_b.reshape(1, -1), *after)
 
 
-def factor_products(jobs, others, masks, depth, extra=None, after=()):
+def factor_products(jobs, others, masks, depth, stacked, extra=None, after=()):
     rank = lax.axis_index("mp")
     count = len(masks)
     length = jobs[0][0].shape[0]
@@ -472,41 +472,35 @@
     part = depth // LINE
     channels = jobs[0][2][0].shape[1]
     factors_first = [job[3] for job in jobs]
-    sizes = [(channels, part) if first else (part, channels) for first in factors_first]
-    more = 0 if extra is None else extra.shape[1]
-    own = line_place() % 2
-    order = jnp.stack([1 - own, 3 - own, own, 2 + own])
-    places = jnp.stack([(rank ^ mask) * rows for mask in masks])
-    numbers = jnp.concatenate([order, places]).astype(jnp.int32)
+    places = jnp.stack([(rank ^ mask) * rows for mask in masks]).astype(jnp.int32)
     in_specs = []
-    operands = [numbers]
+    operands = [places]
     for rows_of, half, factors, _ in jobs:
-        in_specs.append(pl.BlockSpec((length, part), lambda b, numbers_ref: (0, numbers_ref[b])))
+        in_specs.append(pl.BlockSpec((length, part), lambda b, _: (0, b)))
         operands.append(rows_of)
         for other in others:
             for mask in masks:
                 in_specs.append(
                     pl.BlockSpec(
                         (rows, part),
-                        lambda b, numbers_ref, half=half: (0, half * LINE + numbers_ref[b]),
+                        lambda b, _, half=half: (0, half * LINE + b),
                     )
                 )
                 operands.append(other[mask])
         for factor in factors:
             in_specs.append(fixed(factor.shape))
             operands.append(factor)
+    more = 0 if extra is None else extra.shape[1]
     if more:
-        in_specs.append(
-            pl.BlockSpec((1, more, channels), lambda b, numbers_ref: (numbers_ref[b], 0, 0))
-        )
+        in_specs.append(pl.BlockSpec((1, more, channels), lambda b, _: (b, 0, 0)))
         operands.append(extra)
     in_specs += [anywhere()] * len(after)
     operands += list(after)
 
-    def kernel(numbers_ref, *refs):
+    def kernel(places_ref, *refs):
         scratch = refs[-1]
         outs = refs[len(operands) - 1 : -1]
-        step = pl.program_id(0)
+
         at = 0
         for turn, first in enumerate(factors_first):
             source = refs[at]
@@ -517,7 +511,7 @@
             for g in range(len(others) + 1):
                 if g:
                     for piece, ref in enumerate(groups[g - 1]):
-                        place = pl.multiple_of(numbers_ref[LINE + piece], rows)
+                        place = pl.multiple_of(places_ref[piece], rows)
                         scratch[pl.ds(place, rows), :] = ref[...]
                     value = scratch[...]
                 else:
@@ -527,89 +521,58 @@
                 term = product(*pair, TOKENS)
                 total = term if total is None else total + term
             at += len(others) + 1
-            total = total.astype(jnp.bfloat16)
-            height = sizes[turn][0]
-
-            @pl.when(step < LINE // 2)
-            def _():
-                outs[2 * turn][0, :height, :] = total
-
-            @pl.when(step >= LINE // 2)
-            def _():
-                outs[2 * turn + 1][0, :height, :] = total
-
-        if more:
-
-            @pl.when(step < LINE // 2)
-            def _():
-                outs[0][0, sizes[0][0] :, :] = refs[at][0]
-
-            @pl.when(step >= LINE // 2)
-            def _():
-                outs[1][0, sizes[0][0] :, :] = refs[at][0]
-
-    early = lambda b, numbers_ref: (jnp.minimum(b, LINE // 2 - 1), 0, 0)
-    late = lambda b, numbers_ref: (jnp.maximum(b - LINE // 2, 0), 0, 0)
+            if stacked:
+                outs[0][0, turn] = total.astype(jnp.bfloat16)
+            elif more:
+                outs[0][0, :part, :] = total.astype(jnp.bfloat16)
+                outs[0][0, part:, :] = refs[at][0]
+            else:
+                outs[turn][...] = total.astype(jnp.bfloat16)
+
+    if stacked:
+        out_specs = [pl.BlockSpec((1, len(jobs), part, part), lambda b, _: (b, 0, 0, 0))]
+        out_shape = [jax.ShapeDtypeStruct((LINE, len(jobs), part, part), jnp.bfloat16)]
+    elif more:
+        out_specs = [pl.BlockSpec((1, part + more, channels), lambda b, _: (b, 0, 0))]
+        out_shape = [jax.ShapeDtypeStruct((LINE, part + more, channels), jnp.bfloat16)]
+    else:
+        out_specs = [
+            pl.BlockSpec((channels, part), lambda b, _: (0, b))
+            if first
+            else pl.BlockSpec((part, channels), lambda b, _: (b, 0))
+            for first in factors_first
+        ]
+        out_shape = [
+            jax.ShapeDtypeStruct(
+                (channels, depth) if first else (depth, channels), jnp.bfloat16
+            )
+            for first in factors_first
+        ]
     return pl.pallas_call(
         kernel,
         grid_spec=pltpu.PrefetchScalarGridSpec(
             num_scalar_prefetch=1,
             grid=(LINE,),
             in_specs=in_specs,
-            out_specs=[
-                pl.BlockSpec((1, height + more, width), index)
-                for height, width in sizes
-                for index in (early, late)
-            ],
+            out_specs=out_specs,
             scratch_shapes=[pltpu.VMEM((length, part), jnp.bfloat16)],
         ),
-        out_shape=[
-            jax.ShapeDtypeStruct((LINE // 2, height + more, width), jnp.bfloat16)
-            for height, width in sizes
-            for _ in range(2)
-        ],
+        out_shape=out_shape,
         compiler_params=pltpu.CompilerParams(vmem_limit_bytes=56 << 20),
-        cost_estimate=estimate(4 * len(jobs)),
+        cost_estimate=estimate(5 * len(jobs)),
         name="factor_products",
     )(*operands)
 
 
-def add_blocks(kept, got, bit, after):
-    count, rows, width = kept.shape
-    own = (line_place() // bit) % 2
-    order = jnp.stack([1 - own, own]) if count == 2 else jnp.zeros((1,), jnp.int32)
-
-    def kernel(order_ref, kept_ref, got_ref, *refs):
-        total = kept_ref[...].astype(jnp.float32) + got_ref[...].astype(jnp.float32)
-        total = total.astype(jnp.bfloat16)
-        if count == 1:
-            refs[-1][...] = total
-            return
-        step = pl.program_id(0)
-
-        @pl.when(step == 0)
-        def _():
-            refs[-2][...] = total
-
-        @pl.when(step == 1)
-        def _():
-            refs[-1][...] = total
-
-    block = pl.BlockSpec((1, rows, width), lambda b, order_ref: (order_ref[b], 0, 0))
-    result = pl.BlockSpec((1, rows, width), lambda b, order_ref: (0, 0, 0))
-    return pl.pallas_call(
-        kernel,
-        grid_spec=pltpu.PrefetchScalarGridSpec(
-            num_scalar_prefetch=1,
-            grid=(count,),
-            in_specs=[block, block] + [anywhere()] * len(after),
-            out_specs=[result] * count,
-        ),
-        out_shape=[jax.ShapeDtypeStruct((1, rows, width), jnp.bfloat16)] * count,
-        compiler_params=pltpu.CompilerParams(vmem_limit_bytes=40 << 20),
-        cost_estimate=estimate(1),
-        name="add_blocks",
-    )(order.astype(jnp.int32), kept, got, *after)
+def touch(values, after):
+    return pl.pallas_call(
+        lambda *refs: None,
+        in_specs=[anywhere()] * (1 + len(after)),
+        out_specs=anywhere(),
+        out_shape=jax.ShapeDtypeStruct(values.shape, values.dtype),
+        input_output_aliases={0: 0},
+        name="touch",
+    )(values, *after)
 
 
 def project_back(pre, w_dt, key_grad, query_grad, keys, fade, after):
@@ -639,34 +602,83 @@
     )(pre, w_dt, key_grad, query_grad, keys, fade, *after)
 
 
-def narrow_products(low_rank, pre, proj_grad, acts, after):
+def narrow_products(low_rank, pre, proj_grad, acts, conv_sums, sums):
     length, channels = pre.shape
     tile = min(256, channels)
     rank_width, width = low_rank.shape[1], proj_grad.shape[1]
-    padding = -(rank_width + width) % (16 * LINE)
-    total = rank_width + width + padding
-
-    def kernel(low_ref, pre_ref, pg_ref, acts_ref, *refs):
-        out_ref = refs[-1]
+    used = rank_width + width
+    total = used + 32
+
+    def kernel(low_ref, pre_ref, pg_ref, acts_ref, conv_ref, sums_ref, out_ref):
         first = product(low_ref[...], pre_ref[...].astype(jnp.bfloat16), TOKENS)
         out_ref[:rank_width, :] = first.astype(jnp.bfloat16)
         second = product(pg_ref[...], acts_ref[...].astype(jnp.bfloat16), TOKENS)
-        out_ref[rank_width : rank_width + width, :] = second.astype(jnp.bfloat16)
-        if padding:
-            out_ref[rank_width + width :, :] = jnp.zeros((padding, tile), jnp.bfloat16)
-
-    column = pl.BlockSpec((length, tile), lambda c: (0, c))
+        out_ref[rank_width:used, :] = second.astype(jnp.bfloat16)
+        rows = jnp.concatenate(
+            [conv_ref[...], sums_ref[...], jnp.zeros((22, tile), jnp.float32)], 0
+        )
+        out_ref[used:, :] = rows.astype(jnp.bfloat16)
+
+    column = lambda height: pl.BlockSpec((height, tile), lambda c: (0, c))
     return pl.pallas_call(
         kernel,
         grid=(channels // tile,),
-        in_specs=[fixed(low_rank.shape), column, fixed(proj_grad.shape), column]
-        + [anywhere()] * len(after),
-        out_specs=pl.BlockSpec((total, tile), lambda c: (0, c)),
+        in_specs=[
+            fixed(low_rank.shape),
+            column(length),
+            fixed(proj_grad.shape),
+            column(length),
+            column(8),
+            column(2),
+        ],
+        out_specs=column(total),
         out_shape=jax.ShapeDtypeStruct((total, channels), jnp.bfloat16),
         compiler_params=pltpu.CompilerParams(vmem_limit_bytes=48 << 20),
         cost_estimate=estimate(4),
         name="narrow_products",
-    )(low_rank, pre, proj_grad, acts, *after)
+    )(low_rank, pre, proj_grad, acts, conv_sums, sums)
+
+
+def project_normed(inner_grad, gate_grad, w_in, after):
+    length, channels = inner_grad.shape
+    depth = w_in.shape[1]
+    tile = min(512, depth)
+    height = min(512, length)
+
+    def kernel(inner_ref, gate_ref, w_ref, *refs):
+        refs[-1][...] = product(inner_ref[...], w_ref[0], ACROSS) + product(
+            gate_ref[...], w_ref[1], ACROSS
+        )
+
+    rows = pl.BlockSpec((height, channels), lambda c, r: (r, 0))
+    return pl.pallas_call(
+        kernel,
+        grid=(depth // tile, length // height),
+        in_specs=[rows, rows, pl.BlockSpec((2, tile, channels), lambda c, r: (0, c, 0))]
+        + [anywhere()] * len(after),
+        out_specs=pl.BlockSpec((height, tile), lambda c, r: (r, c)),
+        out_shape=jax.ShapeDtypeStruct((length, depth), jnp.float32),
+        compiler_params=pltpu.CompilerParams(vmem_limit_bytes=48 << 20),
+        cost_estimate=estimate(6),
+        name="project_normed",
+    )(inner_grad, gate_grad, w_in, *after)
+
+
+def put_rows(values, rows, at):
+    height, width = rows.shape
+
+    def kernel(rows_ref, values_ref, out_ref):
+        out_ref[0] = rows_ref[...]
+
+    return pl.pallas_call(
+        kernel,
+        grid=(1,),
+        in_specs=[whole((height, width)), anywhere()],
+        out_specs=pl.BlockSpec((1, height, width), lambda c: (0, at // height, 0)),
+        out_shape=jax.ShapeDtypeStruct(values.shape, values.dtype),
+        input_output_aliases={1: 0},
+        name="put_rows",
+    )(rows, values)
 
 
 def to_tiles(values):
@@ -754,129 +766,83 @@
     return parts
 
 
-def line_place():
-    return lax.axis_index("dp") // (lax.axis_size("dp") // LINE)
-
-
-def near_step(give, keep, after):
+def line_groups():
     side = lax.axis_size("dp") // LINE
-    return add_blocks(keep, swap(give, "dp", side), 2, after)
-
-
-def far_step(give, keep, after):
+    return [[z * side + x for z in range(LINE)] for x in range(side)]
+
+
+def scatter_line(values):
+    return lax.psum_scatter(
+        values, "dp", scatter_dimension=0, tiled=True, axis_index_groups=line_groups()
+    )
+
+
+def gather_line(values):
+    return lax.all_gather(values, "dp", axis=0, tiled=True, axis_index_groups=line_groups())
+
+
+def side_pieces(values):
+    pieces = {0: values}
+    for bit in bits_down(lax.axis_size("dp") // LINE):
+        for mask in list(pieces):
+            pieces[mask | bit] = swap(pieces[mask], "dp", bit)
+    return pieces
+
+
+def join_blocks(pieces, tall, place, shape, buffer=None):
     side = lax.axis_size("dp") // LINE
-    return add_blocks(keep, swap(give, "dp", 2 * side), 2, after)[0][0]
-
-
-def spread(piece, apart=False):
-    rows = piece.shape[0]
-    held = [(piece, [0])]
-    for bit in bits_down(lax.axis_size("dp")):
-        if apart:
-            parts = [[one] for one in held]
-        elif len(held) > 1:
-            parts = [held[:-1], held[-1:]] if bit == 1 else [held]
-        else:
-            parts = [held]
-        for part in parts:
-            masks = [mask for _, group in part for mask in group]
-            arrays = [array for array, _ in part]
-            sent = arrays[0] if len(arrays) == 1 else jnp.concatenate(arrays, 0)
-            held.append((swap(sent, "dp", bit), [mask | bit for mask in masks]))
-    table = {mask: (array, which) for array, masks in held for which, mask in enumerate(masks)}
-    return table, [array for array, _ in held[1:]]
-
-
-def join(pieces, rows, height, lines_first, target=None, buffer=None):
-    side = lax.axis_size("dp") // LINE
-    rank = lax.axis_index("dp")
+    rank = lax.axis_index("dp") % side
     masks = list(pieces)
     count = len(masks)
-    width = pieces[masks[0]][0].shape[1]
-    more = rows - height
-    origin = jnp.stack([rank ^ mask for mask in masks])
-    line, flank = origin // side, origin % side
-    down, right = (line, flank) if lines_first else (flank, line)
-    grid_down, grid_right = (LINE, side) if lines_first else (side, LINE)
-    shape = (height * grid_down, width * grid_right)
-    low_shape = (more * grid_down, width * grid_right)
+    width = pieces[masks[0]].shape[2]
+    flank = jnp.stack([rank ^ mask for mask in masks]).astype(jnp.int32)
+    block = (1,) * (len(shape) - 2) + (tall, width)
     if width % 128:
-        total = jnp.zeros(shape, jnp.float32)
-        low = jnp.zeros(low_shape, jnp.float32)
+        total = jnp.zeros(shape, jnp.float32) if buffer is None else buffer
         for step, mask in enumerate(masks):
-            array, which = pieces[mask]
-            value = array[which * rows : (which + 1) * rows].astype(jnp.float32)
-            right_at = right[step] * width
-            total = lax.dynamic_update_slice(total, value[:height], (down[step] * height, right_at))
-            if more:
-                low = lax.dynamic_update_slice(low, value[height:], (down[step] * more, right_at))
-        if target is not None:
-            if buffer is None:
-                buffer = jnp.zeros((2,) + shape, jnp.float32)
-            total = lax.dynamic_update_slice(buffer, total[None], (target, 0, 0))
-        return (total, low) if more else total
-    places = jnp.stack([down, right]).astype(jnp.int32)
-
-    def kernel(places_ref, *refs):
-        outs = refs[-2:] if more else refs[-1:]
+            for number in range(LINE):
+                value = pieces[mask][number, :tall].astype(jnp.float32).reshape(block)
+                at = tuple(i * n for i, n in zip(place(number, flank[step]), block))
+                total = lax.dynamic_update_slice(total, value, at)
+        return total
+
+    def kernel(flank_ref, *refs):
         step = pl.program_id(0)
         for turn in range(count):
 
             @pl.when(step == turn)
             def _():
-                value = refs[turn][:height, :].astype(jnp.float32)
-                outs[0][...] = value if target is None else value[None]
-                if more:
-                    outs[1][...] = refs[turn][height:, :].astype(jnp.float32)
-
-    in_specs = [
-        pl.BlockSpec((rows, width), lambda step, places_ref, which=pieces[mask][1]: (which, 0))
-        for mask in masks
-    ]
-    operands = [places] + [pieces[mask][0] for mask in masks]
+                refs[-1][...] = refs[turn][...].astype(jnp.float32).reshape(block)
+
+    def source(turn):
+        def index(step, cut, flank_ref):
+            return (jnp.where(step < turn, 0, jnp.where(step == turn, cut, LINE - 1)), 0, 0)
+
+        return pl.BlockSpec((1, tall, width), index)
+
+    in_specs = [source(turn) for turn in range(count)]
+    operands = [flank] + [pieces[mask] for mask in masks]
     aliases = {}
-    if target is None:
-        out_shapes = [jax.ShapeDtypeStruct(shape, jnp.float32)]
-        out_specs = [
-            pl.BlockSpec(
-                (height, width),
-                lambda step, places_ref: (places_ref[0, step], places_ref[1, step]),
-            )
-        ]
-    else:
-        out_shapes = [jax.ShapeDtypeStruct((2,) + shape, jnp.float32)]
-        out_specs = [
-            pl.BlockSpec(
-                (1, height, width),
-                lambda step, places_ref: (target, places_ref[0, step], places_ref[1, step]),
-            )
-        ]
-        if buffer is not None:
-            in_specs.append(pl.BlockSpec(memory_space=pl.ANY))
-            operands.append(buffer)
-            aliases = {len(operands) - 1: 0}
-    if more:
-        out_shapes.append(jax.ShapeDtypeStruct(low_shape, jnp.float32))
-        out_specs.append(
-            pl.BlockSpec(
-                (more, width), lambda step, places_ref: (places_ref[0, step], places_ref[1, step])
-            )
-        )
-    results = pl.pallas_call(
+    if buffer is not None:
+        in_specs.append(anywhere())
+        operands.append(buffer)
+        aliases = {len(operands) - 1: 0}
+    return pl.pallas_call(
         kernel,
         grid_spec=pltpu.PrefetchScalarGridSpec(
             num_scalar_prefetch=1,
-            grid=(count,),
+            grid=(count, LINE),
             in_specs=in_specs,
-            out_specs=out_specs,
+            out_specs=pl.BlockSpec(
+                block, lambda step, cut, flank_ref: place(cut, flank_ref[step])
+            ),
         ),
-        out_shape=out_shapes,
+        out_shape=jax.ShapeDtypeStruct(shape, jnp.float32),
         input_output_aliases=aliases,
         compiler_params=pltpu.CompilerParams(vmem_limit_bytes=40 << 20),
-        cost_estimate=estimate(count * 0.6),
-        name="join",
+        cost_estimate=estimate(count * 2),
+        name="join_blocks",
     )(*operands)
-    return results if more else results[0]
 
 
 def tie(values, other):
@@ -931,7 +897,8 @@
     proj = sum_mp(proj_part, gate_silu)
     others = []
     for rows in beside:
-        others.append(gather_pieces(tie(rows, proj), "mp"))
+        rows = tie(rows, proj)
+        others.append({mask: swap(rows, "mp", mask) if mask else rows for mask in masks})
     low_rank = proj[:, :R].astype(jnp.bfloat16)
     keys = proj[:, R : R + state_size]
     queries = proj[:, R + state_size :]
@@ -965,52 +932,47 @@
         state_size,
     )
     chunks = length // CHUNK
-    fetched = [rows[masks[1]] for rows in others]
-    later = scan_backward(*back_args, (chunks // 2, chunks), None, [gated, gate_grad] + fetched)
+    cut = chunks * 5 // 8
+    later = scan_backward(*back_args, (cut, chunks), None, [gated, gate_grad])
     gate_job = (group_normed, 0, trade_side(gate_grad), False)
     out_job = (group_ograd, 1, trade_side(gated), True)
-    gate_give, gate_keep, out_give, out_keep = factor_products(
-        [gate_job, out_job], others, masks, depth, None, (later[6],)
-    )
+    stacked = channels // side == depth // LINE
+    parts = factor_products(
+        [gate_job, out_job], others, masks, depth, stacked, None, (later[6],)
+    )
+    scattered = [scatter_line(value) for value in parts]
     pre_tiles, agrad_tiles, key_grad, query_grad, fade, sums, _ = scan_backward(
-        *back_args, (0, chunks // 2), later, (gate_give, out_give)
+        *back_args, (0, cut), later, parts
     )
     pre_full = from_tiles(pre_tiles)
-    gate_give, gate_keep = near_step(gate_give, gate_keep, (fade,))
-    proj_back = project_back(pre_full, w_dt, key_grad, query_grad, keys, fade, (gate_give,))
-    out_give, out_keep = near_step(out_give, out_keep, (proj_back,))
+    proj_back = project_back(pre_full, w_dt, key_grad, query_grad, keys, fade, ())
     proj_grad = sum_mp(proj_back).astype(jnp.bfloat16)
-    gate_piece = far_step(gate_give, gate_keep, ())
-    gate_pieces, gate_came = spread(gate_piece)
     inner_grad, conv_sums = finish_inner(
-        from_tiles(agrad_tiles),
-        proj_grad,
-        w_x_rows,
-        inner,
-        allows,
-        conv_w,
-        conv_b,
-        (out_give, gate_piece),
+        from_tiles(agrad_tiles), proj_grad, w_x_rows, inner, allows, conv_w, conv_b, ()
     )
     inner_parts = trade_side(inner_grad)
-    out_piece = far_step(out_give, out_keep, (inner_grad,))
-    out_pieces, out_came = spread(out_piece)
-    narrow = narrow_products(low_rank, pre_full, proj_grad, acts, (inner_grad,))
+    narrow = narrow_products(
+        low_rank, pre_full, proj_grad, acts, conv_sums, sums.reshape(2, channels)
+    )
     branch_out = scatter_mp(product(tie(gated, inner_grad), w_out))
     block_out = (source_rows + branch_out).astype(jnp.bfloat16)
     extra = sum((part.astype(jnp.float32) for part in trade_side(narrow))).astype(jnp.bfloat16)
     width = channels // side
-    tall = narrow.shape[0] // LINE
-    extra = extra.reshape(LINE, tall, width)
+    extra = extra.reshape(LINE, extra.shape[0] // LINE, width)
+    gain_rows = -(-depth // (16 * width)) * 16
+    extra = jnp.concatenate([extra, jnp.zeros((LINE, gain_rows, width), jnp.bfloat16)], 1)
     inner_job = (group_normed, 0, inner_parts, False)
-    inner_give, inner_keep = factor_products([inner_job], others, masks, depth, extra)
-    w_in_grad = join(gate_pieces, depth // LINE, depth // LINE, True, 1)
-    w_out_grad = join(out_pieces, width, width, False)
-    inner_give, inner_keep = near_step(inner_give, inner_keep, (out_piece, gate_came[0]))
-    inner_piece = far_step(inner_give, inner_keep, gate_came[1:3] + out_came[:1])
-    normed_grad = scatter_mp(
-        product(inner_grad, w_in[0], ACROSS) + product(gate_grad, w_in[1], ACROSS)
-    )
+    (inner_part,) = factor_products([inner_job], others, masks, depth, False, extra)
+    scattered = [touch(value, (inner_part,)) for value in scattered]
+    if stacked:
+        gate_sum, out_sum = gather_line(scattered[0][:, 0]), gather_line(scattered[0][:, 1])
+    else:
+        gate_sum, out_sum = gather_line(scattered[0]), gather_line(scattered[1])
+        gate_sum = gate_sum.reshape(LINE, depth // LINE, width)
+        out_sum = out_sum.reshape(width, LINE, depth // LINE).transpose(1, 0, 2)
+    gate_pieces, out_pieces = side_pieces(gate_sum), side_pieces(out_sum)
+    normed_part = project_normed(inner_grad, gate_grad, w_in, (inner_part,))
+    normed_grad = scatter_mp(normed_part)
     scaled = normed_grad * norm_gain
     gain_part = jnp.sum(normed_grad * source_rows * inv_root, 0)
     cubed = inv_root * inv_root * inv_root
@@ -1020,29 +982,57 @@
     input_grad = (out_grad.astype(jnp.float32) + input_grad).astype(jnp.bfloat16)
     for bit in bits_down(size):
         gain_part = gain_part + swap(gain_part, "mp", bit)
-    partial = [conv_sums[:5].reshape(-1), sums.reshape(-1), gain_part]
-    partial = jnp.concatenate([value.astype(jnp.bfloat16) for value in partial])
-    used = partial.shape[0]
-    count = -(-used // (16 * width)) * 16
-    partial = jnp.concatenate([partial, jnp.zeros(count * width - used, jnp.bfloat16)])
-    tail = jnp.concatenate([inner_piece, partial.reshape(count, width)], 0)
-    pieces, _ = spread(tail, True)
-    w_in_grad, low = join(pieces, tail.shape[0], depth // LINE, True, 0, w_in_grad)
-    low = low.reshape(LINE, -1, channels)
-    narrow = low[:, :tall].reshape(LINE * tall, channels)
-    total = low[:, tall : tall + count].reshape(LINE, count, side, width)
-    total = jnp.sum(total, (0, 2)).reshape(-1)
+    part = depth // LINE
+    tall = part // 2
+    gain = jnp.zeros((gain_rows * width - depth,), jnp.float32)
+    gain = jnp.concatenate([gain_part, gain]).reshape(gain_rows, width).astype(jnp.bfloat16)
+    last = inner_part.shape[1] - gain_rows
+    if last % gain_rows:
+        inner_part = lax.dynamic_update_slice(inner_part, gain[None], (0, last, 0))
+    else:
+        inner_part = put_rows(inner_part, gain, last)
+    inner_piece = scatter_line(
+        touch(inner_part, [out_sum, block_out, input_grad] + list(gate_pieces.values()))
+    )
+    inner_piece = touch(inner_piece, tuple(out_pieces.values()))
+    second_sum = gather_line(inner_piece[:, tall:])
+    first_sum = gather_line(inner_piece[:, :tall])
+    first_pieces, second_pieces = side_pieces(first_sum), side_pieces(second_sum)
+
+    shape = (2, depth, channels)
+    places = [lambda b, f: (f, b), lambda b, f: (1, b, f)]
+    places += [lambda b, f: (0, 2 * b, f), lambda b, f: (0, 2 * b + 1, f)]
+    heights = [width, part, tall, tall]
+    own = [out_pieces, gate_pieces, first_pieces, second_pieces]
+    own, rest = [{0: v[0]} for v in own], [{m: v[m] for m in v if m} for v in own]
+
+    def assemble(which, pieces, buffer=None):
+        full = shape if which else (channels, depth)
+        return join_blocks(pieces[which], heights[which], places[which], full, buffer)
+
+    w_out_grad = assemble(0, rest, assemble(0, own))
+    w_in_grad = assemble(1, rest, assemble(1, own))
+    for which, pieces in ((3, own), (2, own), (3, rest), (2, rest)):
+        w_in_grad = assemble(which, pieces, w_in_grad)
+    flank = lax.axis_index("dp") % side
+    narrow = jnp.zeros((LINE * (last - part), channels), jnp.float32)
+    for mask, piece in second_pieces.items():
+        rows = piece[:, tall : last - tall].reshape(-1, width).astype(jnp.float32)
+        narrow = lax.dynamic_update_slice(narrow, rows, (0, (flank ^ mask) * width))
+    gains = [piece[0, last - tall :] for piece in second_pieces.values()]
+    gain = sum((value.astype(jnp.float32) for value in gains)).reshape(-1)[:depth]
+    split = R + R + 2 * state_size
     return (
         block_out,
         input_grad,
-        total[7 * channels : used],
+        gain,
         w_in_grad,
-        total[: 4 * channels].reshape(4, channels),
-        total[4 * channels : 5 * channels],
-        narrow[R : 2 * R + 2 * state_size].T,
+        narrow[split : split + 4],
+        narrow[split + 4],
+        narrow[R:split].T,
         narrow[:R],
-        total[5 * channels : 6 * channels],
-        total[6 * channels : 7 * channels],
+        narrow[split + 8],
+        narrow[split + 9],
         w_out_grad,
     )
 

time: 481 us -> 456 us (0.948)
  starting transfers between devices: 49.6 us -> 26 us
  waiting for transfers between devices: 221 us -> 200 us
  local copies, waits for them, and re-layouts: 30.1 us -> 49.6 us
  between operations: 5.49 us -> 18.7 us
  matrix products: 12.9 us -> 5.35 us
  Pallas kernels: 137 us -> 132 us
    ppermute x47 -> x30, waiting for transfers between devices: 221 us -> 115 us  [swap(): return lax.ppermute(values, axis, [(i, i ^ offset) for i in range(size)])]
    all_gather x0 -> x4, waiting for transfers between devices: none -> 84.1 us  [gather_line(): lax.all_gather(values, 'dp', axis=0, tiled=True, axis_index_groups=line_g...]
    ppermute x47 -> x30, starting transfers between devices: 49.6 us -> 25.6 us  [swap(): return lax.ppermute(values, axis, [(i, i ^ offset) for i in range(size)])]
    dot_general x4 -> x2, matrix products: 12.9 us -> 5.35 us  [product(): lax.dot_general(left, right, dims, preferred_element_type=jnp.float32)]
    unnamed x130 -> x118, local copies, waits for them, and re-layouts: 12.3 us -> 19.6 us
    slice x3 -> x9, local copies, waits for them, and re-layouts: 0.09 us -> 7.21 us  [the longest x1 2.39 us: on_device(): scattered[0][:, 0]]
    pallas_call x9 -> x13, Pallas kernels: 30.8 us -> 29.1 us  [the longest x8 18.9 us: join_blocks(): pl.pallas_call(kernel, grid_spec=pltpu.PrefetchScalarGridSpec(num_scalar_...]
  transfers between devices with their start and end apart: 47 -> 36, of which waited for: 21 -> 19; matrix products, arithmetic and copies ran while one was open for 9% -> 10% of each run, Pallas kernels for 23% -> 26%
where the time goes in v3:
time: 456 us; the launch traced here: 455 us
  waiting for transfers between devices  200 us (44%)
  Pallas kernels  132 us (29%)
  local copies, waits for them, and re-layouts  49.6 us (11%)
  starting transfers between devices  26 us (6%)
  other arithmetic  22.6 us (5%)
  between operations  18.7 us (4%)
  matrix products  5.35 us (1%)
    ppermute x30, waiting for transfers between devices, swap(): return lax.ppermute(values, axis, [(i, i ^ offset) for i in range(size)])  115 us
    all_gather x4, waiting for transfers between devices, gather_line(): lax.all_gather(values, 'dp', axis=0, tiled=True, axis_index_groups=line_g...  84.1 us
    pallas_call x2, Pallas kernels, scan_backward(): pl.pallas_call(kernel, grid=(span[1] - span[0],), in_specs=in_specs, out_...  38.8 us
    ppermute x30, starting transfers between devices, swap(): return lax.ppermute(values, axis, [(i, i ^ offset) for i in range(size)])  25.6 us
    unnamed x118, local copies, waits for them, and re-layouts  19.6 us
    pallas_call x8, Pallas kernels, join_blocks(): pl.pallas_call(kernel, grid_spec=pltpu.PrefetchScalarGridSpec(num_scalar_...  18.9 us
    pallas_call x2, Pallas kernels, factor_products(): pl.pallas_call(kernel, grid_spec=pltpu.PrefetchScalarGridSpec(num_scalar_...  17.6 us
    pallas_call x1, Pallas kernels, scan_forward(): pl.pallas_call(lambda *refs: forward_kernel(chunk, n, length, *refs[:3],...  16.7 us
  transfers between devices with their start and end apart: 36, of which 19 were waited for; matrix products, arithmetic and copies ran while one was open for 10% of the time, Pallas kernels for 26%

profile of v3, /device:TPU:0, one launch (start us, length us, event | category | flops | bytes accessed | tf_op | source)
XLA Modules:
  0.0 454.7 jit_solution(5021457427296893531)
XLA Ops:
  19.6 6.5 %collective-permute-done.refs_1_ = bf16[128,2048]{1,0:T(8,128)(2,1)} collective-permute-done((bf16[128,2048]{1,0:T(8,128)(2,1)S(1)}, bf16[128,2048]{1,0:T(8,128)(2,1)}, u32[]{:S(2)}, u32[]{:S(2)}) %collective-permute-start) | collective-permute-done | bytes 524320 | tf_op jit(solution)/shard_map/ppermute | solution.py:698
  32.2 9.1 %project_in.1 = (bf16[512,2048]{1,0:T(8,128)(2,1)}, f32[512,1024]{1,0:T(8,128)}, f32[512,1024]{1,0:T(8,128)}, f32[512,160]{1,0:T(8,128)}) custom-call(s32[4]{0:T(128)} %pad_add_fusion.places_ref, bf16[128,2048]{1,0:T(8,128)(2,1)} %copy-done.36, bf16[128,2048]{1,0:T(8,128)(2,1)} %collective-permute-done.refs_1_, ...), custom_call_target="tpu_custom_call" | custom-call | flops 1 | bytes 1 | tf_op jit(solution)/shard_map/project_in/pallas_call | solution.py:339
  47.5 11.6 %project_gate.1 = (bf16[512,2048]{1,0:T(8,128)(2,1)}, f32[512,1024]{1,0:T(8,128)}, f32[512,1024]{1,0:T(8,128)}, f32[512,1024]{1,0:T(8,128)}) custom-call(s32[4]{0:T(128)} %pad_add_fusion.places_ref, bf16[128,2048]{1,0:T(8,128)(2,1)} %copy-done.41, bf16[128,2048]{1,0:T(8,128)(2,1)} %copy-done.42, bf16[128,2048]{1,0:T(8,128)(2,1)} %copy-done.43, ...), custom_call_target="tpu_custom_call" | custom-call | flops 1 | bytes 1 | tf_op jit(solution)/shard_map/project_gate/pallas_call | solution.py:395
  69.7 16.7 %scan_forward.1 = (f32[64,64,128]{2,1,0:T(8,128)S(1)}, f32[512,16,8,128]{3,2,1,0:T(8,128)}) custom-call(f32[16960]{0:T(1024)S(1)} %pad_maximum_fusion.1.refs_0_, f32[64,64,128]{2,1,0:T(8,128)S(1)} %divide_bitcast_fusion.refs_1_, f32[64,64,128]{2,1,0:T(8,128)} %bitcast.104, f32[512,1024]{1,0:T(8,128)} %get-tuple-element.38.refs_3_, ...), custom_call_target="tpu_custom_call" | custom-call | flops 1 | bytes 1 | tf_op jit(solution)/shard_map/scan_forward/pallas_call | solution.py:110
  91.5 15.2 %scan_backward.2 = (f32[64,64,128]{2,1,0:T(8,128)S(1)}, f32[64,64,128]{2,1,0:T(8,128)}, f32[512,16]{1,0:T(8,128)S(1)}, f32[512,16]{1,0:T(8,128)S(1)}, f32[512,12...) custom-call(f32[16960]{0:T(1024)S(1)} %pad_maximum_fusion.1.refs_0_, f32[64,64,128]{2,1,0:T(8,128)} %copy-done.3, ...), custom_call_target="tpu_custom_call" | custom-call | flops 1 | bytes 1 | tf_op jit(solution)/shard_map/scan_backward/pallas_call | solution.py:268
  109.5 4.2 collective-permute-done.14.refs_13_
  114.5 10.2 %factor_products.2.refs_14_ = bf16[4,2,512,512]{3,2,1,0:T(8,128)(2,1)} custom-call(s32[4]{0:T(128)} %pad_add_fusion.places_ref, bf16[512,2048]{1,0:T(8,128)(2,1)} %get-tuple-element.37.refs_4_.refs_0_, bf16[128,4096]{1,0:T(8,128)(2,1)} %broadcast_add_fusion.refs_1_.refs_8_, bf16[128,4096]{1,0:T(8,128)(2,1)} %collective-permute-done.10.refs_2_.refs_9_, ...), custom_call_target="tpu_custom_call" | custom-call | flops 1 | bytes 1 | tf_op jit(solution)/shard_map/factor_products/pallas_call | solution.py:551
  130.0 23.6 %scan_backward.3 = (f32[64,64,128]{2,1,0:T(8,128)S(1)}, f32[64,64,128]{2,1,0:T(8,128)S(1)}, f32[512,16]{1,0:T(8,128)S(1)}, f32[512,16]{1,0:T(8,128)S(1)}, f32[51...) custom-call(f32[16960]{0:T(1024)S(1)} %pad_maximum_fusion.1.refs_0_,, ...), custom_call_target="tpu_custom_call", output_to_operand_aliasing={{0}: (9, {}), {1}: (10, {}), {2}: (11, {}), {3}: (12, {}), ... | custom-call | flops 1 | bytes 1 | tf_op jit(solution)/shard_map/scan_backward/pallas_call | solution.py:268
  158.0 6.9 %collective-permute-done.16 = f32[256,160]{1,0:T(8,128)S(1)} collective-permute-done((f32[256,160]{1,0:T(8,128)S(1)}, f32[256,160]{1,0:T(8,128)S(1)}, u32[]{:S(2)}, u32[]{:S(2)}) %collective-permute-start.16) | collective-permute-done | bytes 163872 | tf_op jit(solution)/shard_map/ppermute | solution.py:698
  167.4 7.0 %finish_inner.1 = (bf16[512,1024]{1,0:T(8,128)(2,1)}, f32[8,1024]{1,0:T(8,128)}) custom-call(f32[512,1024]{1,0:T(8,128)} %bitcast.113, bf16[512,160]{1,0:T(8,128)(2,1)} %convert_element_type.156.pg_ref, bf16[160,1024]{1,0:T(8,128)(2,1)} %bitcast.126, f32[512,1024]{1,0:T(8,128)} %get-tuple-element.57.inner_ref, f32[512,3]{1,0:T(8,128)} %copy.47.refs_5_.allow_ref, ...), custom_call_target="tpu_custom_call" | custom-call | flops 1 | bytes 1 | tf_op jit(solution)/shard_map/finish_inner/pallas_call | solution.py:443
  179.8 7.6 %collective-permute-done.21 = bf16[320,512]{1,0:T(8,128)(2,1)S(1)} collective-permute-done((bf16[320,512]{1,0:T(8,128)(2,1)S(1)}, bf16[320,512]{1,0:T(8,128)(2,1)S(1)}, u32[]{:S(2)}, u32[]{:S(2)}) %collective-permute-start.21) | collective-permute-done | bytes 327712 | tf_op jit(solution)/shard_map/ppermute | solution.py:698
  188.3 9.6 %collective-permute-done.20.refs_6_ = bf16[512,512]{1,0:T(8,128)(2,1)S(1)} collective-permute-done((bf16[512,512]{1,0:T(8,128)(2,1)S(1)}, bf16[512,512]{1,0:T(8,128)(2,1)S(1)}, u32[]{:S(2)}, u32[]{:S(2)}) %collective-permute-start.20) | collective-permute-done | bytes 524320 | tf_op jit(solution)/shard_map/ppermute | solution.py:698
  198.6 7.3 %factor_products.3.refs_0_.values_ref.refs_1_ = bf16[4,608,512]{2,1,0:T(8,128)(2,1)} custom-call(s32[4]{0:T(128)} %pad_add_fusion.places_ref, bf16[512,2048]{1,0:T(8,128)(2,1)} %get-tuple-element.37.refs_4_.refs_0_, bf16[128,4096]{1,0:T(8,128)(2,1)} %broadcast_add_fusion.refs_1_.refs_8_, bf16[128,4096]{1,0:T(8,128)(2,1)} %collective-permute-done.10.refs_2_.refs_9_, ...), custom_call_target="tpu_custom_call" | custom-call | flops 1 | bytes 1 | tf_op jit(solution)/shard_map/factor_products/pallas_call | solution.py:551
  211.5 8.9 %project_normed.1 = f32[512,2048]{1,0:T(8,128)} custom-call(bf16[512,1024]{1,0:T(8,128)(2,1)S(1)} %copy-done.14, bf16[512,1024]{1,0:T(8,128)(2,1)S(1)} %get-tuple-element.67.refs_8_.gate_ref, bf16[2,2048,1024]{2,1,0:T(8,128)(2,1)} %w_ref.3, bf16[4,608,512]{2,1,0:T(8,128)(2,1)S(1)} %copy-done), custom_call_target="tpu_custom_call" | custom-call | flops 1 | bytes 1 | tf_op jit(solution)/shard_map/project_normed/pallas_call | solution.py:654
  222.3 4.4 fusion.13
  233.3 22.6 %all-gather.13.cloned.1.call-done = bf16[4,1,512,512]{3,2,1,0:T(8,128)(2,1)} async-done(((bf16[1,1,512,512]{3,2,1,0:T(8,128)(2,1)}), bf16[4,1,512,512]{3,2,1,0:T(8,128)(2,1)}) %all-gather.13.cloned.1.call-update) | async-done | bytes 2097168 | tf_op jit(solution)/shard_map/all_gather | solution.py:781
  265.9 8.8 %collective-permute-done.23 = bf16[1,1,128,2048]{3,2,1,0:T(8,128)(2,1)} collective-permute-done((bf16[1,1,128,2048]{3,2,1,0:T(8,128)(2,1)}, bf16[1,1,128,2048]{3,2,1,0:T(8,128)(2,1)}, u32[]{:S(2)}, u32[]{:S(2)}) %collective-permute-start.23) | collective-permute-done | bytes 524320 | tf_op jit(solution)/shard_map/ppermute | solution.py:698
  278.0 6.6 %collective-permute-done.24 = f32[2048]{0:T(1024)S(1)} collective-permute-done((f32[2048]{0:T(1024)S(1)}, f32[2048]{0:T(1024)S(1)}, u32[]{:S(2)}, u32[]{:S(2)}) %collective-permute-start.24) | collective-permute-done | bytes 8224 | tf_op jit(solution)/shard_map/ppermute | solution.py:698
  289.7 13.2 %all-gather.11.cloned.1.call-done = bf16[4,1,512,512]{3,2,1,0:T(8,128)(2,1)} async-done(((bf16[1,1,512,512]{3,2,1,0:T(8,128)(2,1)}), bf16[4,1,512,512]{3,2,1,0:T(8,128)(2,1)}) %all-gather.11.cloned.1.call-update) | async-done | bytes 2097168 | tf_op jit(solution)/shard_map/all_gather | solution.py:781
  308.0 45.3 %collective-permute-done.27.refs_2_.refs_0_ = bf16[4,512,512]{2,1,0:T(8,128)(2,1)} collective-permute-done((bf16[4,512,512]{2,1,0:T(8,128)(2,1)S(1)}, bf16[4,512,512]{2,1,0:T(8,128)(2,1)}, u32[]{:S(2)}, u32[]{:S(2)}) %collective-permute-start.27) | collective-permute-done | bytes 2097184 | tf_op jit(solution)/shard_map/ppermute | solution.py:698
  357.7 33.0 %all-gather.7.cloned.1.call-done.refs_0_ = bf16[4,352,512]{2,1,0:T(8,128)(2,1)} async-done(((bf16[1,352,512]{2,1,0:T(8,128)(2,1)}), bf16[4,352,512]{2,1,0:T(8,128)(2,1)}) %all-gather.7.cloned.1.call-update) | async-done | bytes 1441808 | tf_op jit(solution)/shard_map/all_gather | solution.py:781
  397.5 4.4 join_blocks.15
  404.3 15.3 %all-gather.9.cloned.1.call-done.refs_0_ = bf16[4,256,512]{2,1,0:T(8,128)(2,1)} async-done(((bf16[1,256,512]{2,1,0:T(8,128)(2,1)}), bf16[4,256,512]{2,1,0:T(8,128)(2,1)}) %all-gather.9.cloned.1.call-update) | async-done | bytes 1048592 | tf_op jit(solution)/shard_map/all_gather | solution.py:781
  431.5 14.5 %collective-permute-done.29.refs_0_ = bf16[4,256,512]{2,1,0:T(8,128)(2,1)S(1)} collective-permute-done((bf16[4,256,512]{2,1,0:T(8,128)(2,1)}, bf16[4,256,512]{2,1,0:T(8,128)(2,1)S(1)}, u32[]{:S(2)}, u32[]{:S(2)}) %collective-permute-start.29) | collective-permute-done | bytes 1048608 | tf_op jit(solution)/shard_map/ppermute | solution.py:698
  (270 shorter events, 123.4 us)
Async XLA Ops:
  7.2 198.8 %reduce-scatter.3.cloned.1.call-start = ((), (), s32[]{:S(2)}) async-start(), calls=%async_computation.2 | async-start | bytes 5242880 | tf_op jit(solution)/shard_map/reduce_scatter | solution.py:775
  11.0 15.1 %collective-permute-start = (bf16[128,2048]{1,0:T(8,128)(2,1)S(1)}, bf16[128,2048]{1,0:T(8,128)(2,1)}, u32[]{:S(2)}, u32[]{:S(2)}) collective-permute-start(bf16[128,2048]{1,0:T(8,128)(2,1)S(1)} %fusion.4.refs_0_), channel_id=1, source_target_pairs={{0,2},{1,3},{2,0},{3,1},{4,6},{5,7},{6,4},{7,5},{8,10},{9,11},{10,... | collective-permute-start | bytes 1572872 | tf_op jit(solution)/shard_map/ppermute | solution.py:698
  14.1 18.1 %collective-permute-start.1 = (bf16[128,2048]{1,0:T(8,128)(2,1)S(1)}, bf16[128,2048]{1,0:T(8,128)(2,1)}, u32[]{:S(2)}, u32[]{:S(2)}) collective-permute-start(bf16[128,2048]{1,0:T(8,128)(2,1)S(1)} %fusion.4.refs_0_), channel_id=1, source_target_pairs={{0,1},{1,0},{2,3},{3,2},{4,5},{5,4},{6,7},{7,6},{8,9},{9,8},{10,11... | collective-permute-start | bytes 1572872 | tf_op jit(solution)/shard_map/ppermute | solution.py:698
  16.1 30.1 %collective-permute-start.8 = (bf16[128,4096]{1,0:T(8,128)(2,1)}, bf16[128,4096]{1,0:T(8,128)(2,1)S(1)}, u32[]{:S(2)}, u32[]{:S(2)}) collective-permute-start(bf16[128,4096]{1,0:T(8,128)(2,1)} %pad_maximum_fusion), channel_id=1, source_target_pairs={{0,4},{4,0},{8,12},{12,8},{16,20},{20,16},{24,28},{28,24},{1,5},{5... | collective-permute-start | bytes 3145736 | tf_op jit(solution)/shard_map/ppermute | solution.py:698
  28.1 14.8 %collective-permute-start.5 = (bf16[128,2048]{1,0:T(8,128)(2,1)S(1)}, bf16[128,2048]{1,0:T(8,128)(2,1)S(1)}, u32[]{:S(2)}, u32[]{:S(2)}) collective-permute-start(bf16[128,2048]{1,0:T(8,128)(2,1)S(1)} %broadcast_add_fusion.1.refs_0_), channel_id=1, source_target_pairs={{0,2},{1,3},{2,0},{3,1},{4,6},{5,7},{6,4},{7,5},{8,10},{9,11},{10,... | collective-permute-start | bytes 1572872 | tf_op jit(solution)/shard_map/ppermute | solution.py:698
  45.1 16.0 %collective-permute-start.4 = (f32[256,160]{1,0:T(8,128)S(1)}, f32[256,160]{1,0:T(8,128)}, u32[]{:S(2)}, u32[]{:S(2)}) collective-permute-start(f32[256,160]{1,0:T(8,128)S(1)} %dynamic-slice_add_fusion.1), channel_id=1, source_target_pairs={{0,2},{1,3},{2,0},{3,1},{4,6},{5,7},{6,4},{7,5},{8,10},{9,11},{10,... | collective-permute-start | bytes 491528 | tf_op jit(solution)/shard_map/ppermute | solution.py:698
  66.2 47.5 %collective-permute-start.10 = (bf16[128,4096]{1,0:T(8,128)(2,1)}, bf16[128,4096]{1,0:T(8,128)(2,1)}, u32[]{:S(2)}, u32[]{:S(2)}) collective-permute-start(bf16[128,4096]{1,0:T(8,128)(2,1)} %broadcast_add_fusion.refs_1_.refs_8_), channel_id=1, source_target_pairs={{0,2},{1,3},{2,0},{3,1},{4,6},{5,7},{6,4},{7,5},{8,10},{9,11},{10,... | collective-permute-start | bytes 3145736 | tf_op jit(solution)/shard_map/ppermute | solution.py:698
  67.9 45.8 %collective-permute-start.11 = (bf16[128,4096]{1,0:T(8,128)(2,1)}, bf16[128,4096]{1,0:T(8,128)(2,1)}, u32[]{:S(2)}, u32[]{:S(2)}) collective-permute-start(bf16[128,4096]{1,0:T(8,128)(2,1)} %broadcast_add_fusion.refs_1_.refs_8_), channel_id=1, source_target_pairs={{0,1},{1,0},{2,3},{3,2},{4,5},{5,4},{6,7},{7,6},{8,9},{9,8},{10,11... | collective-permute-start | bytes 3145736 | tf_op jit(solution)/shard_map/ppermute | solution.py:698
  67.9 45.8 %collective-permute-start.12 = (bf16[128,4096]{1,0:T(8,128)(2,1)}, bf16[128,4096]{1,0:T(8,128)(2,1)}, u32[]{:S(2)}, u32[]{:S(2)}) collective-permute-start(bf16[128,4096]{1,0:T(8,128)(2,1)} %broadcast_add_fusion.refs_1_.refs_8_), channel_id=1, source_target_pairs={{0,3},{1,2},{2,1},{3,0},{4,7},{5,6},{6,5},{7,4},{8,11},{9,10},{10,... | collective-permute-start | bytes 3145736 | tf_op jit(solution)/shard_map/ppermute | solution.py:698
  88.6 20.9 %collective-permute-start.13 = (bf16[512,512]{1,0:T(8,128)(2,1)S(1)}, bf16[512,512]{1,0:T(8,128)(2,1)S(1)}, u32[]{:S(2)}, u32[]{:S(2)}) collective-permute-start(bf16[512,512]{1,0:T(8,128)(2,1)S(1)} %get-tuple-element.78), channel_id=1, source_target_pairs={{0,4},{4,0},{8,12},{12,8},{16,20},{20,16},{24,28},{28,24},{1,5},{5... | collective-permute-start | bytes 1572872 | tf_op jit(solution)/shard_map/ppermute | solution.py:698
  91.1 22.6 %collective-permute-start.14 = (bf16[512,512]{1,0:T(8,128)(2,1)S(1)}, bf16[512,512]{1,0:T(8,128)(2,1)S(1)}, u32[]{:S(2)}, u32[]{:S(2)}) collective-permute-start(bf16[512,512]{1,0:T(8,128)(2,1)S(1)} %get-tuple-element.76), channel_id=1, source_target_pairs={{0,4},{4,0},{8,12},{12,8},{16,20},{20,16},{24,28},{28,24},{1,5},{5... | collective-permute-start | bytes 1572872 | tf_op jit(solution)/shard_map/ppermute | solution.py:698
  124.8 131.1 %all-gather.13.cloned.1.call-start = ((), (), s32[]{:S(2)}) async-start(), calls=%async_computation.7 | async-start | bytes 2621440 | tf_op jit(solution)/shard_map/all_gather | solution.py:781
  179.1 18.7 %collective-permute-start.20 = (bf16[512,512]{1,0:T(8,128)(2,1)S(1)}, bf16[512,512]{1,0:T(8,128)(2,1)S(1)}, u32[]{:S(2)}, u32[]{:S(2)}) collective-permute-start(bf16[512,512]{1,0:T(8,128)(2,1)S(1)} %get-tuple-element.74), channel_id=1, source_target_pairs={{0,4},{4,0},{8,12},{12,8},{16,20},{20,16},{24,28},{28,24},{1,5},{5... | collective-permute-start | bytes 1572872 | tf_op jit(solution)/shard_map/ppermute | solution.py:698
  208.4 94.5 %all-gather.11.cloned.1.call-start = ((), (), s32[]{:S(2)}) async-start(), calls=%async_computation.6 | async-start | bytes 2621440 | tf_op jit(solution)/shard_map/all_gather | solution.py:781
  226.7 127.4 %reduce-scatter.5.cloned.1.call-start = ((), (), s32[]{:S(2)}) async-start(), calls=%async_computation.3 | async-start | bytes 3112960 | tf_op jit(solution)/shard_map/reduce_scatter | solution.py:775
  229.5 31.5 %collective-permute-start.18 = (bf16[1,2,128,2048]{3,2,1,0:T(8,128)(2,1)}, bf16[1,2,128,2048]{3,2,1,0:T(8,128)(2,1)}, u32[]{:S(2)}, u32[]{:S(2)}) collective-permute-start(bf16[1,2,128,2048]{3,2,1,0:T(8,128)(2,1)} %fusion), channel_id=1, source_target_pairs={{0,1},{1,0},{2,3},{3,2},{4,5},{5,4},{6,7},{7,6},{8,9},{9,8},{10,11... | collective-permute-start | bytes 3145736 | tf_op jit(solution)/shard_map/ppermute | solution.py:698
  255.9 47.6 %collective-permute-start.26 = (bf16[4,512,512]{2,1,0:T(8,128)(2,1)}, bf16[4,512,512]{2,1,0:T(8,128)(2,1)S(1)}, u32[]{:S(2)}, u32[]{:S(2)}) collective-permute-start(bf16[4,512,512]{2,1,0:T(8,128)(2,1)} %bitcast.114), channel_id=1, source_target_pairs={{0,4},{4,0},{8,12},{12,8},{16,20},{20,16},{24,28},{28,24},{1,5},{5... | collective-permute-start | bytes 6291464 | tf_op jit(solution)/shard_map/ppermute | solution.py:698
  259.5 15.2 %collective-permute-start.23 = (bf16[1,1,128,2048]{3,2,1,0:T(8,128)(2,1)}, bf16[1,1,128,2048]{3,2,1,0:T(8,128)(2,1)}, u32[]{:S(2)}, u32[]{:S(2)}) collective-permute-start(bf16[1,1,128,2048]{3,2,1,0:T(8,128)(2,1)} %dynamic-slice_convert_fusion), channel_id=1, source_target_pairs={{0,2},{1,3},{2,0},{3,1},{4,6},{5,7},{6,4},{7,5},{8,10},{9,11},{10,... | collective-permute-start | bytes 1572872 | tf_op jit(solution)/shard_map/ppermute | solution.py:698
  265.3 19.2 %collective-permute-start.19 = (bf16[1,1,128,2048]{3,2,1,0:T(8,128)(2,1)}, bf16[1,1,128,2048]{3,2,1,0:T(8,128)(2,1)}, u32[]{:S(2)}, u32[]{:S(2)}) collective-permute-start(bf16[1,1,128,2048]{3,2,1,0:T(8,128)(2,1)} %dynamic-slice_convert_fusion.1), channel_id=1, source_target_pairs={{0,2},{1,3},{2,0},{3,1},{4,6},{5,7},{6,4},{7,5},{8,10},{9,11},{10,... | collective-permute-start | bytes 1572872 | tf_op jit(solution)/shard_map/ppermute | solution.py:698
  304.9 85.8 %all-gather.7.cloned.1.call-start = ((), (), s32[]{:S(2)}) async-start(), calls=%async_computation.4 | async-start | bytes 1802240 | tf_op jit(solution)/shard_map/all_gather | solution.py:781
  306.5 46.8 %collective-permute-start.27 = (bf16[4,512,512]{2,1,0:T(8,128)(2,1)S(1)}, bf16[4,512,512]{2,1,0:T(8,128)(2,1)}, u32[]{:S(2)}, u32[]{:S(2)}) collective-permute-start(bf16[4,512,512]{2,1,0:T(8,128)(2,1)S(1)} %bitcast.111), channel_id=1, source_target_pairs={{0,4},{4,0},{8,12},{12,8},{16,20},{20,16},{24,28},{28,24},{1,5},{5... | collective-permute-start | bytes 6291464 | tf_op jit(solution)/shard_map/ppermute | solution.py:698
  356.0 63.6 %all-gather.9.cloned.1.call-start = ((), (), s32[]{:S(2)}) async-start(), calls=%async_computation.5 | async-start | bytes 1310720 | tf_op jit(solution)/shard_map/all_gather | solution.py:781
  390.7 35.3 %collective-permute-start.28 = (bf16[4,352,512]{2,1,0:T(8,128)(2,1)}, bf16[4,352,512]{2,1,0:T(8,128)(2,1)S(1)}, u32[]{:S(2)}, u32[]{:S(2)}) collective-permute-start(bf16[4,352,512]{2,1,0:T(8,128)(2,1)} %all-gather.7.cloned.1.call-done.refs_0_), channel_id=1, source_target_pairs={{0,4},{4,0},{8,12},{12,8},{16,20},{20,16},{24,28},{28,24},{1,5},{5... | collective-permute-start | bytes 4325384 | tf_op jit(solution)/shard_map/ppermute | solution.py:698
  419.6 26.4 %collective-permute-start.29 = (bf16[4,256,512]{2,1,0:T(8,128)(2,1)}, bf16[4,256,512]{2,1,0:T(8,128)(2,1)S(1)}, u32[]{:S(2)}, u32[]{:S(2)}) collective-permute-start(bf16[4,256,512]{2,1,0:T(8,128)(2,1)} %all-gather.9.cloned.1.call-done.refs_0_), channel_id=1, source_target_pairs={{0,4},{4,0},{8,12},{12,8},{16,20},{20,16},{24,28},{28,24},{1,5},{5... | collective-permute-start | bytes 3145736 | tf_op jit(solution)/shard_map/ppermute | solution.py:698
  (70 other events, 523.5 us)
Sparse Core Ops, SparseCore 0:
  124.9 78.0 reduce-scatter.2
  208.5 47.3 all-gather.12
  258.2 44.6 all-gather.10
  305.1 48.8 reduce-scatter.4
  356.1 34.5 all-gather.6
  392.8 26.7 all-gather.8

commit v4 on v3

--- a/solution.py
+++ b/solution.py
@@ -789,7 +789,7 @@
     return pieces
 
 
-def join_blocks(pieces, tall, place, shape, buffer=None):
+def join_blocks(pieces, tall, place, shape, buffer=None, cuts=LINE, pick=lambda number: number):
     side = lax.axis_size("dp") // LINE
     rank = lax.axis_index("dp") % side
     masks = list(pieces)
@@ -800,8 +800,8 @@
     if width % 128:
         total = jnp.zeros(shape, jnp.float32) if buffer is None else buffer
         for step, mask in enumerate(masks):
-            for number in range(LINE):
-                value = pieces[mask][number, :tall].astype(jnp.float32).reshape(block)
+            for number in range(cuts):
+                value = pieces[mask][pick(number), :tall].astype(jnp.float32).reshape(block)
                 at = tuple(i * n for i, n in zip(place(number, flank[step]), block))
                 total = lax.dynamic_update_slice(total, value, at)
         return total
@@ -816,7 +816,8 @@
 
     def source(turn):
         def index(step, cut, flank_ref):
-            return (jnp.where(step < turn, 0, jnp.where(step == turn, cut, LINE - 1)), 0, 0)
+            number = jnp.where(step < turn, 0, jnp.where(step == turn, cut, cuts - 1))
+            return (pick(number), 0, 0)
 
         return pl.BlockSpec((1, tall, width), index)
 
@@ -831,7 +832,7 @@
         kernel,
         grid_spec=pltpu.PrefetchScalarGridSpec(
             num_scalar_prefetch=1,
-            grid=(count, LINE),
+            grid=(count, cuts),
             in_specs=in_specs,
             out_specs=pl.BlockSpec(
                 block, lambda step, cut, flank_ref: place(cut, flank_ref[step])
@@ -963,14 +964,16 @@
     extra = jnp.concatenate([extra, jnp.zeros((LINE, gain_rows, width), jnp.bfloat16)], 1)
     inner_job = (group_normed, 0, inner_parts, False)
     (inner_part,) = factor_products([inner_job], others, masks, depth, False, extra)
-    scattered = [touch(value, (inner_part,)) for value in scattered]
+    sums_of = [gather_line(touch(value, (extra,))) for value in scattered]
     if stacked:
-        gate_sum, out_sum = gather_line(scattered[0][:, 0]), gather_line(scattered[0][:, 1])
+        blocks = sums_of[0].reshape(2 * LINE, width, width)
+        halves = [blocks[:LINE], blocks[LINE:]]
     else:
-        gate_sum, out_sum = gather_line(scattered[0]), gather_line(scattered[1])
-        gate_sum = gate_sum.reshape(LINE, depth // LINE, width)
-        out_sum = out_sum.reshape(width, LINE, depth // LINE).transpose(1, 0, 2)
-    gate_pieces, out_pieces = side_pieces(gate_sum), side_pieces(out_sum)
+        halves = [
+            sums_of[0].reshape(LINE, depth // LINE, width),
+            sums_of[1].reshape(width, LINE, depth // LINE).transpose(1, 0, 2),
+        ]
+    half_pieces = [side_pieces(value) for value in halves]
     normed_part = project_normed(inner_grad, gate_grad, w_in, (inner_part,))
     normed_grad = scatter_mp(normed_part)
     scaled = normed_grad * norm_gain
@@ -992,28 +995,41 @@
     else:
         inner_part = put_rows(inner_part, gain, last)
     inner_piece = scatter_line(
-        touch(inner_part, [out_sum, block_out, input_grad] + list(gate_pieces.values()))
-    )
-    inner_piece = touch(inner_piece, tuple(out_pieces.values()))
+        touch(inner_part, sums_of + [block_out, input_grad])
+    )
+    inner_piece = touch(inner_piece, tuple(half_pieces[0].values()))
     second_sum = gather_line(inner_piece[:, tall:])
     first_sum = gather_line(inner_piece[:, :tall])
-    first_pieces, second_pieces = side_pieces(first_sum), side_pieces(second_sum)
+    second_pieces = side_pieces(second_sum)
+    first_pieces = side_pieces(touch(first_sum, tuple(half_pieces[1].values())))
 
     shape = (2, depth, channels)
-    places = [lambda b, f: (f, b), lambda b, f: (1, b, f)]
-    places += [lambda b, f: (0, 2 * b, f), lambda b, f: (0, 2 * b + 1, f)]
-    heights = [width, part, tall, tall]
-    own = [out_pieces, gate_pieces, first_pieces, second_pieces]
-    own, rest = [{0: v[0]} for v in own], [{m: v[m] for m in v if m} for v in own]
-
-    def assemble(which, pieces, buffer=None):
-        full = shape if which else (channels, depth)
-        return join_blocks(pieces[which], heights[which], places[which], full, buffer)
-
-    w_out_grad = assemble(0, rest, assemble(0, own))
-    w_in_grad = assemble(1, rest, assemble(1, own))
-    for which, pieces in ((3, own), (2, own), (3, rest), (2, rest)):
-        w_in_grad = assemble(which, pieces, w_in_grad)
+    part_out = lambda start: lambda b, f: (f, b + start)
+    part_gate = lambda start: lambda b, f: (1, b + start, f)
+    others_of = lambda pieces: {mask: pieces[mask] for mask in pieces if mask}
+
+    def finished(place_of, height, full, job):
+        if not stacked:
+            pieces = half_pieces[1 - job]
+            buffer = join_blocks({0: pieces[0]}, height, place_of(0), full)
+            return join_blocks(others_of(pieces), height, place_of(0), full, buffer)
+        pick = lambda number: 2 * number + job
+        buffer = join_blocks({0: blocks}, height, place_of(0), full, None, LINE, pick)
+        for turn, pieces in enumerate(half_pieces):
+            start = turn * LINE // 2
+            buffer = join_blocks(
+                others_of(pieces), height, place_of(start), full, buffer, LINE // 2, pick
+            )
+        return buffer
+
+    w_out_grad = finished(part_out, width, (channels, depth), 1 if stacked else 0)
+    w_in_grad = finished(part_gate, part, shape, 0 if stacked else 1)
+    upper = lambda b, f: (0, 2 * b, f)
+    lower = lambda b, f: (0, 2 * b + 1, f)
+    w_in_grad = join_blocks({0: second_pieces[0]}, tall, lower, shape, w_in_grad)
+    w_in_grad = join_blocks({0: first_pieces[0]}, tall, upper, shape, w_in_grad)
+    w_in_grad = join_blocks(others_of(second_pieces), tall, lower, shape, w_in_grad)
+    w_in_grad = join_blocks(others_of(first_pieces), tall, upper, shape, w_in_grad)
     flank = lax.axis_index("dp") % side
     narrow = jnp.zeros((LINE * (last - part), channels), jnp.float32)
     for mask, piece in second_pieces.items():

time: 456 us -> 452 us (level)
    all_gather x4 -> x3, waiting for transfers between devices: 84.1 us -> 48.7 us  [gather_line(): lax.all_gather(values, 'dp', axis=0, tiled=True, axis_index_groups=line_g...]
    ppermute x30, waiting for transfers between devices: 115 us -> 134 us  [swap(): return lax.ppermute(values, axis, [(i, i ^ offset) for i in range(size)])]
    reduce_scatter x2, waiting for transfers between devices: 0.77 us -> 15.6 us  [scatter_line(): lax.psum_scatter(values, 'dp', scatter_dimension=0, tiled=True, axis_inde...]
    unnamed x118 -> x120, local copies, waits for them, and re-layouts: 19.6 us -> 24.6 us
    pallas_call x8 -> x10, Pallas kernels: 18.9 us -> 17.7 us  [join_blocks(): pl.pallas_call(kernel, grid_spec=pltpu.PrefetchScalarGridSpec(num_scalar_...]
  transfers between devices with their start and end apart: 36 -> 35, of which waited for: 19 -> 19; matrix products, arithmetic and copies ran while one was open for 10% -> 10% of each run, Pallas kernels for 26% -> 26%
where the time goes in v4:
time: 452 us; the launch traced here: 450 us
  waiting for transfers between devices  198 us (44%)
  Pallas kernels  131 us (29%)
  local copies, waits for them, and re-layouts  52.6 us (12%)
  starting transfers between devices  26.9 us (6%)
  other arithmetic  19.9 us (4%)
  between operations  18.4 us (4%)
    ppermute x30, waiting for transfers between devices, swap(): return lax.ppermute(values, axis, [(i, i ^ offset) for i in range(size)])  134 us
    all_gather x3, waiting for transfers between devices, gather_line(): lax.all_gather(values, 'dp', axis=0, tiled=True, axis_index_groups=line_g...  48.7 us
    pallas_call x2, Pallas kernels, scan_backward(): pl.pallas_call(kernel, grid=(span[1] - span[0],), in_specs=in_specs, out_...  38.8 us
    ppermute x30, starting transfers between devices, swap(): return lax.ppermute(values, axis, [(i, i ^ offset) for i in range(size)])  26.5 us
    unnamed x120, local copies, waits for them, and re-layouts  24.6 us
    pallas_call x10, Pallas kernels, join_blocks(): pl.pallas_call(kernel, grid_spec=pltpu.PrefetchScalarGridSpec(num_scalar_...  17.7 us
    pallas_call x2, Pallas kernels, factor_products(): pl.pallas_call(kernel, grid_spec=pltpu.PrefetchScalarGridSpec(num_scalar_...  17.6 us
    pallas_call x1, Pallas kernels, scan_forward(): pl.pallas_call(lambda *refs: forward_kernel(chunk, n, length, *refs[:3],...  16.7 us
  transfers between devices with their start and end apart: 35, of which 19 were waited for; matrix products, arithmetic and copies ran while one was open for 10% of the time, Pallas kernels for 26%

profile of v4, /device:TPU:0, one launch (start us, length us, event | category | flops | bytes accessed | tf_op | source)
XLA Modules:
  0.0 450.2 jit_solution(6344179711148950417)
XLA Ops:
  19.6 6.5 %collective-permute-done.refs_1_ = bf16[128,2048]{1,0:T(8,128)(2,1)} collective-permute-done((bf16[128,2048]{1,0:T(8,128)(2,1)S(1)}, bf16[128,2048]{1,0:T(8,128)(2,1)}, u32[]{:S(2)}, u32[]{:S(2)}) %collective-permute-start) | collective-permute-done | bytes 524320 | tf_op jit(solution)/shard_map/ppermute | solution.py:698
  32.1 9.1 %project_in.1 = (bf16[512,2048]{1,0:T(8,128)(2,1)}, f32[512,1024]{1,0:T(8,128)}, f32[512,1024]{1,0:T(8,128)}, f32[512,160]{1,0:T(8,128)}) custom-call(s32[4]{0:T(128)} %pad_add_fusion.places_ref, bf16[128,2048]{1,0:T(8,128)(2,1)} %copy-done.35, bf16[128,2048]{1,0:T(8,128)(2,1)} %collective-permute-done.refs_1_, ...), custom_call_target="tpu_custom_call" | custom-call | flops 1 | bytes 1 | tf_op jit(solution)/shard_map/project_in/pallas_call | solution.py:339
  47.5 11.6 %project_gate.1 = (bf16[512,2048]{1,0:T(8,128)(2,1)}, f32[512,1024]{1,0:T(8,128)}, f32[512,1024]{1,0:T(8,128)}, f32[512,1024]{1,0:T(8,128)}) custom-call(s32[4]{0:T(128)} %pad_add_fusion.places_ref, bf16[128,2048]{1,0:T(8,128)(2,1)} %copy-done.42, bf16[128,2048]{1,0:T(8,128)(2,1)} %copy-done.43, bf16[128,2048]{1,0:T(8,128)(2,1)} %copy-done.44, ...), custom_call_target="tpu_custom_call" | custom-call | flops 1 | bytes 1 | tf_op jit(solution)/shard_map/project_gate/pallas_call | solution.py:395
  69.7 16.7 %scan_forward.1 = (f32[64,64,128]{2,1,0:T(8,128)S(1)}, f32[512,16,8,128]{3,2,1,0:T(8,128)}) custom-call(f32[16960]{0:T(1024)S(1)} %pad_maximum_fusion.1.refs_0_, f32[64,64,128]{2,1,0:T(8,128)S(1)} %divide_bitcast_fusion.refs_1_, f32[64,64,128]{2,1,0:T(8,128)} %bitcast.107, f32[512,1024]{1,0:T(8,128)} %get-tuple-element.38.refs_3_, ...), custom_call_target="tpu_custom_call" | custom-call | flops 1 | bytes 1 | tf_op jit(solution)/shard_map/scan_forward/pallas_call | solution.py:110
  91.5 15.2 %scan_backward.2 = (f32[64,64,128]{2,1,0:T(8,128)S(1)}, f32[64,64,128]{2,1,0:T(8,128)}, f32[512,16]{1,0:T(8,128)S(1)}, f32[512,16]{1,0:T(8,128)S(1)}, f32[512,12...) custom-call(f32[16960]{0:T(1024)S(1)} %pad_maximum_fusion.1.refs_0_, f32[64,64,128]{2,1,0:T(8,128)} %copy-done.4, ...), custom_call_target="tpu_custom_call" | custom-call | flops 1 | bytes 1 | tf_op jit(solution)/shard_map/scan_backward/pallas_call | solution.py:268
  109.5 4.2 collective-permute-done.14.refs_13_
  114.5 10.2 %factor_products.2.refs_14_ = bf16[4,2,512,512]{3,2,1,0:T(8,128)(2,1)} custom-call(s32[4]{0:T(128)} %pad_add_fusion.places_ref, bf16[512,2048]{1,0:T(8,128)(2,1)} %get-tuple-element.37.refs_4_.refs_0_, bf16[128,4096]{1,0:T(8,128)(2,1)} %broadcast_add_fusion.refs_1_.refs_8_, bf16[128,4096]{1,0:T(8,128)(2,1)} %collective-permute-done.10.refs_2_.refs_9_, ...), custom_call_target="tpu_custom_call" | custom-call | flops 1 | bytes 1 | tf_op jit(solution)/shard_map/factor_products/pallas_call | solution.py:551
  130.0 23.6 %scan_backward.3 = (f32[64,64,128]{2,1,0:T(8,128)S(1)}, f32[64,64,128]{2,1,0:T(8,128)S(1)}, f32[512,16]{1,0:T(8,128)S(1)}, f32[512,16]{1,0:T(8,128)S(1)}, f32[51...) custom-call(f32[16960]{0:T(1024)S(1)} %pad_maximum_fusion.1.refs_0_,, ...), custom_call_target="tpu_custom_call", output_to_operand_aliasing={{0}: (9, {}), {1}: (10, {}), {2}: (11, {}), {3}: (12, {}), ... | custom-call | flops 1 | bytes 1 | tf_op jit(solution)/shard_map/scan_backward/pallas_call | solution.py:268
  158.0 7.0 %collective-permute-done.16 = f32[256,160]{1,0:T(8,128)S(1)} collective-permute-done((f32[256,160]{1,0:T(8,128)S(1)}, f32[256,160]{1,0:T(8,128)S(1)}, u32[]{:S(2)}, u32[]{:S(2)}) %collective-permute-start.16) | collective-permute-done | bytes 163872 | tf_op jit(solution)/shard_map/ppermute | solution.py:698
  167.4 7.0 %finish_inner.1 = (bf16[512,1024]{1,0:T(8,128)(2,1)}, f32[8,1024]{1,0:T(8,128)}) custom-call(f32[512,1024]{1,0:T(8,128)} %bitcast.112, bf16[512,160]{1,0:T(8,128)(2,1)} %convert_element_type.156.pg_ref, bf16[160,1024]{1,0:T(8,128)(2,1)} %bitcast.126, f32[512,1024]{1,0:T(8,128)} %get-tuple-element.57.inner_ref, f32[512,3]{1,0:T(8,128)} %copy.46.refs_5_.allow_ref, ...), custom_call_target="tpu_custom_call" | custom-call | flops 1 | bytes 1 | tf_op jit(solution)/shard_map/finish_inner/pallas_call | solution.py:443
  178.2 8.4 %collective-permute-done.21 = bf16[320,512]{1,0:T(8,128)(2,1)S(1)} collective-permute-done((bf16[320,512]{1,0:T(8,128)(2,1)S(1)}, bf16[320,512]{1,0:T(8,128)(2,1)S(1)}, u32[]{:S(2)}, u32[]{:S(2)}) %collective-permute-start.21) | collective-permute-done | bytes 327712 | tf_op jit(solution)/shard_map/ppermute | solution.py:698
  187.5 15.6 %reduce-scatter.3.cloned.1.call-done.refs_0_ = bf16[1,2,512,512]{3,2,1,0:T(8,128)(2,1)} async-done(((bf16[4,2,512,512]{3,2,1,0:T(8,128)(2,1)}), bf16[1,2,512,512]{3,2,1,0:T(8,128)(2,1)}) %reduce-scatter.3.cloned.1.call-update) | async-done | bytes 1048592 | tf_op jit(solution)/shard_map/reduce_scatter | solution.py:775
  206.0 11.7 %collective-permute-done.20.refs_6_ = bf16[512,512]{1,0:T(8,128)(2,1)S(1)} collective-permute-done((bf16[512,512]{1,0:T(8,128)(2,1)S(1)}, bf16[512,512]{1,0:T(8,128)(2,1)S(1)}, u32[]{:S(2)}, u32[]{:S(2)}) %collective-permute-start.20) | collective-permute-done | bytes 524320 | tf_op jit(solution)/shard_map/ppermute | solution.py:698
  218.5 7.4 %factor_products.3.refs_0_.values_ref = bf16[4,608,512]{2,1,0:T(8,128)(2,1)} custom-call(s32[4]{0:T(128)} %pad_add_fusion.places_ref, bf16[512,2048]{1,0:T(8,128)(2,1)} %get-tuple-element.37.refs_4_.refs_0_, bf16[128,4096]{1,0:T(8,128)(2,1)} %broadcast_add_fusion.refs_1_.refs_8_, bf16[128,4096]{1,0:T(8,128)(2,1)} %collective-permute-done.10.refs_2_.refs_9_, ...), custom_call_target="tpu_custom_call" | custom-call | flops 1 | bytes 1 | tf_op jit(solution)/shard_map/factor_products/pallas_call | solution.py:551
  228.2 8.7 %project_normed.1 = f32[512,2048]{1,0:T(8,128)} custom-call(bf16[512,1024]{1,0:T(8,128)(2,1)S(1)} %copy-done.12, bf16[512,1024]{1,0:T(8,128)(2,1)S(1)} %get-tuple-element.67.refs_8_.gate_ref, bf16[2,2048,1024]{2,1,0:T(8,128)(2,1)} %w_ref.3, bf16[4,608,512]{2,1,0:T(8,128)(2,1)S(1)} %copy-done.1), custom_call_target="tpu_custom_call" | custom-call | flops 1 | bytes 1 | tf_op jit(solution)/shard_map/project_normed/pallas_call | solution.py:654
  253.6 9.3 %collective-permute-done.23 = bf16[1,1,128,2048]{3,2,1,0:T(8,128)(2,1)} collective-permute-done((bf16[1,1,128,2048]{3,2,1,0:T(8,128)(2,1)}, bf16[1,1,128,2048]{3,2,1,0:T(8,128)(2,1)}, u32[]{:S(2)}, u32[]{:S(2)}) %collective-permute-start.23) | collective-permute-done | bytes 524320 | tf_op jit(solution)/shard_map/ppermute | solution.py:698
  265.9 7.4 %collective-permute-done.24 = f32[2048]{0:T(1024)S(1)} collective-permute-done((f32[2048]{0:T(1024)S(1)}, f32[2048]{0:T(1024)S(1)}, u32[]{:S(2)}, u32[]{:S(2)}) %collective-permute-start.24) | collective-permute-done | bytes 8224 | tf_op jit(solution)/shard_map/ppermute | solution.py:698
  278.1 7.9 %all-gather.4.cloned.1.call-done.refs_1_ = bf16[4,2,512,512]{3,2,1,0:T(8,128)(2,1)} async-done(((bf16[1,2,512,512]{3,2,1,0:T(8,128)(2,1)}), bf16[4,2,512,512]{3,2,1,0:T(8,128)(2,1)}) %all-gather.4.cloned.1.call-update) | async-done | bytes 4194320 | tf_op jit(solution)/shard_map/all_gather | solution.py:781
  286.0 3.8 fusion.31
  292.7 45.9 %collective-permute-done.26.refs_2_.refs_0_ = bf16[4,512,512]{2,1,0:T(8,128)(2,1)S(1)} collective-permute-done((bf16[4,512,512]{2,1,0:T(8,128)(2,1)S(1)}, bf16[4,512,512]{2,1,0:T(8,128)(2,1)S(1)}, u32[]{:S(2)}, u32[]{:S(2)}) %collective-permute-start.26) | collective-permute-done | bytes 2097184 | tf_op jit(solution)/shard_map/ppermute | solution.py:698
  344.9 30.4 %all-gather.6.cloned.1.call-done.refs_0_ = bf16[4,352,512]{2,1,0:T(8,128)(2,1)} async-done(((bf16[1,352,512]{2,1,0:T(8,128)(2,1)}), bf16[4,352,512]{2,1,0:T(8,128)(2,1)}) %all-gather.6.cloned.1.call-update) | async-done | bytes 1441808 | tf_op jit(solution)/shard_map/all_gather | solution.py:781
  393.9 10.4 %all-gather.8.cloned.1.call-done.refs_0_ = bf16[4,256,512]{2,1,0:T(8,128)(2,1)} async-done(((bf16[1,256,512]{2,1,0:T(8,128)(2,1)}), bf16[4,256,512]{2,1,0:T(8,128)(2,1)}) %all-gather.8.cloned.1.call-update) | async-done | bytes 1048592 | tf_op jit(solution)/shard_map/all_gather | solution.py:781
  410.7 10.8 %collective-permute-done.27.refs_0_ = bf16[4,352,512]{2,1,0:T(8,128)(2,1)S(1)} collective-permute-done((bf16[4,352,512]{2,1,0:T(8,128)(2,1)}, bf16[4,352,512]{2,1,0:T(8,128)(2,1)S(1)}, u32[]{:S(2)}, u32[]{:S(2)}) %collective-permute-start.27) | collective-permute-done | bytes 1441824 | tf_op jit(solution)/shard_map/ppermute | solution.py:698
  426.9 14.9 %collective-permute-done.29.refs_0_ = bf16[4,256,512]{2,1,0:T(8,128)(2,1)S(1)} collective-permute-done((bf16[4,256,512]{2,1,0:T(8,128)(2,1)}, bf16[4,256,512]{2,1,0:T(8,128)(2,1)S(1)}, u32[]{:S(2)}, u32[]{:S(2)}) %collective-permute-start.29) | collective-permute-done | bytes 1048608 | tf_op jit(solution)/shard_map/ppermute | solution.py:698
  (272 shorter events, 128.1 us)
Async XLA Ops:
  7.2 195.8 %reduce-scatter.3.cloned.1.call-start = ((), (), s32[]{:S(2)}) async-start(), calls=%async_computation.2 | async-start | bytes 5242880 | tf_op jit(solution)/shard_map/reduce_scatter | solution.py:775
  11.0 15.1 %collective-permute-start = (bf16[128,2048]{1,0:T(8,128)(2,1)S(1)}, bf16[128,2048]{1,0:T(8,128)(2,1)}, u32[]{:S(2)}, u32[]{:S(2)}) collective-permute-start(bf16[128,2048]{1,0:T(8,128)(2,1)S(1)} %fusion.4.refs_0_), channel_id=1, source_target_pairs={{0,2},{1,3},{2,0},{3,1},{4,6},{5,7},{6,4},{7,5},{8,10},{9,11},{10,... | collective-permute-start | bytes 1572872 | tf_op jit(solution)/shard_map/ppermute | solution.py:698
  14.1 18.1 %collective-permute-start.1 = (bf16[128,2048]{1,0:T(8,128)(2,1)S(1)}, bf16[128,2048]{1,0:T(8,128)(2,1)}, u32[]{:S(2)}, u32[]{:S(2)}) collective-permute-start(bf16[128,2048]{1,0:T(8,128)(2,1)S(1)} %fusion.4.refs_0_), channel_id=1, source_target_pairs={{0,1},{1,0},{2,3},{3,2},{4,5},{5,4},{6,7},{7,6},{8,9},{9,8},{10,11... | collective-permute-start | bytes 1572872 | tf_op jit(solution)/shard_map/ppermute | solution.py:698
  16.1 30.1 %collective-permute-start.8 = (bf16[128,4096]{1,0:T(8,128)(2,1)}, bf16[128,4096]{1,0:T(8,128)(2,1)S(1)}, u32[]{:S(2)}, u32[]{:S(2)}) collective-permute-start(bf16[128,4096]{1,0:T(8,128)(2,1)} %pad_maximum_fusion), channel_id=1, source_target_pairs={{0,4},{4,0},{8,12},{12,8},{16,20},{20,16},{24,28},{28,24},{1,5},{5... | collective-permute-start | bytes 3145736 | tf_op jit(solution)/shard_map/ppermute | solution.py:698
  28.1 14.8 %collective-permute-start.5 = (bf16[128,2048]{1,0:T(8,128)(2,1)S(1)}, bf16[128,2048]{1,0:T(8,128)(2,1)S(1)}, u32[]{:S(2)}, u32[]{:S(2)}) collective-permute-start(bf16[128,2048]{1,0:T(8,128)(2,1)S(1)} %broadcast_add_fusion.1.refs_0_), channel_id=1, source_target_pairs={{0,2},{1,3},{2,0},{3,1},{4,6},{5,7},{6,4},{7,5},{8,10},{9,11},{10,... | collective-permute-start | bytes 1572872 | tf_op jit(solution)/shard_map/ppermute | solution.py:698
  45.0 16.0 %collective-permute-start.4 = (f32[256,160]{1,0:T(8,128)S(1)}, f32[256,160]{1,0:T(8,128)}, u32[]{:S(2)}, u32[]{:S(2)}) collective-permute-start(f32[256,160]{1,0:T(8,128)S(1)} %dynamic-slice_add_fusion.1), channel_id=1, source_target_pairs={{0,2},{1,3},{2,0},{3,1},{4,6},{5,7},{6,4},{7,5},{8,10},{9,11},{10,... | collective-permute-start | bytes 491528 | tf_op jit(solution)/shard_map/ppermute | solution.py:698
  66.2 47.5 %collective-permute-start.10 = (bf16[128,4096]{1,0:T(8,128)(2,1)}, bf16[128,4096]{1,0:T(8,128)(2,1)}, u32[]{:S(2)}, u32[]{:S(2)}) collective-permute-start(bf16[128,4096]{1,0:T(8,128)(2,1)} %broadcast_add_fusion.refs_1_.refs_8_), channel_id=1, source_target_pairs={{0,2},{1,3},{2,0},{3,1},{4,6},{5,7},{6,4},{7,5},{8,10},{9,11},{10,... | collective-permute-start | bytes 3145736 | tf_op jit(solution)/shard_map/ppermute | solution.py:698
  67.8 45.9 %collective-permute-start.11 = (bf16[128,4096]{1,0:T(8,128)(2,1)}, bf16[128,4096]{1,0:T(8,128)(2,1)}, u32[]{:S(2)}, u32[]{:S(2)}) collective-permute-start(bf16[128,4096]{1,0:T(8,128)(2,1)} %broadcast_add_fusion.refs_1_.refs_8_), channel_id=1, source_target_pairs={{0,1},{1,0},{2,3},{3,2},{4,5},{5,4},{6,7},{7,6},{8,9},{9,8},{10,11... | collective-permute-start | bytes 3145736 | tf_op jit(solution)/shard_map/ppermute | solution.py:698
  67.8 45.9 %collective-permute-start.12 = (bf16[128,4096]{1,0:T(8,128)(2,1)}, bf16[128,4096]{1,0:T(8,128)(2,1)}, u32[]{:S(2)}, u32[]{:S(2)}) collective-permute-start(bf16[128,4096]{1,0:T(8,128)(2,1)} %broadcast_add_fusion.refs_1_.refs_8_), channel_id=1, source_target_pairs={{0,3},{1,2},{2,1},{3,0},{4,7},{5,6},{6,5},{7,4},{8,11},{9,10},{10,... | collective-permute-start | bytes 3145736 | tf_op jit(solution)/shard_map/ppermute | solution.py:698
  88.6 20.9 %collective-permute-start.13 = (bf16[512,512]{1,0:T(8,128)(2,1)S(1)}, bf16[512,512]{1,0:T(8,128)(2,1)S(1)}, u32[]{:S(2)}, u32[]{:S(2)}) collective-permute-start(bf16[512,512]{1,0:T(8,128)(2,1)S(1)} %get-tuple-element.78), channel_id=1, source_target_pairs={{0,4},{4,0},{8,12},{12,8},{16,20},{20,16},{24,28},{28,24},{1,5},{5... | collective-permute-start | bytes 1572872 | tf_op jit(solution)/shard_map/ppermute | solution.py:698
  91.1 22.6 %collective-permute-start.14 = (bf16[512,512]{1,0:T(8,128)(2,1)S(1)}, bf16[512,512]{1,0:T(8,128)(2,1)S(1)}, u32[]{:S(2)}, u32[]{:S(2)}) collective-permute-start(bf16[512,512]{1,0:T(8,128)(2,1)S(1)} %get-tuple-element.76), channel_id=1, source_target_pairs={{0,4},{4,0},{8,12},{12,8},{16,20},{20,16},{24,28},{28,24},{1,5},{5... | collective-permute-start | bytes 1572872 | tf_op jit(solution)/shard_map/ppermute | solution.py:698
  124.7 161.2 %all-gather.4.cloned.1.call-start = ((), (), s32[]{:S(2)}) async-start(), calls=%async_computation.3 | async-start | bytes 5242880 | tf_op jit(solution)/shard_map/all_gather | solution.py:781
  176.7 9.8 %collective-permute-start.21 = (bf16[320,512]{1,0:T(8,128)(2,1)S(1)}, bf16[320,512]{1,0:T(8,128)(2,1)S(1)}, u32[]{:S(2)}, u32[]{:S(2)}) collective-permute-start(bf16[320,512]{1,0:T(8,128)(2,1)S(1)} %constant_dynamic-slice_fusion), channel_id=1, source_target_pairs={{0,4},{4,0},{8,12},{12,8},{16,20},{20,16},{24,28},{28,24},{1,5},{5... | collective-permute-start | bytes 983048 | tf_op jit(solution)/shard_map/ppermute | solution.py:698
  203.0 135.6 %reduce-scatter.5.cloned.1.call-start = ((), (), s32[]{:S(2)}) async-start(), calls=%async_computation.4 | async-start | bytes 3112960 | tf_op jit(solution)/shard_map/reduce_scatter | solution.py:775
  204.0 13.7 %collective-permute-start.20 = (bf16[512,512]{1,0:T(8,128)(2,1)S(1)}, bf16[512,512]{1,0:T(8,128)(2,1)S(1)}, u32[]{:S(2)}, u32[]{:S(2)}) collective-permute-start(bf16[512,512]{1,0:T(8,128)(2,1)S(1)} %get-tuple-element.74), channel_id=1, source_target_pairs={{0,4},{4,0},{8,12},{12,8},{16,20},{20,16},{24,28},{28,24},{1,5},{5... | collective-permute-start | bytes 1572872 | tf_op jit(solution)/shard_map/ppermute | solution.py:698
  247.8 15.1 %collective-permute-start.23 = (bf16[1,1,128,2048]{3,2,1,0:T(8,128)(2,1)}, bf16[1,1,128,2048]{3,2,1,0:T(8,128)(2,1)}, u32[]{:S(2)}, u32[]{:S(2)}) collective-permute-start(bf16[1,1,128,2048]{3,2,1,0:T(8,128)(2,1)} %dynamic-slice_convert_fusion), channel_id=1, source_target_pairs={{0,2},{1,3},{2,0},{3,1},{4,6},{5,7},{6,4},{7,5},{8,10},{9,11},{10,... | collective-permute-start | bytes 1572872 | tf_op jit(solution)/shard_map/ppermute | solution.py:698
  253.1 20.2 %collective-permute-start.19 = (bf16[1,1,128,2048]{3,2,1,0:T(8,128)(2,1)}, bf16[1,1,128,2048]{3,2,1,0:T(8,128)(2,1)}, u32[]{:S(2)}, u32[]{:S(2)}) collective-permute-start(bf16[1,1,128,2048]{3,2,1,0:T(8,128)(2,1)} %dynamic-slice_convert_fusion.1), channel_id=1, source_target_pairs={{0,2},{1,3},{2,0},{3,1},{4,6},{5,7},{6,4},{7,5},{8,10},{9,11},{10,... | collective-permute-start | bytes 1572872 | tf_op jit(solution)/shard_map/ppermute | solution.py:698
  264.3 9.0 %collective-permute-start.24 = (f32[2048]{0:T(1024)S(1)}, f32[2048]{0:T(1024)S(1)}, u32[]{:S(2)}, u32[]{:S(2)}) collective-permute-start(f32[2048]{0:T(1024)S(1)} %get-tuple-element.61), channel_id=1, source_target_pairs={{0,2},{1,3},{2,0},{3,1},{4,6},{5,7},{6,4},{7,5},{8,10},{9,11},{10,... | collective-permute-start | bytes 24584 | tf_op jit(solution)/shard_map/ppermute | solution.py:698
  286.0 89.4 %all-gather.6.cloned.1.call-start = ((), (), s32[]{:S(2)}) async-start(), calls=%async_computation.5 | async-start | bytes 1802240 | tf_op jit(solution)/shard_map/all_gather | solution.py:781
  291.2 47.4 %collective-permute-start.26 = (bf16[4,512,512]{2,1,0:T(8,128)(2,1)S(1)}, bf16[4,512,512]{2,1,0:T(8,128)(2,1)S(1)}, u32[]{:S(2)}, u32[]{:S(2)}) collective-permute-start(bf16[4,512,512]{2,1,0:T(8,128)(2,1)S(1)} %bitcast.121), channel_id=1, source_target_pairs={{0,4},{4,0},{8,12},{12,8},{16,20},{20,16},{24,28},{28,24},{1,5},{5... | collective-permute-start | bytes 6291464 | tf_op jit(solution)/shard_map/ppermute | solution.py:698
  341.7 62.6 %all-gather.8.cloned.1.call-start = ((), (), s32[]{:S(2)}) async-start(), calls=%async_computation.6 | async-start | bytes 1310720 | tf_op jit(solution)/shard_map/all_gather | solution.py:781
  341.7 48.8 %collective-permute-start.28 = (bf16[4,512,512]{2,1,0:T(8,128)(2,1)}, bf16[4,512,512]{2,1,0:T(8,128)(2,1)S(1)}, u32[]{:S(2)}, u32[]{:S(2)}) collective-permute-start(bf16[4,512,512]{2,1,0:T(8,128)(2,1)} %bitcast.119), channel_id=1, source_target_pairs={{0,4},{4,0},{8,12},{12,8},{16,20},{20,16},{24,28},{28,24},{1,5},{5... | collective-permute-start | bytes 6291464 | tf_op jit(solution)/shard_map/ppermute | solution.py:698
  375.4 46.1 %collective-permute-start.27 = (bf16[4,352,512]{2,1,0:T(8,128)(2,1)}, bf16[4,352,512]{2,1,0:T(8,128)(2,1)S(1)}, u32[]{:S(2)}, u32[]{:S(2)}) collective-permute-start(bf16[4,352,512]{2,1,0:T(8,128)(2,1)} %all-gather.6.cloned.1.call-done.refs_0_), channel_id=1, source_target_pairs={{0,4},{4,0},{8,12},{12,8},{16,20},{20,16},{24,28},{28,24},{1,5},{5... | collective-permute-start | bytes 4325384 | tf_op jit(solution)/shard_map/ppermute | solution.py:698
  404.3 37.6 %collective-permute-start.29 = (bf16[4,256,512]{2,1,0:T(8,128)(2,1)}, bf16[4,256,512]{2,1,0:T(8,128)(2,1)S(1)}, u32[]{:S(2)}, u32[]{:S(2)}) collective-permute-start(bf16[4,256,512]{2,1,0:T(8,128)(2,1)} %touch.7.refs_0_), channel_id=1, source_target_pairs={{0,4},{4,0},{8,12},{12,8},{16,20},{20,16},{24,28},{28,24},{1,5},{5... | collective-permute-start | bytes 3145736 | tf_op jit(solution)/shard_map/ppermute | solution.py:698
  (70 other events, 480.4 us)
Sparse Core Ops, SparseCore 0:
  124.9 78.0 reduce-scatter.2
  204.7 81.2 all-gather.3
  288.4 48.6 reduce-scatter.4
  341.8 33.5 all-gather.5
  377.5 26.7 all-gather.7

commit v5 on v4

--- a/solution.py
+++ b/solution.py
@@ -719,23 +719,15 @@
     return other[(slice(0, 1),) * other.ndim].reshape(()).astype(jnp.float32) * 0.0
 
 
-def sum_mp(values, after=None):
-    rank = lax.axis_index("mp")
-    half = values.shape[0] // 2
-    odd = rank % 2
-    mine = lax.dynamic_slice_in_dim(values, odd * half, half, 0)
-    other = lax.dynamic_slice_in_dim(values, (1 - odd) * half, half, 0)
-    mine = mine + swap(other, "mp", 1)
-    bit = 2
-    while bit < lax.axis_size("mp"):
-        mine = mine + swap(mine, "mp", bit)
+def sum_mp(values, after=()):
+    bit, size = 1, lax.axis_size("mp")
+    while bit < size:
+        got = swap(values, "mp", bit)
         bit *= 2
-    if after is not None:
-        mine = mine + nothing(after)
-    other = swap(mine, "mp", 1)
-    whole = jnp.zeros(values.shape, values.dtype)
-    whole = lax.dynamic_update_slice_in_dim(whole, mine, odd * half, 0)
-    return lax.dynamic_update_slice_in_dim(whole, other, (1 - odd) * half, 0)
+        if after and bit == size:
+            got = touch(got, after)
+        values = values + got
+    return values
 
 
 def scatter_mp(values):
@@ -895,10 +887,9 @@
     group_ograd, gate_silu, mixer_grad, gate_slope = project_gate(
         list(ograd_pieces.values()), list(ograd_pieces), group_normed, w_in, w_out, beside
     )
-    proj = sum_mp(proj_part, gate_silu)
+    proj = sum_mp(proj_part, (gate_silu,))
     others = []
     for rows in beside:
-        rows = tie(rows, proj)
         others.append({mask: swap(rows, "mp", mask) if mask else rows for mask in masks})
     low_rank = proj[:, :R].astype(jnp.bfloat16)
     keys = proj[:, R : R + state_size]

time: 452 us -> 446 us (0.987)
    ppermute x30 -> x28, waiting for transfers between devices: 134 us -> 137 us  [swap(): return lax.ppermute(values, axis, [(i, i ^ offset) for i in range(size)])]
    unnamed x120 -> x124, local copies, waits for them, and re-layouts: 24.6 us -> 25.3 us
    ppermute x30 -> x28, starting transfers between devices: 26.5 us -> 26.1 us  [swap(): return lax.ppermute(values, axis, [(i, i ^ offset) for i in range(size)])]
  transfers between devices with their start and end apart: 35 -> 33, of which waited for: 19 -> 18; matrix products, arithmetic and copies ran while one was open for 10% -> 9% of each run, Pallas kernels for 26% -> 27%
where the time goes in v5:
time: 446 us; the launch traced here: 444 us
  waiting for transfers between devices  198 us (44%)
  Pallas kernels  131 us (29%)
  local copies, waits for them, and re-layouts  49.7 us (11%)
  starting transfers between devices  26.5 us (6%)
  other arithmetic  19.1 us (4%)
  between operations  17 us (4%)
    ppermute x28, waiting for transfers between devices, swap(): return lax.ppermute(values, axis, [(i, i ^ offset) for i in range(size)])  137 us
    all_gather x3, waiting for transfers between devices, gather_line(): lax.all_gather(values, 'dp', axis=0, tiled=True, axis_index_groups=line_g...  48.7 us
    pallas_call x2, Pallas kernels, scan_backward(): pl.pallas_call(kernel, grid=(span[1] - span[0],), in_specs=in_specs, out_...  38.8 us
    ppermute x28, starting transfers between devices, swap(): return lax.ppermute(values, axis, [(i, i ^ offset) for i in range(size)])  26.1 us
    unnamed x124, local copies, waits for them, and re-layouts  25.3 us
    pallas_call x10, Pallas kernels, join_blocks(): pl.pallas_call(kernel, grid_spec=pltpu.PrefetchScalarGridSpec(num_scalar_...  17.7 us
    pallas_call x2, Pallas kernels, factor_products(): pl.pallas_call(kernel, grid_spec=pltpu.PrefetchScalarGridSpec(num_scalar_...  17.7 us
    pallas_call x1, Pallas kernels, scan_forward(): pl.pallas_call(lambda *refs: forward_kernel(chunk, n, length, *refs[:3],...  16.7 us
  transfers between devices with their start and end apart: 33, of which 18 were waited for; matrix products, arithmetic and copies ran while one was open for 9% of the time, Pallas kernels for 27%

profile of v5, /device:TPU:0, one launch (start us, length us, event | category | flops | bytes accessed | tf_op | source)
XLA Modules:
  0.0 444.5 jit_solution(9017220623179572795)
XLA Ops:
  19.6 6.4 %collective-permute-done.refs_1_ = bf16[128,2048]{1,0:T(8,128)(2,1)S(1)} collective-permute-done((bf16[128,2048]{1,0:T(8,128)(2,1)S(1)}, bf16[128,2048]{1,0:T(8,128)(2,1)S(1)}, u32[]{:S(2)}, u32[]{:S(2)}) %collective-permute-start) | collective-permute-done | bytes 524320 | tf_op jit(solution)/shard_map/ppermute | solution.py:698
  32.3 9.2 %project_in.1 = (bf16[512,2048]{1,0:T(8,128)(2,1)}, f32[512,1024]{1,0:T(8,128)}, f32[512,1024]{1,0:T(8,128)}, f32[512,160]{1,0:T(8,128)}) custom-call(s32[4]{0:T(128)} %pad_add_fusion.places_ref, bf16[128,2048]{1,0:T(8,128)(2,1)} %copy-done.35, bf16[128,2048]{1,0:T(8,128)(2,1)} %copy-done.45, bf16[128,2048]{1,0:T(8,128)(2,1)} %copy-done.46, ...), custom_call_target="tpu_custom_call" | custom-call | flops 1 | bytes 1 | tf_op jit(solution)/shard_map/project_in/pallas_call | solution.py:339
  48.9 11.5 %project_gate.1 = (bf16[512,2048]{1,0:T(8,128)(2,1)}, f32[512,1024]{1,0:T(8,128)}, f32[512,1024]{1,0:T(8,128)}, f32[512,1024]{1,0:T(8,128)}) custom-call(s32[4]{0:T(128)} %pad_add_fusion.places_ref, bf16[128,2048]{1,0:T(8,128)(2,1)} %copy-done.40, bf16[128,2048]{1,0:T(8,128)(2,1)} %copy-done.42, bf16[128,2048]{1,0:T(8,128)(2,1)} %copy-done.43, ...), custom_call_target="tpu_custom_call" | custom-call | flops 1 | bytes 1 | tf_op jit(solution)/shard_map/project_gate/pallas_call | solution.py:395
  64.0 16.7 %scan_forward.1 = (f32[64,64,128]{2,1,0:T(8,128)S(1)}, f32[512,16,8,128]{3,2,1,0:T(8,128)}) custom-call(f32[16960]{0:T(1024)S(1)} %pad_maximum_fusion.1.refs_0_, f32[64,64,128]{2,1,0:T(8,128)S(1)} %divide_bitcast_fusion.refs_1_, f32[64,64,128]{2,1,0:T(8,128)} %bitcast.105, f32[512,1024]{1,0:T(8,128)} %get-tuple-element.38.refs_1_.refs_3_, ...), custom_call_target="tpu_custom_call" | custom-call | flops 1 | bytes 1 | tf_op jit(solution)/shard_map/scan_forward/pallas_call | solution.py:110
  85.8 15.2 %scan_backward.2 = (f32[64,64,128]{2,1,0:T(8,128)S(1)}, f32[64,64,128]{2,1,0:T(8,128)}, f32[512,16]{1,0:T(8,128)S(1)}, f32[512,16]{1,0:T(8,128)S(1)}, f32[512,12...) custom-call(f32[16960]{0:T(1024)S(1)} %pad_maximum_fusion.1.refs_0_, f32[64,64,128]{2,1,0:T(8,128)} %copy-done.4, ...), custom_call_target="tpu_custom_call" | custom-call | flops 1 | bytes 1 | tf_op jit(solution)/shard_map/scan_backward/pallas_call | solution.py:268
  104.0 3.8 collective-permute-done.13.refs_13_
  108.7 10.3 %factor_products.2.refs_14_ = bf16[4,2,512,512]{3,2,1,0:T(8,128)(2,1)} custom-call(s32[4]{0:T(128)} %pad_add_fusion.places_ref, bf16[512,2048]{1,0:T(8,128)(2,1)} %get-tuple-element.37.refs_4_.refs_0_, bf16[128,4096]{1,0:T(8,128)(2,1)} %collective-permute-done.8.refs_7_.refs_1_.refs_8_, bf16[128,4096]{1,0:T(8,128)(2,1)} %collective-permute-done.9.refs_2_.refs_9_, ...), custom_call_target="tpu_custom_call" | custom-call | flops 1 | bytes 1 | tf_op jit(solution)/shard_map/factor_products/pallas_call | solution.py:551
  124.3 23.7 %scan_backward.3 = (f32[64,64,128]{2,1,0:T(8,128)S(1)}, f32[64,64,128]{2,1,0:T(8,128)S(1)}, f32[512,16]{1,0:T(8,128)S(1)}, f32[512,16]{1,0:T(8,128)S(1)}, f32[51...) custom-call(f32[16960]{0:T(1024)S(1)} %pad_maximum_fusion.1.refs_0_,, ...), custom_call_target="tpu_custom_call", output_to_operand_aliasing={{0}: (9, {}), {1}: (10, {}), {2}: (11, {}), {3}: (12, {}), ... | custom-call | flops 1 | bytes 1 | tf_op jit(solution)/shard_map/scan_backward/pallas_call | solution.py:268
  153.1 11.7 %collective-permute-done.15 = f32[512,160]{1,0:T(8,128)S(1)} collective-permute-done((f32[512,160]{1,0:T(8,128)S(1)}, f32[512,160]{1,0:T(8,128)S(1)}, u32[]{:S(2)}, u32[]{:S(2)}) %collective-permute-start.15) | collective-permute-done | bytes 327712 | tf_op jit(solution)/shard_map/ppermute | solution.py:698
  165.5 7.0 %finish_inner.1 = (bf16[512,1024]{1,0:T(8,128)(2,1)}, f32[8,1024]{1,0:T(8,128)}) custom-call(f32[512,1024]{1,0:T(8,128)} %bitcast.110, bf16[512,160]{1,0:T(8,128)(2,1)} %add_convert_fusion.1.pg_ref, bf16[160,1024]{1,0:T(8,128)(2,1)} %bitcast.124, f32[512,1024]{1,0:T(8,128)} %get-tuple-element.57.inner_ref, f32[512,3]{1,0:T(8,128)} %copy.47.refs_5_.allow_ref, ...), custom_call_target="tpu_custom_call" | custom-call | flops 1 | bytes 1 | tf_op jit(solution)/shard_map/finish_inner/pallas_call | solution.py:443
  176.2 7.7 %collective-permute-done.19 = bf16[320,512]{1,0:T(8,128)(2,1)S(1)} collective-permute-done((bf16[320,512]{1,0:T(8,128)(2,1)S(1)}, bf16[320,512]{1,0:T(8,128)(2,1)S(1)}, u32[]{:S(2)}, u32[]{:S(2)}) %collective-permute-start.19) | collective-permute-done | bytes 327712 | tf_op jit(solution)/shard_map/ppermute | solution.py:698
  184.8 12.4 %reduce-scatter.3.cloned.1.call-done.refs_0_ = bf16[1,2,512,512]{3,2,1,0:T(8,128)(2,1)} async-done(((bf16[4,2,512,512]{3,2,1,0:T(8,128)(2,1)}), bf16[1,2,512,512]{3,2,1,0:T(8,128)(2,1)}) %reduce-scatter.3.cloned.1.call-update) | async-done | bytes 1048592 | tf_op jit(solution)/shard_map/reduce_scatter | solution.py:767
  200.2 11.7 %collective-permute-done.18.refs_6_ = bf16[512,512]{1,0:T(8,128)(2,1)S(1)} collective-permute-done((bf16[512,512]{1,0:T(8,128)(2,1)S(1)}, bf16[512,512]{1,0:T(8,128)(2,1)S(1)}, u32[]{:S(2)}, u32[]{:S(2)}) %collective-permute-start.18) | collective-permute-done | bytes 524320 | tf_op jit(solution)/shard_map/ppermute | solution.py:698
  212.8 7.3 %factor_products.3.refs_0_.values_ref = bf16[4,608,512]{2,1,0:T(8,128)(2,1)} custom-call(s32[4]{0:T(128)} %pad_add_fusion.places_ref, bf16[512,2048]{1,0:T(8,128)(2,1)} %get-tuple-element.37.refs_4_.refs_0_, bf16[128,4096]{1,0:T(8,128)(2,1)} %collective-permute-done.8.refs_7_.refs_1_.refs_8_, bf16[128,4096]{1,0:T(8,128)(2,1)} %collective-permute-done.9.refs_2_.refs_9_, ...), custom_call_target="tpu_custom_call" | custom-call | flops 1 | bytes 1 | tf_op jit(solution)/shard_map/factor_products/pallas_call | solution.py:551
  222.5 8.7 %project_normed.1 = f32[512,2048]{1,0:T(8,128)} custom-call(bf16[512,1024]{1,0:T(8,128)(2,1)S(1)} %copy-done.12, bf16[512,1024]{1,0:T(8,128)(2,1)S(1)} %get-tuple-element.63.refs_8_.gate_ref, bf16[2,2048,1024]{2,1,0:T(8,128)(2,1)} %w_ref.3, bf16[4,608,512]{2,1,0:T(8,128)(2,1)S(1)} %copy-done.1), custom_call_target="tpu_custom_call" | custom-call | flops 1 | bytes 1 | tf_op jit(solution)/shard_map/project_normed/pallas_call | solution.py:654
  247.9 9.3 %collective-permute-done.21 = bf16[1,1,128,2048]{3,2,1,0:T(8,128)(2,1)} collective-permute-done((bf16[1,1,128,2048]{3,2,1,0:T(8,128)(2,1)}, bf16[1,1,128,2048]{3,2,1,0:T(8,128)(2,1)}, u32[]{:S(2)}, u32[]{:S(2)}) %collective-permute-start.21) | collective-permute-done | bytes 524320 | tf_op jit(solution)/shard_map/ppermute | solution.py:698
  260.1 7.4 %collective-permute-done.22 = f32[2048]{0:T(1024)S(1)} collective-permute-done((f32[2048]{0:T(1024)S(1)}, f32[2048]{0:T(1024)S(1)}, u32[]{:S(2)}, u32[]{:S(2)}) %collective-permute-start.22) | collective-permute-done | bytes 8224 | tf_op jit(solution)/shard_map/ppermute | solution.py:698
  272.3 7.9 %all-gather.4.cloned.1.call-done.refs_1_ = bf16[4,2,512,512]{3,2,1,0:T(8,128)(2,1)} async-done(((bf16[1,2,512,512]{3,2,1,0:T(8,128)(2,1)}), bf16[4,2,512,512]{3,2,1,0:T(8,128)(2,1)}) %all-gather.4.cloned.1.call-update) | async-done | bytes 4194320 | tf_op jit(solution)/shard_map/all_gather | solution.py:773
  280.3 3.9 fusion.31
  287.0 45.9 %collective-permute-done.24.refs_2_.refs_0_ = bf16[4,512,512]{2,1,0:T(8,128)(2,1)S(1)} collective-permute-done((bf16[4,512,512]{2,1,0:T(8,128)(2,1)S(1)}, bf16[4,512,512]{2,1,0:T(8,128)(2,1)S(1)}, u32[]{:S(2)}, u32[]{:S(2)}) %collective-permute-start.24) | collective-permute-done | bytes 2097184 | tf_op jit(solution)/shard_map/ppermute | solution.py:698
  339.2 30.4 %all-gather.6.cloned.1.call-done.refs_0_ = bf16[4,352,512]{2,1,0:T(8,128)(2,1)} async-done(((bf16[1,352,512]{2,1,0:T(8,128)(2,1)}), bf16[4,352,512]{2,1,0:T(8,128)(2,1)}) %all-gather.6.cloned.1.call-update) | async-done | bytes 1441808 | tf_op jit(solution)/shard_map/all_gather | solution.py:773
  388.2 10.4 %all-gather.8.cloned.1.call-done.refs_0_ = bf16[4,256,512]{2,1,0:T(8,128)(2,1)} async-done(((bf16[1,256,512]{2,1,0:T(8,128)(2,1)}), bf16[4,256,512]{2,1,0:T(8,128)(2,1)}) %all-gather.8.cloned.1.call-update) | async-done | bytes 1048592 | tf_op jit(solution)/shard_map/all_gather | solution.py:773
  404.9 10.8 %collective-permute-done.25.refs_0_ = bf16[4,352,512]{2,1,0:T(8,128)(2,1)S(1)} collective-permute-done((bf16[4,352,512]{2,1,0:T(8,128)(2,1)}, bf16[4,352,512]{2,1,0:T(8,128)(2,1)S(1)}, u32[]{:S(2)}, u32[]{:S(2)}) %collective-permute-start.25) | collective-permute-done | bytes 1441824 | tf_op jit(solution)/shard_map/ppermute | solution.py:698
  421.2 14.9 %collective-permute-done.27.refs_0_ = bf16[4,256,512]{2,1,0:T(8,128)(2,1)S(1)} collective-permute-done((bf16[4,256,512]{2,1,0:T(8,128)(2,1)}, bf16[4,256,512]{2,1,0:T(8,128)(2,1)S(1)}, u32[]{:S(2)}, u32[]{:S(2)}) %collective-permute-start.27) | collective-permute-done | bytes 1048608 | tf_op jit(solution)/shard_map/ppermute | solution.py:698
  (263 shorter events, 123.2 us)
Async XLA Ops:
  7.2 190.1 %reduce-scatter.3.cloned.1.call-start = ((), (), s32[]{:S(2)}) async-start(), calls=%async_computation.2 | async-start | bytes 5242880 | tf_op jit(solution)/shard_map/reduce_scatter | solution.py:767
  11.0 15.0 %collective-permute-start = (bf16[128,2048]{1,0:T(8,128)(2,1)S(1)}, bf16[128,2048]{1,0:T(8,128)(2,1)S(1)}, u32[]{:S(2)}, u32[]{:S(2)}) collective-permute-start(bf16[128,2048]{1,0:T(8,128)(2,1)S(1)} %fusion.4.refs_0_), channel_id=1, source_target_pairs={{0,2},{1,3},{2,0},{3,1},{4,6},{5,7},{6,4},{7,5},{8,10},{9,11},{10,... | collective-permute-start | bytes 1572872 | tf_op jit(solution)/shard_map/ppermute | solution.py:698
  14.1 17.3 %collective-permute-start.1 = (bf16[128,2048]{1,0:T(8,128)(2,1)S(1)}, bf16[128,2048]{1,0:T(8,128)(2,1)S(1)}, u32[]{:S(2)}, u32[]{:S(2)}) collective-permute-start(bf16[128,2048]{1,0:T(8,128)(2,1)S(1)} %fusion.4.refs_0_), channel_id=1, source_target_pairs={{0,1},{1,0},{2,3},{3,2},{4,5},{5,4},{6,7},{7,6},{8,9},{9,8},{10,11... | collective-permute-start | bytes 1572872 | tf_op jit(solution)/shard_map/ppermute | solution.py:698
  16.1 29.7 %collective-permute-start.8 = (bf16[128,4096]{1,0:T(8,128)(2,1)}, bf16[128,4096]{1,0:T(8,128)(2,1)}, u32[]{:S(2)}, u32[]{:S(2)}) collective-permute-start(bf16[128,4096]{1,0:T(8,128)(2,1)} %pad_maximum_fusion), channel_id=1, source_target_pairs={{0,4},{4,0},{8,12},{12,8},{16,20},{20,16},{24,28},{28,24},{1,5},{5... | collective-permute-start | bytes 3145736 | tf_op jit(solution)/shard_map/ppermute | solution.py:698
  27.3 14.8 %collective-permute-start.5 = (bf16[128,2048]{1,0:T(8,128)(2,1)S(1)}, bf16[128,2048]{1,0:T(8,128)(2,1)S(1)}, u32[]{:S(2)}, u32[]{:S(2)}) collective-permute-start(bf16[128,2048]{1,0:T(8,128)(2,1)S(1)} %broadcast_add_fusion.refs_0_), channel_id=1, source_target_pairs={{0,2},{1,3},{2,0},{3,1},{4,6},{5,7},{6,4},{7,5},{8,10},{9,11},{10,... | collective-permute-start | bytes 1572872 | tf_op jit(solution)/shard_map/ppermute | solution.py:698
  44.9 15.5 %collective-permute-start.4 = (f32[512,160]{1,0:T(8,128)S(1)}, f32[512,160]{1,0:T(8,128)S(1)}, u32[]{:S(2)}, u32[]{:S(2)}) collective-permute-start(f32[512,160]{1,0:T(8,128)S(1)} %add.204), channel_id=1, source_target_pairs={{0,2},{1,3},{2,0},{3,1},{4,6},{5,7},{6,4},{7,5},{8,10},{9,11},{10,... | collective-permute-start | bytes 983048 | tf_op jit(solution)/shard_map/ppermute | solution.py:698
  45.9 57.8 %collective-permute-start.10 = (bf16[128,4096]{1,0:T(8,128)(2,1)}, bf16[128,4096]{1,0:T(8,128)(2,1)}, u32[]{:S(2)}, u32[]{:S(2)}) collective-permute-start(bf16[128,4096]{1,0:T(8,128)(2,1)} %collective-permute-done.8.refs_7_.refs_1_.refs_8_), channel_id=1, source_target_pairs={{0,1},{1,0},{2,3},{3,2},{4,5},{5,4},{6,7},{7,6},{8,9},{9,8},{10,11... | collective-permute-start | bytes 3145736 | tf_op jit(solution)/shard_map/ppermute | solution.py:698
  46.0 57.7 %collective-permute-start.11 = (bf16[128,4096]{1,0:T(8,128)(2,1)}, bf16[128,4096]{1,0:T(8,128)(2,1)}, u32[]{:S(2)}, u32[]{:S(2)}) collective-permute-start(bf16[128,4096]{1,0:T(8,128)(2,1)} %collective-permute-done.8.refs_7_.refs_1_.refs_8_), channel_id=1, source_target_pairs={{0,3},{1,2},{2,1},{3,0},{4,7},{5,6},{6,5},{7,4},{8,11},{9,10},{10,... | collective-permute-start | bytes 3145736 | tf_op jit(solution)/shard_map/ppermute | solution.py:698
  47.8 56.2 %collective-permute-start.9 = (bf16[128,4096]{1,0:T(8,128)(2,1)}, bf16[128,4096]{1,0:T(8,128)(2,1)}, u32[]{:S(2)}, u32[]{:S(2)}) collective-permute-start(bf16[128,4096]{1,0:T(8,128)(2,1)} %collective-permute-done.8.refs_7_.refs_1_.refs_8_), channel_id=1, source_target_pairs={{0,2},{1,3},{2,0},{3,1},{4,6},{5,7},{6,4},{7,5},{8,10},{9,11},{10,... | collective-permute-start | bytes 3145736 | tf_op jit(solution)/shard_map/ppermute | solution.py:698
  82.9 21.2 %collective-permute-start.12 = (bf16[512,512]{1,0:T(8,128)(2,1)S(1)}, bf16[512,512]{1,0:T(8,128)(2,1)S(1)}, u32[]{:S(2)}, u32[]{:S(2)}) collective-permute-start(bf16[512,512]{1,0:T(8,128)(2,1)S(1)} %get-tuple-element.74), channel_id=1, source_target_pairs={{0,4},{4,0},{8,12},{12,8},{16,20},{20,16},{24,28},{28,24},{1,5},{5... | collective-permute-start | bytes 1572872 | tf_op jit(solution)/shard_map/ppermute | solution.py:698
  85.5 22.4 %collective-permute-start.13 = (bf16[512,512]{1,0:T(8,128)(2,1)S(1)}, bf16[512,512]{1,0:T(8,128)(2,1)S(1)}, u32[]{:S(2)}, u32[]{:S(2)}) collective-permute-start(bf16[512,512]{1,0:T(8,128)(2,1)S(1)} %get-tuple-element.72), channel_id=1, source_target_pairs={{0,4},{4,0},{8,12},{12,8},{16,20},{20,16},{24,28},{28,24},{1,5},{5... | collective-permute-start | bytes 1572872 | tf_op jit(solution)/shard_map/ppermute | solution.py:698
  119.0 161.2 %all-gather.4.cloned.1.call-start = ((), (), s32[]{:S(2)}) async-start(), calls=%async_computation.3 | async-start | bytes 5242880 | tf_op jit(solution)/shard_map/all_gather | solution.py:773
  150.7 14.0 %collective-permute-start.15 = (f32[512,160]{1,0:T(8,128)S(1)}, f32[512,160]{1,0:T(8,128)S(1)}, u32[]{:S(2)}, u32[]{:S(2)}) collective-permute-start(f32[512,160]{1,0:T(8,128)S(1)} %add.216), channel_id=1, source_target_pairs={{0,2},{1,3},{2,0},{3,1},{4,6},{5,7},{6,4},{7,5},{8,10},{9,11},{10,... | collective-permute-start | bytes 983048 | tf_op jit(solution)/shard_map/ppermute | solution.py:698
  174.9 9.0 %collective-permute-start.19 = (bf16[320,512]{1,0:T(8,128)(2,1)S(1)}, bf16[320,512]{1,0:T(8,128)(2,1)S(1)}, u32[]{:S(2)}, u32[]{:S(2)}) collective-permute-start(bf16[320,512]{1,0:T(8,128)(2,1)S(1)} %constant_dynamic-slice_fusion), channel_id=1, source_target_pairs={{0,4},{4,0},{8,12},{12,8},{16,20},{20,16},{24,28},{28,24},{1,5},{5... | collective-permute-start | bytes 983048 | tf_op jit(solution)/shard_map/ppermute | solution.py:698
  197.3 135.6 %reduce-scatter.5.cloned.1.call-start = ((), (), s32[]{:S(2)}) async-start(), calls=%async_computation.4 | async-start | bytes 3112960 | tf_op jit(solution)/shard_map/reduce_scatter | solution.py:767
  198.3 13.7 %collective-permute-start.18 = (bf16[512,512]{1,0:T(8,128)(2,1)S(1)}, bf16[512,512]{1,0:T(8,128)(2,1)S(1)}, u32[]{:S(2)}, u32[]{:S(2)}) collective-permute-start(bf16[512,512]{1,0:T(8,128)(2,1)S(1)} %get-tuple-element.70), channel_id=1, source_target_pairs={{0,4},{4,0},{8,12},{12,8},{16,20},{20,16},{24,28},{28,24},{1,5},{5... | collective-permute-start | bytes 1572872 | tf_op jit(solution)/shard_map/ppermute | solution.py:698
  242.0 15.1 %collective-permute-start.21 = (bf16[1,1,128,2048]{3,2,1,0:T(8,128)(2,1)}, bf16[1,1,128,2048]{3,2,1,0:T(8,128)(2,1)}, u32[]{:S(2)}, u32[]{:S(2)}) collective-permute-start(bf16[1,1,128,2048]{3,2,1,0:T(8,128)(2,1)} %dynamic-slice_convert_fusion), channel_id=1, source_target_pairs={{0,2},{1,3},{2,0},{3,1},{4,6},{5,7},{6,4},{7,5},{8,10},{9,11},{10,... | collective-permute-start | bytes 1572872 | tf_op jit(solution)/shard_map/ppermute | solution.py:698
  247.3 20.2 %collective-permute-start.17 = (bf16[1,1,128,2048]{3,2,1,0:T(8,128)(2,1)}, bf16[1,1,128,2048]{3,2,1,0:T(8,128)(2,1)}, u32[]{:S(2)}, u32[]{:S(2)}) collective-permute-start(bf16[1,1,128,2048]{3,2,1,0:T(8,128)(2,1)} %dynamic-slice_convert_fusion.1), channel_id=1, source_target_pairs={{0,2},{1,3},{2,0},{3,1},{4,6},{5,7},{6,4},{7,5},{8,10},{9,11},{10,... | collective-permute-start | bytes 1572872 | tf_op jit(solution)/shard_map/ppermute | solution.py:698
  280.2 89.4 %all-gather.6.cloned.1.call-start = ((), (), s32[]{:S(2)}) async-start(), calls=%async_computation.5 | async-start | bytes 1802240 | tf_op jit(solution)/shard_map/all_gather | solution.py:773
  285.5 47.4 %collective-permute-start.24 = (bf16[4,512,512]{2,1,0:T(8,128)(2,1)S(1)}, bf16[4,512,512]{2,1,0:T(8,128)(2,1)S(1)}, u32[]{:S(2)}, u32[]{:S(2)}) collective-permute-start(bf16[4,512,512]{2,1,0:T(8,128)(2,1)S(1)} %bitcast.119), channel_id=1, source_target_pairs={{0,4},{4,0},{8,12},{12,8},{16,20},{20,16},{24,28},{28,24},{1,5},{5... | collective-permute-start | bytes 6291464 | tf_op jit(solution)/shard_map/ppermute | solution.py:698
  335.9 62.6 %all-gather.8.cloned.1.call-start = ((), (), s32[]{:S(2)}) async-start(), calls=%async_computation.6 | async-start | bytes 1310720 | tf_op jit(solution)/shard_map/all_gather | solution.py:773
  336.0 48.8 %collective-permute-start.26 = (bf16[4,512,512]{2,1,0:T(8,128)(2,1)}, bf16[4,512,512]{2,1,0:T(8,128)(2,1)S(1)}, u32[]{:S(2)}, u32[]{:S(2)}) collective-permute-start(bf16[4,512,512]{2,1,0:T(8,128)(2,1)} %bitcast.117), channel_id=1, source_target_pairs={{0,4},{4,0},{8,12},{12,8},{16,20},{20,16},{24,28},{28,24},{1,5},{5... | collective-permute-start | bytes 6291464 | tf_op jit(solution)/shard_map/ppermute | solution.py:698
  369.6 46.1 %collective-permute-start.25 = (bf16[4,352,512]{2,1,0:T(8,128)(2,1)}, bf16[4,352,512]{2,1,0:T(8,128)(2,1)S(1)}, u32[]{:S(2)}, u32[]{:S(2)}) collective-permute-start(bf16[4,352,512]{2,1,0:T(8,128)(2,1)} %all-gather.6.cloned.1.call-done.refs_0_), channel_id=1, source_target_pairs={{0,4},{4,0},{8,12},{12,8},{16,20},{20,16},{24,28},{28,24},{1,5},{5... | collective-permute-start | bytes 4325384 | tf_op jit(solution)/shard_map/ppermute | solution.py:698
  398.6 37.6 %collective-permute-start.27 = (bf16[4,256,512]{2,1,0:T(8,128)(2,1)}, bf16[4,256,512]{2,1,0:T(8,128)(2,1)S(1)}, u32[]{:S(2)}, u32[]{:S(2)}) collective-permute-start(bf16[4,256,512]{2,1,0:T(8,128)(2,1)} %touch.9.refs_0_), channel_id=1, source_target_pairs={{0,4},{4,0},{8,12},{12,8},{16,20},{20,16},{24,28},{28,24},{1,5},{5... | collective-permute-start | bytes 3145736 | tf_op jit(solution)/shard_map/ppermute | solution.py:698
  (70 other events, 473.1 us)
Sparse Core Ops, SparseCore 0:
  119.1 78.0 reduce-scatter.2
  198.9 81.2 all-gather.3
  282.6 48.6 reduce-scatter.4
  336.0 33.5 all-gather.5
  371.7 26.7 all-gather.7

commit v6 on v5

--- a/solution.py
+++ b/solution.py
@@ -958,7 +958,7 @@
     sums_of = [gather_line(touch(value, (extra,))) for value in scattered]
     if stacked:
         blocks = sums_of[0].reshape(2 * LINE, width, width)
-        halves = [blocks[:LINE], blocks[LINE:]]
+        halves = [blocks]
     else:
         halves = [
             sums_of[0].reshape(LINE, depth // LINE, width),
@@ -988,11 +988,12 @@
     inner_piece = scatter_line(
         touch(inner_part, sums_of + [block_out, input_grad])
     )
-    inner_piece = touch(inner_piece, tuple(half_pieces[0].values()))
+    sent = [value for pieces in half_pieces for value in pieces.values()]
+    upper_piece = touch(inner_piece[:, :tall], sent)
     second_sum = gather_line(inner_piece[:, tall:])
-    first_sum = gather_line(inner_piece[:, :tall])
+    first_sum = gather_line(upper_piece)
     second_pieces = side_pieces(second_sum)
-    first_pieces = side_pieces(touch(first_sum, tuple(half_pieces[1].values())))
+    first_pieces = side_pieces(first_sum)
 
     shape = (2, depth, channels)
     part_out = lambda start: lambda b, f: (f, b + start)
@@ -1006,12 +1007,9 @@
             return join_blocks(others_of(pieces), height, place_of(0), full, buffer)
         pick = lambda number: 2 * number + job
         buffer = join_blocks({0: blocks}, height, place_of(0), full, None, LINE, pick)
-        for turn, pieces in enumerate(half_pieces):
-            start = turn * LINE // 2
-            buffer = join_blocks(
-                others_of(pieces), height, place_of(start), full, buffer, LINE // 2, pick
-            )
-        return buffer
+        return join_blocks(
+            others_of(half_pieces[0]), height, place_of(0), full, buffer, LINE, pick
+        )
 
     w_out_grad = finished(part_out, width, (channels, depth), 1 if stacked else 0)
     w_in_grad = finished(part_gate, part, shape, 0 if stacked else 1)

time: 446 us -> 438 us (0.982)
  local copies, waits for them, and re-layouts: 49.7 us -> 42 us
    reduce_scatter x2, waiting for transfers between devices: 12.4 us -> 61.9 us  [scatter_line(): lax.psum_scatter(values, 'dp', scatter_dimension=0, tiled=True, axis_inde...]
    all_gather x3, waiting for transfers between devices: 48.7 us -> 17.6 us  [gather_line(): lax.all_gather(values, 'dp', axis=0, tiled=True, axis_index_groups=line_g...]
    ppermute x28 -> x27, waiting for transfers between devices: 137 us -> 117 us  [swap(): return lax.ppermute(values, axis, [(i, i ^ offset) for i in range(size)])]
    unnamed x124 -> x116, local copies, waits for them, and re-layouts: 25.3 us -> 21.5 us
    pallas_call x10 -> x8, Pallas kernels: 17.7 us -> 20.7 us  [join_blocks(): pl.pallas_call(kernel, grid_spec=pltpu.PrefetchScalarGridSpec(num_scalar_...]
    ppermute x28 -> x27, starting transfers between devices: 26.1 us -> 24.7 us  [swap(): return lax.ppermute(values, axis, [(i, i ^ offset) for i in range(size)])]
  transfers between devices with their start and end apart: 33 -> 32, of which waited for: 18 -> 17; matrix products, arithmetic and copies ran while one was open for 9% -> 9% of each run, Pallas kernels for 27% -> 28%
where the time goes in v6:
time: 438 us; the launch traced here: 437 us
  waiting for transfers between devices  196 us (45%)
  Pallas kernels  134 us (31%)
  local copies, waits for them, and re-layouts  42 us (10%)
  starting transfers between devices  25 us (6%)
  other arithmetic  19.2 us (4%)
  between operations  17 us (4%)
    ppermute x27, waiting for transfers between devices, swap(): return lax.ppermute(values, axis, [(i, i ^ offset) for i in range(size)])  117 us
    reduce_scatter x2, waiting for transfers between devices, scatter_line(): lax.psum_scatter(values, 'dp', scatter_dimension=0, tiled=True, axis_inde...  61.9 us
    pallas_call x2, Pallas kernels, scan_backward(): pl.pallas_call(kernel, grid=(span[1] - span[0],), in_specs=in_specs, out_...  38.8 us
    ppermute x27, starting transfers between devices, swap(): return lax.ppermute(values, axis, [(i, i ^ offset) for i in range(size)])  24.7 us
    unnamed x116, local copies, waits for them, and re-layouts  21.5 us
    pallas_call x8, Pallas kernels, join_blocks(): pl.pallas_call(kernel, grid_spec=pltpu.PrefetchScalarGridSpec(num_scalar_...  20.7 us
    all_gather x3, waiting for transfers between devices, gather_line(): lax.all_gather(values, 'dp', axis=0, tiled=True, axis_index_groups=line_g...  17.6 us
    pallas_call x2, Pallas kernels, factor_products(): pl.pallas_call(kernel, grid_spec=pltpu.PrefetchScalarGridSpec(num_scalar_...  17.6 us
  transfers between devices with their start and end apart: 32, of which 17 were waited for; matrix products, arithmetic and copies ran while one was open for 9% of the time, Pallas kernels for 28%

profile of v6, /device:TPU:0, one launch (start us, length us, event | category | flops | bytes accessed | tf_op | source)
XLA Modules:
  0.0 436.6 jit_solution(17763860438780310019)
XLA Ops:
  19.6 6.4 %collective-permute-done.refs_1_ = bf16[128,2048]{1,0:T(8,128)(2,1)S(1)} collective-permute-done((bf16[128,2048]{1,0:T(8,128)(2,1)S(1)}, bf16[128,2048]{1,0:T(8,128)(2,1)S(1)}, u32[]{:S(2)}, u32[]{:S(2)}) %collective-permute-start) | collective-permute-done | bytes 524320 | tf_op jit(solution)/shard_map/ppermute | solution.py:698
  32.4 9.3 %project_in.1 = (bf16[512,2048]{1,0:T(8,128)(2,1)}, f32[512,1024]{1,0:T(8,128)}, f32[512,1024]{1,0:T(8,128)}, f32[512,160]{1,0:T(8,128)}) custom-call(s32[4]{0:T(128)} %pad_add_fusion.places_ref, bf16[128,2048]{1,0:T(8,128)(2,1)} %copy-done.31, bf16[128,2048]{1,0:T(8,128)(2,1)} %copy-done.41, bf16[128,2048]{1,0:T(8,128)(2,1)} %copy-done.42, ...), custom_call_target="tpu_custom_call" | custom-call | flops 1 | bytes 1 | tf_op jit(solution)/shard_map/project_in/pallas_call | solution.py:339
  49.0 11.5 %project_gate.1 = (bf16[512,2048]{1,0:T(8,128)(2,1)}, f32[512,1024]{1,0:T(8,128)}, f32[512,1024]{1,0:T(8,128)}, f32[512,1024]{1,0:T(8,128)}) custom-call(s32[4]{0:T(128)} %pad_add_fusion.places_ref, bf16[128,2048]{1,0:T(8,128)(2,1)} %copy-done.36, bf16[128,2048]{1,0:T(8,128)(2,1)} %copy-done.38, bf16[128,2048]{1,0:T(8,128)(2,1)} %copy-done.39, ...), custom_call_target="tpu_custom_call" | custom-call | flops 1 | bytes 1 | tf_op jit(solution)/shard_map/project_gate/pallas_call | solution.py:395
  64.1 16.8 %scan_forward.1 = (f32[64,64,128]{2,1,0:T(8,128)S(1)}, f32[512,16,8,128]{3,2,1,0:T(8,128)}) custom-call(f32[16960]{0:T(1024)S(1)} %pad_maximum_fusion.1.refs_0_, f32[64,64,128]{2,1,0:T(8,128)S(1)} %divide_bitcast_fusion.refs_1_, f32[64,64,128]{2,1,0:T(8,128)} %bitcast.105, f32[512,1024]{1,0:T(8,128)} %get-tuple-element.38.refs_1_.refs_3_, ...), custom_call_target="tpu_custom_call" | custom-call | flops 1 | bytes 1 | tf_op jit(solution)/shard_map/scan_forward/pallas_call | solution.py:110
  85.9 15.2 %scan_backward.2 = (f32[64,64,128]{2,1,0:T(8,128)S(1)}, f32[64,64,128]{2,1,0:T(8,128)}, f32[512,16]{1,0:T(8,128)S(1)}, f32[512,16]{1,0:T(8,128)S(1)}, f32[512,12...) custom-call(f32[16960]{0:T(1024)S(1)} %pad_maximum_fusion.1.refs_0_, f32[64,64,128]{2,1,0:T(8,128)} %copy-done.4, ...), custom_call_target="tpu_custom_call" | custom-call | flops 1 | bytes 1 | tf_op jit(solution)/shard_map/scan_backward/pallas_call | solution.py:268
  104.1 3.9 collective-permute-done.13.refs_13_
  108.8 10.2 %factor_products.2.refs_14_ = bf16[4,2,512,512]{3,2,1,0:T(8,128)(2,1)} custom-call(s32[4]{0:T(128)} %pad_add_fusion.places_ref, bf16[512,2048]{1,0:T(8,128)(2,1)} %get-tuple-element.37.refs_4_.refs_0_, bf16[128,4096]{1,0:T(8,128)(2,1)} %collective-permute-done.8.refs_7_.refs_1_.refs_8_, bf16[128,4096]{1,0:T(8,128)(2,1)} %collective-permute-done.9.refs_2_.refs_9_, ...), custom_call_target="tpu_custom_call" | custom-call | flops 1 | bytes 1 | tf_op jit(solution)/shard_map/factor_products/pallas_call | solution.py:551
  124.3 23.7 %scan_backward.3 = (f32[64,64,128]{2,1,0:T(8,128)S(1)}, f32[64,64,128]{2,1,0:T(8,128)S(1)}, f32[512,16]{1,0:T(8,128)S(1)}, f32[512,16]{1,0:T(8,128)S(1)}, f32[51...) custom-call(f32[16960]{0:T(1024)S(1)} %pad_maximum_fusion.1.refs_0_,, ...), custom_call_target="tpu_custom_call", output_to_operand_aliasing={{0}: (9, {}), {1}: (10, {}), {2}: (11, {}), {3}: (12, {}), ... | custom-call | flops 1 | bytes 1 | tf_op jit(solution)/shard_map/scan_backward/pallas_call | solution.py:268
  153.1 11.7 %collective-permute-done.15 = f32[512,160]{1,0:T(8,128)S(1)} collective-permute-done((f32[512,160]{1,0:T(8,128)S(1)}, f32[512,160]{1,0:T(8,128)S(1)}, u32[]{:S(2)}, u32[]{:S(2)}) %collective-permute-start.15) | collective-permute-done | bytes 327712 | tf_op jit(solution)/shard_map/ppermute | solution.py:698
  165.5 7.0 %finish_inner.1 = (bf16[512,1024]{1,0:T(8,128)(2,1)}, f32[8,1024]{1,0:T(8,128)}) custom-call(f32[512,1024]{1,0:T(8,128)} %bitcast.110, bf16[512,160]{1,0:T(8,128)(2,1)} %add_convert_fusion.1.pg_ref, bf16[160,1024]{1,0:T(8,128)(2,1)} %bitcast.120, f32[512,1024]{1,0:T(8,128)} %get-tuple-element.57.inner_ref, f32[512,3]{1,0:T(8,128)} %copy.44.refs_5_.allow_ref, ...), custom_call_target="tpu_custom_call" | custom-call | flops 1 | bytes 1 | tf_op jit(solution)/shard_map/finish_inner/pallas_call | solution.py:443
  176.2 7.8 %collective-permute-done.19 = bf16[320,512]{1,0:T(8,128)(2,1)S(1)} collective-permute-done((bf16[320,512]{1,0:T(8,128)(2,1)S(1)}, bf16[320,512]{1,0:T(8,128)(2,1)S(1)}, u32[]{:S(2)}, u32[]{:S(2)}) %collective-permute-start.19) | collective-permute-done | bytes 327712 | tf_op jit(solution)/shard_map/ppermute | solution.py:698
  184.9 12.4 %reduce-scatter.3.cloned.1.call-done.refs_0_ = bf16[1,2,512,512]{3,2,1,0:T(8,128)(2,1)} async-done(((bf16[4,2,512,512]{3,2,1,0:T(8,128)(2,1)}), bf16[1,2,512,512]{3,2,1,0:T(8,128)(2,1)}) %reduce-scatter.3.cloned.1.call-update) | async-done | bytes 1048592 | tf_op jit(solution)/shard_map/reduce_scatter | solution.py:767
  200.3 11.7 %collective-permute-done.18.refs_6_ = bf16[512,512]{1,0:T(8,128)(2,1)S(1)} collective-permute-done((bf16[512,512]{1,0:T(8,128)(2,1)S(1)}, bf16[512,512]{1,0:T(8,128)(2,1)S(1)}, u32[]{:S(2)}, u32[]{:S(2)}) %collective-permute-start.18) | collective-permute-done | bytes 524320 | tf_op jit(solution)/shard_map/ppermute | solution.py:698
  212.8 7.3 %factor_products.3.refs_0_.values_ref = bf16[4,608,512]{2,1,0:T(8,128)(2,1)} custom-call(s32[4]{0:T(128)} %pad_add_fusion.places_ref, bf16[512,2048]{1,0:T(8,128)(2,1)} %get-tuple-element.37.refs_4_.refs_0_, bf16[128,4096]{1,0:T(8,128)(2,1)} %collective-permute-done.8.refs_7_.refs_1_.refs_8_, bf16[128,4096]{1,0:T(8,128)(2,1)} %collective-permute-done.9.refs_2_.refs_9_, ...), custom_call_target="tpu_custom_call" | custom-call | flops 1 | bytes 1 | tf_op jit(solution)/shard_map/factor_products/pallas_call | solution.py:551
  222.5 8.7 %project_normed.1 = f32[512,2048]{1,0:T(8,128)} custom-call(bf16[512,1024]{1,0:T(8,128)(2,1)S(1)} %copy-done.9, bf16[512,1024]{1,0:T(8,128)(2,1)S(1)} %get-tuple-element.63.refs_8_.gate_ref, bf16[2,2048,1024]{2,1,0:T(8,128)(2,1)} %w_ref.3, bf16[4,608,512]{2,1,0:T(8,128)(2,1)S(1)} %copy-done.1), custom_call_target="tpu_custom_call" | custom-call | flops 1 | bytes 1 | tf_op jit(solution)/shard_map/project_normed/pallas_call | solution.py:654
  247.8 9.3 %collective-permute-done.21 = bf16[1,1,128,2048]{3,2,1,0:T(8,128)(2,1)} collective-permute-done((bf16[1,1,128,2048]{3,2,1,0:T(8,128)(2,1)}, bf16[1,1,128,2048]{3,2,1,0:T(8,128)(2,1)}, u32[]{:S(2)}, u32[]{:S(2)}) %collective-permute-start.21) | collective-permute-done | bytes 524320 | tf_op jit(solution)/shard_map/ppermute | solution.py:698
  260.1 7.4 %collective-permute-done.22 = f32[2048]{0:T(1024)S(1)} collective-permute-done((f32[2048]{0:T(1024)S(1)}, f32[2048]{0:T(1024)S(1)}, u32[]{:S(2)}, u32[]{:S(2)}) %collective-permute-start.22) | collective-permute-done | bytes 8224 | tf_op jit(solution)/shard_map/ppermute | solution.py:698
  272.3 8.0 %all-gather.4.cloned.1.call-done.refs_1_ = bf16[4,2,512,512]{3,2,1,0:T(8,128)(2,1)} async-done(((bf16[1,2,512,512]{3,2,1,0:T(8,128)(2,1)}), bf16[4,2,512,512]{3,2,1,0:T(8,128)(2,1)}) %all-gather.4.cloned.1.call-update) | async-done | bytes 4194320 | tf_op jit(solution)/shard_map/all_gather | solution.py:773
  281.9 49.4 %reduce-scatter.5.cloned.1.call-done = bf16[1,608,512]{2,1,0:T(8,128)(2,1)} async-done(((bf16[4,608,512]{2,1,0:T(8,128)(2,1)}), bf16[1,608,512]{2,1,0:T(8,128)(2,1)}) %reduce-scatter.5.cloned.1.call-update) | async-done | bytes 622608 | tf_op jit(solution)/shard_map/reduce_scatter | solution.py:767
  334.8 38.2 %collective-permute-done.25.refs_2_.refs_0_ = bf16[8,512,512]{2,1,0:T(8,128)(2,1)} collective-permute-done((bf16[8,512,512]{2,1,0:T(8,128)(2,1)}, bf16[8,512,512]{2,1,0:T(8,128)(2,1)}, u32[]{:S(2)}, u32[]{:S(2)}) %collective-permute-start.25) | collective-permute-done | bytes 4194336 | tf_op jit(solution)/shard_map/ppermute | solution.py:698
  381.6 4.2 join_blocks.15
  385.8 4.3 join_blocks.9.refs_1_
  390.2 9.6 %all-gather.8.cloned.1.call-done.refs_0_ = bf16[4,256,512]{2,1,0:T(8,128)(2,1)} async-done(((bf16[1,256,512]{2,1,0:T(8,128)(2,1)}), bf16[4,256,512]{2,1,0:T(8,128)(2,1)}) %all-gather.8.cloned.1.call-update) | async-done | bytes 1048592 | tf_op jit(solution)/shard_map/all_gather | solution.py:773
  413.4 14.9 %collective-permute-done.26.refs_0_ = bf16[4,256,512]{2,1,0:T(8,128)(2,1)S(1)} collective-permute-done((bf16[4,256,512]{2,1,0:T(8,128)(2,1)}, bf16[4,256,512]{2,1,0:T(8,128)(2,1)S(1)}, u32[]{:S(2)}, u32[]{:S(2)}) %collective-permute-start.26) | collective-permute-done | bytes 1048608 | tf_op jit(solution)/shard_map/ppermute | solution.py:698
  (249 shorter events, 110.8 us)
Async XLA Ops:
  7.2 190.1 %reduce-scatter.3.cloned.1.call-start = ((), (), s32[]{:S(2)}) async-start(), calls=%async_computation.2 | async-start | bytes 5242880 | tf_op jit(solution)/shard_map/reduce_scatter | solution.py:767
  11.0 15.0 %collective-permute-start = (bf16[128,2048]{1,0:T(8,128)(2,1)S(1)}, bf16[128,2048]{1,0:T(8,128)(2,1)S(1)}, u32[]{:S(2)}, u32[]{:S(2)}) collective-permute-start(bf16[128,2048]{1,0:T(8,128)(2,1)S(1)} %fusion.4.refs_0_), channel_id=1, source_target_pairs={{0,2},{1,3},{2,0},{3,1},{4,6},{5,7},{6,4},{7,5},{8,10},{9,11},{10,... | collective-permute-start | bytes 1572872 | tf_op jit(solution)/shard_map/ppermute | solution.py:698
  14.1 17.4 %collective-permute-start.1 = (bf16[128,2048]{1,0:T(8,128)(2,1)S(1)}, bf16[128,2048]{1,0:T(8,128)(2,1)S(1)}, u32[]{:S(2)}, u32[]{:S(2)}) collective-permute-start(bf16[128,2048]{1,0:T(8,128)(2,1)S(1)} %fusion.4.refs_0_), channel_id=1, source_target_pairs={{0,1},{1,0},{2,3},{3,2},{4,5},{5,4},{6,7},{7,6},{8,9},{9,8},{10,11... | collective-permute-start | bytes 1572872 | tf_op jit(solution)/shard_map/ppermute | solution.py:698
  16.1 29.8 %collective-permute-start.8 = (bf16[128,4096]{1,0:T(8,128)(2,1)}, bf16[128,4096]{1,0:T(8,128)(2,1)}, u32[]{:S(2)}, u32[]{:S(2)}) collective-permute-start(bf16[128,4096]{1,0:T(8,128)(2,1)} %pad_maximum_fusion), channel_id=1, source_target_pairs={{0,4},{4,0},{8,12},{12,8},{16,20},{20,16},{24,28},{28,24},{1,5},{5... | collective-permute-start | bytes 3145736 | tf_op jit(solution)/shard_map/ppermute | solution.py:698
  27.3 14.9 %collective-permute-start.5 = (bf16[128,2048]{1,0:T(8,128)(2,1)S(1)}, bf16[128,2048]{1,0:T(8,128)(2,1)S(1)}, u32[]{:S(2)}, u32[]{:S(2)}) collective-permute-start(bf16[128,2048]{1,0:T(8,128)(2,1)S(1)} %broadcast_add_fusion.refs_0_), channel_id=1, source_target_pairs={{0,2},{1,3},{2,0},{3,1},{4,6},{5,7},{6,4},{7,5},{8,10},{9,11},{10,... | collective-permute-start | bytes 1572872 | tf_op jit(solution)/shard_map/ppermute | solution.py:698
  44.9 15.5 %collective-permute-start.4 = (f32[512,160]{1,0:T(8,128)S(1)}, f32[512,160]{1,0:T(8,128)S(1)}, u32[]{:S(2)}, u32[]{:S(2)}) collective-permute-start(f32[512,160]{1,0:T(8,128)S(1)} %add.202), channel_id=1, source_target_pairs={{0,2},{1,3},{2,0},{3,1},{4,6},{5,7},{6,4},{7,5},{8,10},{9,11},{10,... | collective-permute-start | bytes 983048 | tf_op jit(solution)/shard_map/ppermute | solution.py:698
  46.0 57.8 %collective-permute-start.10 = (bf16[128,4096]{1,0:T(8,128)(2,1)}, bf16[128,4096]{1,0:T(8,128)(2,1)}, u32[]{:S(2)}, u32[]{:S(2)}) collective-permute-start(bf16[128,4096]{1,0:T(8,128)(2,1)} %collective-permute-done.8.refs_7_.refs_1_.refs_8_), channel_id=1, source_target_pairs={{0,1},{1,0},{2,3},{3,2},{4,5},{5,4},{6,7},{7,6},{8,9},{9,8},{10,11... | collective-permute-start | bytes 3145736 | tf_op jit(solution)/shard_map/ppermute | solution.py:698
  46.1 57.8 %collective-permute-start.11 = (bf16[128,4096]{1,0:T(8,128)(2,1)}, bf16[128,4096]{1,0:T(8,128)(2,1)}, u32[]{:S(2)}, u32[]{:S(2)}) collective-permute-start(bf16[128,4096]{1,0:T(8,128)(2,1)} %collective-permute-done.8.refs_7_.refs_1_.refs_8_), channel_id=1, source_target_pairs={{0,3},{1,2},{2,1},{3,0},{4,7},{5,6},{6,5},{7,4},{8,11},{9,10},{10,... | collective-permute-start | bytes 3145736 | tf_op jit(solution)/shard_map/ppermute | solution.py:698
  47.9 56.2 %collective-permute-start.9 = (bf16[128,4096]{1,0:T(8,128)(2,1)}, bf16[128,4096]{1,0:T(8,128)(2,1)}, u32[]{:S(2)}, u32[]{:S(2)}) collective-permute-start(bf16[128,4096]{1,0:T(8,128)(2,1)} %collective-permute-done.8.refs_7_.refs_1_.refs_8_), channel_id=1, source_target_pairs={{0,2},{1,3},{2,0},{3,1},{4,6},{5,7},{6,4},{7,5},{8,10},{9,11},{10,... | collective-permute-start | bytes 3145736 | tf_op jit(solution)/shard_map/ppermute | solution.py:698
  83.0 21.1 %collective-permute-start.12 = (bf16[512,512]{1,0:T(8,128)(2,1)S(1)}, bf16[512,512]{1,0:T(8,128)(2,1)S(1)}, u32[]{:S(2)}, u32[]{:S(2)}) collective-permute-start(bf16[512,512]{1,0:T(8,128)(2,1)S(1)} %get-tuple-element.72), channel_id=1, source_target_pairs={{0,4},{4,0},{8,12},{12,8},{16,20},{20,16},{24,28},{28,24},{1,5},{5... | collective-permute-start | bytes 1572872 | tf_op jit(solution)/shard_map/ppermute | solution.py:698
  85.6 22.4 %collective-permute-start.13 = (bf16[512,512]{1,0:T(8,128)(2,1)S(1)}, bf16[512,512]{1,0:T(8,128)(2,1)S(1)}, u32[]{:S(2)}, u32[]{:S(2)}) collective-permute-start(bf16[512,512]{1,0:T(8,128)(2,1)S(1)} %get-tuple-element.70), channel_id=1, source_target_pairs={{0,4},{4,0},{8,12},{12,8},{16,20},{20,16},{24,28},{28,24},{1,5},{5... | collective-permute-start | bytes 1572872 | tf_op jit(solution)/shard_map/ppermute | solution.py:698
  119.1 161.2 %all-gather.4.cloned.1.call-start = ((), (), s32[]{:S(2)}) async-start(), calls=%async_computation.3 | async-start | bytes 5242880 | tf_op jit(solution)/shard_map/all_gather | solution.py:773
  150.8 14.0 %collective-permute-start.15 = (f32[512,160]{1,0:T(8,128)S(1)}, f32[512,160]{1,0:T(8,128)S(1)}, u32[]{:S(2)}, u32[]{:S(2)}) collective-permute-start(f32[512,160]{1,0:T(8,128)S(1)} %add.214), channel_id=1, source_target_pairs={{0,2},{1,3},{2,0},{3,1},{4,6},{5,7},{6,4},{7,5},{8,10},{9,11},{10,... | collective-permute-start | bytes 983048 | tf_op jit(solution)/shard_map/ppermute | solution.py:698
  174.9 9.0 %collective-permute-start.19 = (bf16[320,512]{1,0:T(8,128)(2,1)S(1)}, bf16[320,512]{1,0:T(8,128)(2,1)S(1)}, u32[]{:S(2)}, u32[]{:S(2)}) collective-permute-start(bf16[320,512]{1,0:T(8,128)(2,1)S(1)} %constant_dynamic-slice_fusion), channel_id=1, source_target_pairs={{0,4},{4,0},{8,12},{12,8},{16,20},{20,16},{24,28},{28,24},{1,5},{5... | collective-permute-start | bytes 983048 | tf_op jit(solution)/shard_map/ppermute | solution.py:698
  197.3 134.0 %reduce-scatter.5.cloned.1.call-start = ((), (), s32[]{:S(2)}) async-start(), calls=%async_computation.4 | async-start | bytes 3112960 | tf_op jit(solution)/shard_map/reduce_scatter | solution.py:767
  198.3 13.7 %collective-permute-start.18 = (bf16[512,512]{1,0:T(8,128)(2,1)S(1)}, bf16[512,512]{1,0:T(8,128)(2,1)S(1)}, u32[]{:S(2)}, u32[]{:S(2)}) collective-permute-start(bf16[512,512]{1,0:T(8,128)(2,1)S(1)} %get-tuple-element.68), channel_id=1, source_target_pairs={{0,4},{4,0},{8,12},{12,8},{16,20},{20,16},{24,28},{28,24},{1,5},{5... | collective-permute-start | bytes 1572872 | tf_op jit(solution)/shard_map/ppermute | solution.py:698
  242.0 15.1 %collective-permute-start.21 = (bf16[1,1,128,2048]{3,2,1,0:T(8,128)(2,1)}, bf16[1,1,128,2048]{3,2,1,0:T(8,128)(2,1)}, u32[]{:S(2)}, u32[]{:S(2)}) collective-permute-start(bf16[1,1,128,2048]{3,2,1,0:T(8,128)(2,1)} %dynamic-slice_convert_fusion), channel_id=1, source_target_pairs={{0,2},{1,3},{2,0},{3,1},{4,6},{5,7},{6,4},{7,5},{8,10},{9,11},{10,... | collective-permute-start | bytes 1572872 | tf_op jit(solution)/shard_map/ppermute | solution.py:698
  247.3 20.2 %collective-permute-start.17 = (bf16[1,1,128,2048]{3,2,1,0:T(8,128)(2,1)}, bf16[1,1,128,2048]{3,2,1,0:T(8,128)(2,1)}, u32[]{:S(2)}, u32[]{:S(2)}) collective-permute-start(bf16[1,1,128,2048]{3,2,1,0:T(8,128)(2,1)} %dynamic-slice_convert_fusion.1), channel_id=1, source_target_pairs={{0,2},{1,3},{2,0},{3,1},{4,6},{5,7},{6,4},{7,5},{8,10},{9,11},{10,... | collective-permute-start | bytes 1572872 | tf_op jit(solution)/shard_map/ppermute | solution.py:698
  258.5 9.0 %collective-permute-start.22 = (f32[2048]{0:T(1024)S(1)}, f32[2048]{0:T(1024)S(1)}, u32[]{:S(2)}, u32[]{:S(2)}) collective-permute-start(f32[2048]{0:T(1024)S(1)} %get-tuple-element.61), channel_id=1, source_target_pairs={{0,2},{1,3},{2,0},{3,1},{4,6},{5,7},{6,4},{7,5},{8,10},{9,11},{10,... | collective-permute-start | bytes 24584 | tf_op jit(solution)/shard_map/ppermute | solution.py:698
  280.3 92.8 %all-gather.6.cloned.1.call-start = ((), (), s32[]{:S(2)}) async-start(), calls=%async_computation.5 | async-start | bytes 1802240 | tf_op jit(solution)/shard_map/all_gather | solution.py:773
  280.3 92.7 %collective-permute-start.25 = (bf16[8,512,512]{2,1,0:T(8,128)(2,1)}, bf16[8,512,512]{2,1,0:T(8,128)(2,1)}, u32[]{:S(2)}, u32[]{:S(2)}) collective-permute-start(bf16[8,512,512]{2,1,0:T(8,128)(2,1)} %bitcast.101), channel_id=1, source_target_pairs={{0,4},{4,0},{8,12},{12,8},{16,20},{20,16},{24,28},{28,24},{1,5},{5... | collective-permute-start | bytes 12582920 | tf_op jit(solution)/shard_map/ppermute | solution.py:698
  333.1 66.7 %all-gather.8.cloned.1.call-start = ((), (), s32[]{:S(2)}) async-start(), calls=%async_computation.6 | async-start | bytes 1310720 | tf_op jit(solution)/shard_map/all_gather | solution.py:773
  373.1 34.8 %collective-permute-start.24 = (bf16[4,352,512]{2,1,0:T(8,128)(2,1)}, bf16[4,352,512]{2,1,0:T(8,128)(2,1)S(1)}, u32[]{:S(2)}, u32[]{:S(2)}) collective-permute-start(bf16[4,352,512]{2,1,0:T(8,128)(2,1)} %all-gather.6.cloned.1.call-done.refs_0_), channel_id=1, source_target_pairs={{0,4},{4,0},{8,12},{12,8},{16,20},{20,16},{24,28},{28,24},{1,5},{5... | collective-permute-start | bytes 4325384 | tf_op jit(solution)/shard_map/ppermute | solution.py:698
  399.8 28.5 %collective-permute-start.26 = (bf16[4,256,512]{2,1,0:T(8,128)(2,1)}, bf16[4,256,512]{2,1,0:T(8,128)(2,1)S(1)}, u32[]{:S(2)}, u32[]{:S(2)}) collective-permute-start(bf16[4,256,512]{2,1,0:T(8,128)(2,1)} %all-gather.8.cloned.1.call-done.refs_0_), channel_id=1, source_target_pairs={{0,4},{4,0},{8,12},{12,8},{16,20},{20,16},{24,28},{28,24},{1,5},{5... | collective-permute-start | bytes 3145736 | tf_op jit(solution)/shard_map/ppermute | solution.py:698
  (65 other events, 460.6 us)
Sparse Core Ops, SparseCore 0:
  119.2 78.0 reduce-scatter.2
  199.0 81.2 all-gather.3
  282.7 48.6 reduce-scatter.4
  333.4 34.4 all-gather.5
  373.2 26.5 all-gather.7
